TPU v7x, 32 devices: a whole 2x2x4 slice. The times are simulated.
32 devices in a mesh: ctx: 4 (over z), tis: 2 (over y), rep: 4 (over x, core).
Axes of the slice: x: 2, y: 2, z: 4, core: 2. Of those that a mesh axis runs over, the one named last changes fastest.
Arguments:
- donor_feat: bfloat16 [4, 64, 256], P('rep', 'ctx'), may hold values from -6 to 6
- acceptor_feat: bfloat16 [4, 64, 256], P('rep', 'ctx'), may hold values from -6 to 6
- donor_pos: int32 [4, 64], P('rep', 'ctx'), may hold values from 0 to 65535
- acceptor_pos: int32 [4, 64], P('rep'), may hold values from 0 to 65535
- pair_mask: int32 [4, 64, 80], P('rep', 'ctx'), may hold values from 0 to 1
- targets: int32 [4, 64, 8], P('rep', 'ctx', 'tis'), may hold values from 0 to 80, as said below
- dist_table: bfloat16 [128, 256], replicated, may hold values from -3 to 3
- hidden_weights: bfloat16 [8, 256, 512], P('tis'), may hold values from -0.375 to 0.375
- output_weights: bfloat16 [8, 512], P('tis')
Outputs:
- donor_loss: float32 [4, 64, 8], P('rep', 'ctx', 'tis')
- grad_hidden: float32 [8, 256, 512], P('tis', ('ctx', 'rep'))
- grad_acceptor: float32 [4, 64, 256], P('rep', 'ctx')
Inputs may be any that keep to these rules, and one draw needn't show every extreme that they name: `targets`: each target is a valid slot of its donor, or 80 for no splice.
All inputs are finite; a program needn't handle non-finite values.
Results may differ from a plain program's by a relative error of at most 0.002.
The roundings to bfloat16 on the way count: a program that leaves them out, or rounds other values in their place, can miss the bound.
Values may be sent and summed in bfloat16 or wider, within the bound.
No kernel may reach another device: no remote copies, remote signals or barrier semaphores. Data moves between devices by JAX's collectives and lax.ppermute only.
A program may use at most 64 MiB of HBM per device.

v0:
```python
import jax
import jax.numpy as jnp
from jax import lax
from jax.sharding import PartitionSpec as P

BLOCK_BP = 65536
SPAN_BLOCKS = 4
BIN_BP = 2048
BINS = 128


def passed_along(value, axis, steps):
    count = lax.axis_size(axis)
    first, last = (max(0, -steps), min(count, count - steps))
    return lax.ppermute(value, axis, [(source, source + steps) for source in range(first, last)])


def silu_grad(values):
    sig = jax.nn.sigmoid(values)
    return sig * (1.0 + values * (1.0 - sig))


def on_device(
    donor_feat,
    acceptor_feat,
    donor_pos,
    acceptor_pos,
    pair_mask,
    targets,
    dist_table,
    hidden_weights,
    output_weights,
):
    seq_dev, don_blk, width = donor_feat.shape
    acc_blk = acceptor_feat.shape[1]
    blocks = lax.axis_size("ctx")
    reach = SPAN_BLOCKS + 1
    slots = reach * acc_blk
    here = lax.axis_index("ctx")
    pieces = [acceptor_feat]
    current = acceptor_feat
    for offset in range(1, reach):
        current = passed_along(current, "ctx", -1)
        pieces.append(current)
    window = jnp.stack(pieces, axis=1).reshape(seq_dev, slots, width)
    pos_pad = jnp.concatenate(
        [acceptor_pos, jnp.zeros((seq_dev, SPAN_BLOCKS * acc_blk), jnp.int32)], axis=1
    )
    pos_win = lax.dynamic_slice_in_dim(pos_pad, here * acc_blk, slots, 1)
    slot_block = jnp.arange(slots, dtype=jnp.int32) // acc_blk
    inchain = here + slot_block < blocks
    dist = slot_block * BLOCK_BP + pos_win[:, None, :] - donor_pos[:, :, None]
    valid = (pair_mask > 0) & (dist > 0) & (dist <= SPAN_BLOCKS * BLOCK_BP) & inchain[None, None, :]
    bins = jnp.clip((dist - 1) // BIN_BP, 0, BINS - 1)
    lookup = (
        (bins[..., None] == jnp.arange(BINS, dtype=jnp.int32))
        .astype(jnp.bfloat16)
        .reshape(-1, BINS)
    )
    table = jnp.dot(lookup, dist_table, preferred_element_type=jnp.float32).reshape(
        seq_dev, don_blk, slots, width
    )
    pre = (
        donor_feat.astype(jnp.float32)[:, :, None, :] + window.astype(jnp.float32)[:, None] + table
    )
    flat = jax.nn.silu(pre).astype(jnp.bfloat16).reshape(-1, width)
    grad_pair = jnp.zeros((flat.shape[0], width), jnp.float32)
    losses = []
    fulls = []
    slot_ids = jnp.arange(slots, dtype=jnp.int32)
    for tissue in range(hidden_weights.shape[0]):
        w_in = hidden_weights[tissue]
        w_out = output_weights[tissue]
        goal = targets[:, :, tissue]
        hid = jnp.dot(flat, w_in, preferred_element_type=jnp.float32)
        act = jax.nn.silu(hid).astype(jnp.bfloat16)
        logits = jnp.dot(act, w_out, preferred_element_type=jnp.float32).reshape(
            seq_dev, don_blk, slots
        )
        masked = jnp.where(valid, logits, -jnp.inf)
        top = jnp.maximum(jnp.max(masked, axis=-1), 0.0)
        expo = jnp.exp(masked - top[..., None])
        total = jnp.sum(expo, axis=-1) + jnp.exp(-top)
        picked = jnp.take_along_axis(logits, jnp.minimum(goal, slots - 1)[..., None], axis=-1)[
            ..., 0
        ]
        picked = jnp.where(goal == slots, 0.0, picked)
        losses.append(top + jnp.log(total) - picked)
        onehot = (goal[..., None] == slot_ids).astype(jnp.float32)
        grad_logits = expo / total[..., None] - onehot
        grad_act = grad_logits.reshape(-1)[:, None] * w_out.astype(jnp.float32)[None, :]
        grad_hid = (grad_act * silu_grad(hid)).astype(jnp.bfloat16)
        grad_pair = grad_pair + lax.dot_general(
            grad_hid, w_in, (((1,), (1,)), ((), ())), preferred_element_type=jnp.float32
        )
        fulls.append(
            lax.dot_general(
                flat, grad_hid, (((0,), (0,)), ((), ())), preferred_element_type=jnp.float32
            )
        )
    stacked = jnp.stack(fulls, axis=1)
    grad_hidden = jnp.transpose(
        lax.psum_scatter(stacked, ("ctx", "rep"), scatter_dimension=0, tiled=True), (1, 0, 2)
    )
    grad_pre = grad_pair.reshape(seq_dev, don_blk, slots, width) * silu_grad(pre)
    contrib = jnp.sum(grad_pre, axis=1).reshape(seq_dev, reach, acc_blk, width)
    carried = contrib[:, reach - 1]
    for offset in range(reach - 2, -1, -1):
        carried = passed_along(carried, "ctx", 1) + contrib[:, offset]
    grad_acceptor = lax.psum(carried, "tis")
    donor_loss = jnp.stack(losses, axis=-1)
    return (donor_loss, grad_hidden, grad_acceptor)


def solution(mesh):
    placed = (
        P("rep", "ctx", None),
        P("rep", "ctx", None),
        P("rep", "ctx"),
        P("rep", None),
        P("rep", "ctx", None),
        P("rep", "ctx", "tis"),
        P(),
        P("tis", None, None),
        P("tis", None),
    )
    return jax.shard_map(
        on_device,
        mesh=mesh,
        in_specs=placed,
        out_specs=(P("rep", "ctx", "tis"), P("tis", ("ctx", "rep"), None), P("rep", "ctx", None)),
        check_vma=False,
    )
```

profile of v0, /device:TPU:0, one launch (start us, length us, event | category | flops | bytes accessed | tf_op | source)
XLA Modules:
  0.0 133.5 jit_solution(13141909445420512982)
XLA Ops:
  7.2 1.3 collective-permute-start
  8.5 0.7 constant_dynamic-update-slice_fusion.4
  9.2 0.7 bitcast_convert_fusion.1
  9.9 0.8 slice_bitcast_fusion.8
  10.8 0.9 slice_reduce_fusion.3
  11.6 0.7 bitcast_add_fusion.4
  12.4 0.7 fusion.28
  13.2 0.8 collective-permute-done
  14.0 1.3 collective-permute-start.1
  15.3 5.1 %collective-permute-done.1 = bf16[1,16,256]{2,1,0:T(8,128)(2,1)S(1)} collective-permute-done((bf16[1,16,256]{2,1,0:T(8,128)(2,1)S(1)}, bf16[1,16,256]{2,1,0:T(8,128)(2,1)S(1)}, u32[]{:S(2)}, u32[]{:S(2)}) %collective-permute-start.1) | collective-permute-done | bytes 8224 | tf_op jit(solution)/shard_map/ppermute | solution.py:15
  20.4 1.3 collective-permute-start.2
  21.7 4.2 %collective-permute-done.2 = bf16[1,16,256]{2,1,0:T(8,128)(2,1)S(1)} collective-permute-done((bf16[1,16,256]{2,1,0:T(8,128)(2,1)S(1)}, bf16[1,16,256]{2,1,0:T(8,128)(2,1)S(1)}, u32[]{:S(2)}, u32[]{:S(2)}) %collective-permute-start.2) | collective-permute-done | bytes 8224 | tf_op jit(solution)/shard_map/ppermute | solution.py:15
  25.9 1.3 collective-permute-start.3
  27.2 4.2 %collective-permute-done.3 = bf16[1,16,256]{2,1,0:T(8,128)(2,1)S(1)} collective-permute-done((bf16[1,16,256]{2,1,0:T(8,128)(2,1)S(1)}, bf16[1,16,256]{2,1,0:T(8,128)(2,1)S(1)}, u32[]{:S(2)}, u32[]{:S(2)}) %collective-permute-start.3) | collective-permute-done | bytes 8224 | tf_op jit(solution)/shard_map/ppermute | solution.py:15
  31.5 1.7 %multiply_convert_fusion.8 = (bf16[16,80,256]{2,1,0:T(8,128)(2,1)S(1)}, f32[16,80,256]{2,1,0:T(8,128)}) fusion(bf16[128,256]{1,0:T(8,128)(2,1)S(1)} %copy-done, s32[16,80]{1,0:T(8,128)S(1)} %fusion.28, f32[80,256]{1,0:T(8,128)S(1)} %bitcast_convert_fusion, f32[16,256]{1,0:T(8,128)S(1)} %bitcast_convert_fusion.1), kind=kOutput, calls=%fused_computation.22 | convolution fusion | flops 86343680 | bytes 2135040 | tf_op jit(solution)/shard_map/dot_general | solution.py:60
  33.2 0.8 multiply_convert_fusion.7
  34.1 2.3 %multiply_convert_fusion.4 = (bf16[1280,512]{1,0:T(8,128)(2,1)S(1)}, f32[1280,512]{1,0:T(8,128)}) fusion(bf16[1280,256]{1,0:T(8,128)(2,1)S(1)} %bitcast.251, bf16[4,256,512]{2,1,0:T(8,128)(2,1)S(1)} %copy-done.6), kind=kOutput, calls=%fused_computation.11 | convolution fusion | flops 338821120 | bytes 4849664 | tf_op jit(solution)/shard_map/dot_general | solution.py:75
  36.3 2.3 %multiply_convert_fusion.5 = (bf16[1280,512]{1,0:T(8,128)(2,1)S(1)}, f32[1280,512]{1,0:T(8,128)}) fusion(bf16[1280,256]{1,0:T(8,128)(2,1)S(1)} %bitcast.252, bf16[4,256,512]{2,1,0:T(8,128)(2,1)S(1)} %copy-done.6), kind=kOutput, calls=%fused_computation.13 | convolution fusion | flops 338821120 | bytes 4849664 | tf_op jit(solution)/shard_map/dot_general | solution.py:75
  38.7 2.3 %multiply_convert_fusion.6 = (bf16[1280,512]{1,0:T(8,128)(2,1)S(1)}, f32[1280,512]{1,0:T(8,128)}) fusion(bf16[1280,256]{1,0:T(8,128)(2,1)S(1)} %bitcast.253, bf16[4,256,512]{2,1,0:T(8,128)(2,1)S(1)} %copy-done.6), kind=kOutput, calls=%fused_computation.15 | convolution fusion | flops 338821120 | bytes 4849664 | tf_op jit(solution)/shard_map/dot_general | solution.py:75
  41.5 0.6 fusion.42
  42.0 0.6 fusion.44
  43.9 1.0 multiply_convert_fusion.3
  44.8 1.4 %convolution_bitcast_fusion.3 = f32[256,1,512]{2,0,1:T(8,128)} fusion(bf16[1280,256]{1,0:T(8,128)(2,1)S(1)} %bitcast.254, bf16[1280,512]{1,0:T(8,128)(2,1)S(1)} %multiply_convert_fusion.3), kind=kOutput, calls=%fused_computation.27 | convolution fusion | flops 335544320 | bytes 2490368 | tf_op jit(solution)/shard_map/dot_general | solution.py:97
  46.2 2.5 %fusion.10 = f32[1280,256]{1,0:T(8,128)} fusion(bf16[1280,512]{1,0:T(8,128)(2,1)S(1)} %multiply_convert_fusion.3, bf16[4,256,512]{2,1,0:T(8,128)(2,1)} %param.18), kind=kOutput, calls=%fused_computation.39 | convolution fusion | flops 335544320 | bytes 2883584 | tf_op jit(solution)/shard_map/dot_general | solution.py:93
  48.8 2.7 %multiply_convert_fusion = bf16[1280,512]{1,0:T(8,128)(2,1)S(1)} fusion(f32[1280,512]{1,0:T(8,128)} %get-tuple-element.42, f32[512]{0:T(512)S(1)} %mul.185, f32[1280]{0:T(1024)S(1)} %mul.183), kind=kLoop, calls=%fused_computation.7 | loop fusion | flops 6553600 | bytes 3939328 | tf_op jit(solution)/shard_map/convert_element_type | solution.py:92
  51.5 1.3 convolution_bitcast_fusion
  53.0 2.7 %multiply_convert_fusion.1 = bf16[1280,512]{1,0:T(8,128)(2,1)S(1)} fusion(f32[1280,512]{1,0:T(8,128)} %get-tuple-element.44, f32[512]{0:T(512)S(1)} %mul.177, f32[1280]{0:T(1024)S(1)} %mul.175), kind=kLoop, calls=%fused_computation.8 | loop fusion | flops 6553600 | bytes 3939328 | tf_op jit(solution)/shard_map/convert_element_type | solution.py:92
  55.7 1.3 convolution_bitcast_fusion.1
  57.1 2.7 %multiply_convert_fusion.2 = bf16[1280,512]{1,0:T(8,128)(2,1)S(1)} fusion(f32[1280,512]{1,0:T(8,128)} %get-tuple-element.46, f32[512]{0:T(512)S(1)} %mul.169, f32[1280]{0:T(1024)S(1)} %mul.167), kind=kLoop, calls=%fused_computation.9 | loop fusion | flops 6553600 | bytes 3939328 | tf_op jit(solution)/shard_map/convert_element_type | solution.py:92
  59.8 1.0 copy-done.1
  62.2 1.5 %pad_maximum_fusion = f32[256,4,512]{2,0,1:T(8,128)} fusion(f32[256,1,512]{2,0,1:T(8,128)S(1)} %copy-done.3, f32[256,1,512]{2,0,1:T(8,128)S(1)} %copy-done.4, f32[256,1,512]{2,0,1:T(8,128)S(1)} %convolution_bitcast_fusion.2, f32[256,1,512]{2,0,1:T(8,128)S(1)} %copy-done.2), kind=kLoop, calls=%fused_computation.19 | loop fusion | flops 1572864 | bytes 4194304 | tf_op jit(solution)/shard_map/stack | solution.py:101
  63.8 2.4 %convolution_add_fusion.2 = f32[1280,256]{1,0:T(8,128)S(1)} fusion(f32[1280,256]{1,0:T(8,128)} %fusion.10, bf16[1280,512]{1,0:T(8,128)(2,1)} %copy-done.1, bf16[4,256,512]{2,1,0:T(8,128)(2,1)} %param.18), kind=kOutput, calls=%fused_computation.6 | convolution fusion | flops 335872000 | bytes 4194304 | tf_op jit(solution)/shard_map/dot_general | solution.py:93
  66.8 0.6 convolution_add_fusion
  67.4 0.7 copy-done.5
  68.6 3.9 %collective-permute-start.4 = (f32[1,16,256]{2,1,0:T(8,128)S(1)}, f32[1,16,256]{2,1,0:T(8,128)S(1)}, u32[]{:S(2)}, u32[]{:S(2)}) collective-permute-start(f32[1,16,256]{2,1,0:T(8,128)S(1)} %slice_bitcast_fusion.4), channel_id=1, source_target_pairs={{0,8},{8,16},{16,24},{1,9},{9,17},{17,25},{2,10},{10,18},{18,26},{... | collective-permute-start | bytes 49160 | tf_op jit(solution)/shard_map/ppermute | solution.py:15
  72.5 1.4 %collective-permute-done.4 = f32[1,16,256]{2,1,0:T(8,128)S(1)} collective-permute-done((f32[1,16,256]{2,1,0:T(8,128)S(1)}, f32[1,16,256]{2,1,0:T(8,128)S(1)}, u32[]{:S(2)}, u32[]{:S(2)}) %collective-permute-start.4) | collective-permute-done | bytes 16416 | tf_op jit(solution)/shard_map/ppermute | solution.py:15
  73.9 4.2 %collective-permute-start.5 = (f32[1,16,256]{2,1,0:T(8,128)S(1)}, f32[1,16,256]{2,1,0:T(8,128)S(1)}, u32[]{:S(2)}, u32[]{:S(2)}) collective-permute-start(f32[1,16,256]{2,1,0:T(8,128)S(1)} %fusion.26), channel_id=1, source_target_pairs={{0,8},{8,16},{16,24},{1,9},{9,17},{17,25},{2,10},{10,18},{18,26},{... | collective-permute-start | bytes 49160 | tf_op jit(solution)/shard_map/ppermute | solution.py:15
  78.2 0.7 gather_fusion
  78.9 0.7 gather_fusion.1
  79.5 0.7 gather_fusion.3
  80.2 0.7 gather_fusion.2
  80.9 3.9 %collective-permute-start.6 = (f32[1,16,256]{2,1,0:T(8,128)S(1)}, f32[1,16,256]{2,1,0:T(8,128)S(1)}, u32[]{:S(2)}, u32[]{:S(2)}) collective-permute-start(f32[1,16,256]{2,1,0:T(8,128)S(1)} %fusion.25), channel_id=1, source_target_pairs={{0,8},{8,16},{16,24},{1,9},{9,17},{17,25},{2,10},{10,18},{18,26},{... | collective-permute-start | bytes 49160 | tf_op jit(solution)/shard_map/ppermute | solution.py:15
  84.8 1.4 %collective-permute-done.6 = f32[1,16,256]{2,1,0:T(8,128)S(1)} collective-permute-done((f32[1,16,256]{2,1,0:T(8,128)S(1)}, f32[1,16,256]{2,1,0:T(8,128)S(1)}, u32[]{:S(2)}, u32[]{:S(2)}) %collective-permute-start.6) | collective-permute-done | bytes 16416 | tf_op jit(solution)/shard_map/ppermute | solution.py:15
  86.2 4.2 %collective-permute-start.7 = (f32[1,16,256]{2,1,0:T(8,128)S(1)}, f32[1,16,256]{2,1,0:T(8,128)S(1)}, u32[]{:S(2)}, u32[]{:S(2)}) collective-permute-start(f32[1,16,256]{2,1,0:T(8,128)S(1)} %fusion.24), channel_id=1, source_target_pairs={{0,8},{8,16},{16,24},{1,9},{9,17},{17,25},{2,10},{10,18},{18,26},{... | collective-permute-start | bytes 49160 | tf_op jit(solution)/shard_map/ppermute | solution.py:15
  90.4 0.6 pad_maximum_fusion.1
  91.0 0.8 collective-permute-done.7
  91.8 8.8 %psum.7 = f32[1,16,256]{2,1,0:T(8,128)} all-reduce(f32[1,16,256]{2,1,0:T(8,128)S(1)} %fusion.23), channel_id=1, replica_groups=mesh['ctx'=4,'tis'=2,'rep'=4] {'tis'}, use_global_device_ids=true, to_apply=%region_10.12 | all-reduce | flops 4096 | bytes 32768 | tf_op jit(solution)/shard_map/psum | solution.py:110
  100.6 26.0 %reduce-scatter.2.cloned.1.call-done = f32[16,4,512]{2,0,1:T(8,128)} async-done(((f32[256,4,512]{2,0,1:T(8,128)}), f32[16,4,512]{2,0,1:T(8,128)}) %reduce-scatter.2.cloned.1.call-update) | async-done | bytes 131088 | tf_op jit(solution)/shard_map/reduce_scatter | solution.py:103
  (63 shorter events, 4.6 us)
Async XLA Ops:
  7.2 24.3 %copy-start = (bf16[128,256]{1,0:T(8,128)(2,1)S(1)}, bf16[128,256]{1,0:T(8,128)(2,1)}, u32[]{:S(2)}) copy-start(bf16[128,256]{1,0:T(8,128)(2,1)} %param.17) | copy-start | bytes 196612
  7.2 119.4 %reduce-scatter.2.cloned.1.call-start = ((), (), s32[]{:S(2)}) async-start(), calls=%async_computation.1 | async-start | bytes 2228224 | tf_op jit(solution)/shard_map/reduce_scatter | solution.py:103
  7.2 6.8 %collective-permute-start = (bf16[1,16,256]{2,1,0:T(8,128)(2,1)}, bf16[1,16,256]{2,1,0:T(8,128)(2,1)S(1)}, u32[]{:S(2)}, u32[]{:S(2)}) collective-permute-start(bf16[1,16,256]{2,1,0:T(8,128)(2,1)} %param.12), channel_id=1, source_target_pairs={{8,0},{16,8},{24,16},{9,1},{17,9},{25,17},{10,2},{18,10},{26,18},{... | collective-permute-start | bytes 24584 | tf_op jit(solution)/shard_map/ppermute | solution.py:15
  14.0 6.4 %collective-permute-start.1 = (bf16[1,16,256]{2,1,0:T(8,128)(2,1)S(1)}, bf16[1,16,256]{2,1,0:T(8,128)(2,1)S(1)}, u32[]{:S(2)}, u32[]{:S(2)}) collective-permute-start(bf16[1,16,256]{2,1,0:T(8,128)(2,1)S(1)} %collective-permute-done), channel_id=1, source_target_pairs={{8,0},{16,8},{24,16},{9,1},{17,9},{25,17},{10,2},{18,10},{26,18},{... | collective-permute-start | bytes 24584 | tf_op jit(solution)/shard_map/ppermute | solution.py:15
  20.4 5.5 %collective-permute-start.2 = (bf16[1,16,256]{2,1,0:T(8,128)(2,1)S(1)}, bf16[1,16,256]{2,1,0:T(8,128)(2,1)S(1)}, u32[]{:S(2)}, u32[]{:S(2)}) collective-permute-start(bf16[1,16,256]{2,1,0:T(8,128)(2,1)S(1)} %collective-permute-done.1), channel_id=1, source_target_pairs={{8,0},{16,8},{24,16},{9,1},{17,9},{25,17},{10,2},{18,10},{26,18},{... | collective-permute-start | bytes 24584 | tf_op jit(solution)/shard_map/ppermute | solution.py:15
  25.9 5.5 %collective-permute-start.3 = (bf16[1,16,256]{2,1,0:T(8,128)(2,1)S(1)}, bf16[1,16,256]{2,1,0:T(8,128)(2,1)S(1)}, u32[]{:S(2)}, u32[]{:S(2)}) collective-permute-start(bf16[1,16,256]{2,1,0:T(8,128)(2,1)S(1)} %collective-permute-done.2), channel_id=1, source_target_pairs={{8,0},{16,8},{24,16},{9,1},{17,9},{25,17},{10,2},{18,10},{26,18},{... | collective-permute-start | bytes 24584 | tf_op jit(solution)/shard_map/ppermute | solution.py:15
  31.5 1.7 %copy-start.6 = (bf16[4,256,512]{2,1,0:T(8,128)(2,1)S(1)}, bf16[4,256,512]{2,1,0:T(8,128)(2,1)}, u32[]{:S(2)}) copy-start(bf16[4,256,512]{2,1,0:T(8,128)(2,1)} %param.18) | copy-start | bytes 3145732
  38.7 2.3 %copy-start.8 = (bf16[4,512]{1,0:T(4,128)(2,1)S(1)}, bf16[4,512]{1,0:T(4,128)(2,1)}, u32[]{:S(2)}) copy-start(bf16[4,512]{1,0:T(4,128)(2,1)} %param.19) | copy-start | bytes 12292
  41.5 1.7 %copy-start.10 = (s32[1,16,80]{2,1,0:T(8,128)S(1)}, s32[1,16,80]{2,1,0:T(8,128)}, u32[]{:S(2)}) copy-start(s32[1,16,80]{2,1,0:T(8,128)} %param.15) | copy-start | bytes 15364
  41.5 1.7 %copy-start.11 = (s32[1,16]{1,0:T(1,128)S(1)}, s32[1,16]{1,0:T(1,128)}, u32[]{:S(2)}) copy-start(s32[1,16]{1,0:T(1,128)} %param.13) | copy-start | bytes 196
  59.8 1.1 copy-start.1
  60.9 1.0 copy-start.2
  60.9 1.2 copy-start.3
  60.9 1.4 %copy-start.4 = (f32[256,1,512]{2,0,1:T(8,128)S(1)}, f32[256,1,512]{2,0,1:T(8,128)}, u32[]{:S(2)}) copy-start(f32[256,1,512]{2,0,1:T(8,128)} %convolution_bitcast_fusion.1) | copy-start | bytes 1572868
  63.8 2.4 %copy-start.7 = (bf16[4,256,512]{2,1,0:T(8,128)(2,1)S(1)}, bf16[4,256,512]{2,1,0:T(8,128)(2,1)}, u32[]{:S(2)}) copy-start(bf16[4,256,512]{2,1,0:T(8,128)(2,1)} %param.18) | copy-start | bytes 3145732
  66.8 1.3 copy-start.5
  68.1 16.7 %copy-start.9 = (s32[1,16,4]{1,2,0:T(4,128)S(1)}, s32[1,16,4]{1,2,0:T(4,128)}, u32[]{:S(2)}) copy-start(s32[1,16,4]{1,2,0:T(4,128)} %param.16) | copy-start | bytes 772
  68.6 5.4 %collective-permute-start.4 = (f32[1,16,256]{2,1,0:T(8,128)S(1)}, f32[1,16,256]{2,1,0:T(8,128)S(1)}, u32[]{:S(2)}, u32[]{:S(2)}) collective-permute-start(f32[1,16,256]{2,1,0:T(8,128)S(1)} %slice_bitcast_fusion.4), channel_id=1, source_target_pairs={{0,8},{8,16},{16,24},{1,9},{9,17},{17,25},{2,10},{10,18},{18,26},{... | collective-permute-start | bytes 49160 | tf_op jit(solution)/shard_map/ppermute | solution.py:15
  73.9 6.9 %collective-permute-start.5 = (f32[1,16,256]{2,1,0:T(8,128)S(1)}, f32[1,16,256]{2,1,0:T(8,128)S(1)}, u32[]{:S(2)}, u32[]{:S(2)}) collective-permute-start(f32[1,16,256]{2,1,0:T(8,128)S(1)} %fusion.26), channel_id=1, source_target_pairs={{0,8},{8,16},{16,24},{1,9},{9,17},{17,25},{2,10},{10,18},{18,26},{... | collective-permute-start | bytes 49160 | tf_op jit(solution)/shard_map/ppermute | solution.py:15
  80.9 5.3 %collective-permute-start.6 = (f32[1,16,256]{2,1,0:T(8,128)S(1)}, f32[1,16,256]{2,1,0:T(8,128)S(1)}, u32[]{:S(2)}, u32[]{:S(2)}) collective-permute-start(f32[1,16,256]{2,1,0:T(8,128)S(1)} %fusion.25), channel_id=1, source_target_pairs={{0,8},{8,16},{16,24},{1,9},{9,17},{17,25},{2,10},{10,18},{18,26},{... | collective-permute-start | bytes 49160 | tf_op jit(solution)/shard_map/ppermute | solution.py:15
  86.2 5.6 %collective-permute-start.7 = (f32[1,16,256]{2,1,0:T(8,128)S(1)}, f32[1,16,256]{2,1,0:T(8,128)S(1)}, u32[]{:S(2)}, u32[]{:S(2)}) collective-permute-start(f32[1,16,256]{2,1,0:T(8,128)S(1)} %fusion.24), channel_id=1, source_target_pairs={{0,8},{8,16},{16,24},{1,9},{9,17},{17,25},{2,10},{10,18},{18,26},{... | collective-permute-start | bytes 49160 | tf_op jit(solution)/shard_map/ppermute | solution.py:15
Sparse Core Ops, SparseCore 0:
  63.9 62.6 reduce-scatter.1
where the time goes:
time: 134 us; the launch traced here: 133 us
  waiting for transfers between devices  44.1 us (33%)
  matrix products  22.2 us (17%)
  starting transfers between devices  21.4 us (16%)
  other arithmetic  15.5 us (12%)
  between operations  14.4 us (11%)
  blocking collectives  8.77 us (7%)
  local copies, waits for them, and re-layouts  7.15 us (5%)
    reduce_scatter x1, waiting for transfers between devices, on_device(): lax.psum_scatter(stacked, ('ctx', 'rep'), scatter_dimension=0, tiled=True)  26 us
    ppermute x8, starting transfers between devices, passed_along(): lax.ppermute(value, axis, [(source, source + steps) for source in range(f...  21.4 us
    ppermute x8, waiting for transfers between devices, passed_along(): lax.ppermute(value, axis, [(source, source + steps) for source in range(f...  18 us
    convert_element_type x4, other arithmetic, on_device(): grad_hid = (grad_act * silu_grad(hid)).astype(jnp.bfloat16)  9.14 us
    psum x1, blocking collectives, on_device(): grad_acceptor = lax.psum(carried, 'tis')  8.77 us
    dot_general x4, matrix products, on_device(): hid = jnp.dot(flat, w_in, preferred_element_type=jnp.float32)  7.73 us
    dot_general x4, matrix products, on_device(): lax.dot_general(grad_hid, w_in, (((1,), (1,)), ((), ())), preferred_eleme...  6.09 us
    dot_general x4, matrix products, on_device(): lax.dot_general(flat, grad_hid, (((0,), (0,)), ((), ())), preferred_eleme...  4.53 us
  transfers between devices with their start and end apart: 9, of which 8 were waited for; matrix products, arithmetic and copies ran while one was open for 9% of the time, Pallas kernels for 0%

commit v1 on v0

--- a/solution.py
+++ b/solution.py
@@ -1,12 +1,17 @@
+import functools
+
 import jax
 import jax.numpy as jnp
 from jax import lax
+from jax.experimental import pallas as pl
+from jax.experimental.pallas import tpu as pltpu
 from jax.sharding import PartitionSpec as P
 
 BLOCK_BP = 65536
 SPAN_BLOCKS = 4
 BIN_BP = 2048
 BINS = 128
+LANES = 128
 
 
 def passed_along(value, axis, steps):
@@ -15,12 +20,16 @@
     return lax.ppermute(value, axis, [(source, source + steps) for source in range(first, last)])
 
 
+def swapped(value, axis, bits):
+    return lax.ppermute(value, axis, [(i, i ^ bits) for i in range(lax.axis_size(axis))])
+
+
 def silu_grad(values):
     sig = jax.nn.sigmoid(values)
     return sig * (1.0 + values * (1.0 - sig))
 
 
-def on_device(
+def general(
     donor_feat,
     acceptor_feat,
     donor_pos,
@@ -38,10 +47,12 @@
     slots = reach * acc_blk
     here = lax.axis_index("ctx")
     pieces = [acceptor_feat]
-    current = acceptor_feat
     for offset in range(1, reach):
-        current = passed_along(current, "ctx", -1)
-        pieces.append(current)
+        pieces.append(
+            passed_along(acceptor_feat, "ctx", -offset)
+            if offset < blocks
+            else jnp.zeros_like(acceptor_feat)
+        )
     window = jnp.stack(pieces, axis=1).reshape(seq_dev, slots, width)
     pos_pad = jnp.concatenate(
         [acceptor_pos, jnp.zeros((seq_dev, SPAN_BLOCKS * acc_blk), jnp.int32)], axis=1
@@ -81,13 +92,10 @@
         top = jnp.maximum(jnp.max(masked, axis=-1), 0.0)
         expo = jnp.exp(masked - top[..., None])
         total = jnp.sum(expo, axis=-1) + jnp.exp(-top)
-        picked = jnp.take_along_axis(logits, jnp.minimum(goal, slots - 1)[..., None], axis=-1)[
-            ..., 0
-        ]
-        picked = jnp.where(goal == slots, 0.0, picked)
+        onehot = goal[..., None] == slot_ids
+        picked = jnp.sum(jnp.where(onehot, logits, 0.0), axis=-1)
         losses.append(top + jnp.log(total) - picked)
-        onehot = (goal[..., None] == slot_ids).astype(jnp.float32)
-        grad_logits = expo / total[..., None] - onehot
+        grad_logits = expo / total[..., None] - onehot.astype(jnp.float32)
         grad_act = grad_logits.reshape(-1)[:, None] * w_out.astype(jnp.float32)[None, :]
         grad_hid = (grad_act * silu_grad(hid)).astype(jnp.bfloat16)
         grad_pair = grad_pair + lax.dot_general(
@@ -104,12 +112,272 @@
     )
     grad_pre = grad_pair.reshape(seq_dev, don_blk, slots, width) * silu_grad(pre)
     contrib = jnp.sum(grad_pre, axis=1).reshape(seq_dev, reach, acc_blk, width)
-    carried = contrib[:, reach - 1]
-    for offset in range(reach - 2, -1, -1):
-        carried = passed_along(carried, "ctx", 1) + contrib[:, offset]
+    carried = contrib[:, 0]
+    for offset in range(1, min(reach, blocks)):
+        carried = carried + passed_along(contrib[:, offset], "ctx", offset)
     grad_acceptor = lax.psum(carried, "tis")
     donor_loss = jnp.stack(losses, axis=-1)
     return (donor_loss, grad_hidden, grad_acceptor)
+
+
+def silu_parts(values):
+    sig = 0.5 * jnp.tanh(0.5 * values) + 0.5
+    out = values * sig
+    return out, sig + out * (1.0 - sig)
+
+
+def spread(columns, lane):
+    ids = lax.broadcasted_iota(jnp.int32, columns.shape, 1)
+    return jnp.dot(
+        jnp.where(ids == lane, columns, jnp.zeros_like(columns)),
+        jnp.ones((LANES, LANES), jnp.bfloat16),
+        preferred_element_type=jnp.float32,
+    )
+
+
+def head_kernel(blocks, don_blk, width, slots, *refs):
+    packed = refs[:blocks]
+    (apos_ref, table_ref, w_ref, wo_ref) = refs[blocks : blocks + 4]
+    (gh_ref, acc_ref, loss_ref) = refs[blocks + 4 : blocks + 7]
+    (feat, aux, pair_s, dpre_s, dhid_s, logit_s, gh_s) = refs[blocks + 7 :]
+    here = lax.axis_index("ctx")
+    rep = lax.axis_index("rep")
+    cross = lax.div(rep, 2)
+    core = lax.rem(rep, 2)
+    blk = don_blk
+    hidden = w_ref.shape[1]
+    for k in range(blocks):
+        owner = here ^ k
+        feat[owner] = packed[k][:, : 2 * width].astype(jnp.float32)
+        aux[owner] = packed[k][:, 2 * width :]
+    ids = lax.broadcasted_iota(jnp.int32, (blk, LANES), 1)
+    rows = lax.broadcasted_iota(jnp.int32, (blk, LANES), 0)
+    w = w_ref[...]
+    w_out = wo_ref[...].astype(jnp.float32)
+    w_rep = jnp.broadcast_to(wo_ref[...], (LANES, hidden))
+    table = table_ref[...]
+    apos = apos_ref[...]
+    ones = jnp.ones((LANES, LANES), jnp.bfloat16)
+
+    def acceptor_rows(a):
+        pos = jnp.zeros((blk, LANES), jnp.int32)
+        wide = jnp.concatenate(
+            [apos, jnp.zeros((1, LANES - apos.shape[1]), jnp.int32)], axis=1
+        )
+        wide = jnp.broadcast_to(wide, (blk, LANES))
+        wide = jnp.where(ids == rows + a * blk, wide, pos)
+        high = jnp.dot(
+            (wide >> 8).astype(jnp.float32).astype(jnp.bfloat16), ones,
+            preferred_element_type=jnp.float32,
+        )
+        low = jnp.dot(
+            (wide & 255).astype(jnp.float32).astype(jnp.bfloat16), ones,
+            preferred_element_type=jnp.float32,
+        )
+        return (high * 256.0 + low).astype(jnp.int32)
+
+    apos_rows = [acceptor_rows(a) for a in range(blocks)]
+    tile_of = {}
+    for b in range(blocks):
+        for a in range(b, min(blocks, b + SPAN_BLOCKS + 1)):
+            tile_of[(b, a)] = len(tile_of)
+    lane3 = lax.broadcasted_iota(jnp.int32, (blk, blk, LANES), 2)
+    row3 = lax.broadcasted_iota(jnp.int32, (blk, blk, LANES), 1)
+    acc_total = [jnp.zeros((blk, width), jnp.float32) for _ in range(blocks)]
+    gh_total = None
+    for b in range(blocks):
+        extra = aux[b]
+        dpos = (spread(extra, slots) * 256.0 + spread(extra, slots + 1)).astype(jnp.int32)
+        goal = spread(extra, slots + 2 + here).astype(jnp.int32)
+        donors = feat[b, :, :width]
+        near = list(range(b, min(blocks, b + SPAN_BLOCKS + 1)))
+        valids = []
+        logits = []
+        for a in near:
+            k = a - b
+            tile = tile_of[(b, a)]
+            dist = k * BLOCK_BP + apos_rows[a][None] - dpos[:, None, :]
+            open_slot = jnp.where(
+                lane3 == row3 + k * blk, extra.astype(jnp.float32)[:, None, :], 0.0
+            ).astype(jnp.bfloat16)
+            mask = jnp.dot(
+                open_slot.reshape(blk * blk, LANES), ones, preferred_element_type=jnp.float32
+            ).reshape(blk, blk, LANES)
+            valids.append((mask > 0.5) & (dist > 0) & (dist <= SPAN_BLOCKS * BLOCK_BP))
+            bins = jnp.clip((dist - 1) >> 11, 0, BINS - 1)
+            lookup = jnp.where(bins == lane3, 1.0, 0.0).astype(jnp.bfloat16)
+            looked = jnp.dot(
+                lookup.reshape(blk * blk, BINS), table, preferred_element_type=jnp.float32
+            )
+            pre = (donors[:, None, :] + feat[a, :, width:][None]).reshape(
+                blk * blk, width
+            ) + looked
+            value, slope = silu_parts(pre)
+            pair = value.astype(jnp.bfloat16)
+            pair_s[tile] = pair
+            dpre_s[tile] = slope
+            hid = jnp.dot(pair, w, preferred_element_type=jnp.float32)
+            value, slope = silu_parts(hid)
+            dhid_s[tile] = slope * w_out
+            logits.append(
+                lax.dot_general(
+                    value.astype(jnp.bfloat16),
+                    w_rep,
+                    (((1,), (1,)), ((), ())),
+                    preferred_element_type=jnp.float32,
+                ).reshape(blk, blk, LANES)
+            )
+        top = jnp.zeros((blk, 1, LANES), jnp.float32)
+        for valid, logit in zip(valids, logits):
+            top = jnp.maximum(
+                top, jnp.max(jnp.where(valid, logit, -jnp.inf), axis=1, keepdims=True)
+            )
+        total = jnp.exp(-top)
+        picked = jnp.zeros((blk, 1, LANES), jnp.float32)
+        expos = []
+        goals = []
+        for a, valid, logit in zip(near, valids, logits):
+            expo = jnp.exp(jnp.where(valid, logit, -jnp.inf) - top)
+            total = total + jnp.sum(expo, axis=1, keepdims=True)
+            chosen = goal[:, None, :] == row3 + (a - b) * blk
+            picked = picked + jnp.sum(jnp.where(chosen, logit, 0.0), axis=1, keepdims=True)
+            expos.append(expo)
+            goals.append(chosen)
+        loss_ref[b ^ here] = (top + jnp.log(total) - picked).reshape(blk, LANES)
+        share = 1.0 / total
+        for a, expo, chosen in zip(near, expos, goals):
+            tile = tile_of[(b, a)]
+            grad_logit = (expo * share - jnp.where(chosen, 1.0, 0.0)).reshape(blk * blk, LANES)
+            grad_logit = jnp.concatenate([grad_logit] * (hidden // LANES), axis=1)
+            grad_hid = (grad_logit * dhid_s[tile]).astype(jnp.bfloat16)
+            part = lax.dot_general(
+                pair_s[tile], grad_hid, (((0,), (0,)), ((), ())),
+                preferred_element_type=jnp.float32,
+            )
+            if tile == 0:
+                gh_s[...] = part
+            else:
+                gh_s[...] += part
+            grad_pair = lax.dot_general(
+                grad_hid, w, (((1,), (1,)), ((), ())), preferred_element_type=jnp.float32
+            )
+            acc_total[a] = acc_total[a] + jnp.sum(
+                (grad_pair * dpre_s[tile]).reshape(blk, blk, width), axis=0
+            )
+    for a in range(blocks):
+        acc_ref[a ^ here] = acc_total[a]
+    chunk = gh_ref.shape[3]
+    for c in range(blocks):
+        for x in range(2):
+            for y in range(2):
+                start = ((c * 2 + x) * 2 + y) * chunk
+                gh_ref[y ^ core, x ^ cross, c ^ here] = gh_s[start : start + chunk, :]
+
+
+def finish_kernel(parts, width, hidden, *refs):
+    pieces = refs[:parts]
+    (loss_ref, gh_ref, acc_ref) = refs[parts:]
+    here = lax.axis_index("ctx")
+    total = None
+    lanes = lax.broadcasted_iota(jnp.int32, (pieces[0].shape[0], LANES), 1)
+    losses = jnp.zeros(lanes.shape, jnp.float32)
+    for k in range(parts):
+        owner = here ^ k
+        gh_ref[owner] = pieces[k][:, :hidden]
+        acc = pieces[k][:, hidden : hidden + width]
+        total = acc if total is None else total + acc
+        losses = jnp.where(lanes == owner, pieces[k][:, hidden + width :], losses)
+    acc_ref[0] = total
+    loss_ref[0] = losses[:, :parts]
+
+
+def shared(
+    donor_feat,
+    acceptor_feat,
+    donor_pos,
+    acceptor_pos,
+    pair_mask,
+    targets,
+    dist_table,
+    hidden_weights,
+    output_weights,
+):
+    _, blk, width = donor_feat.shape
+    blocks = lax.axis_size("ctx")
+    slots = pair_mask.shape[2]
+    tissues, _, hidden = hidden_weights.shape
+    here = lax.axis_index("ctx")
+    bf16 = jnp.bfloat16
+    spare = LANES - slots - 2 - tissues
+    packed = jnp.concatenate(
+        [
+            donor_feat[0],
+            acceptor_feat[0],
+            pair_mask[0].astype(bf16),
+            (donor_pos[0] >> 8).astype(bf16)[:, None],
+            (donor_pos[0] & 255).astype(bf16)[:, None],
+            targets[0].astype(bf16),
+            jnp.zeros((blk, spare), bf16),
+        ],
+        axis=1,
+    )
+    pieces = [packed] + [swapped(packed, "ctx", k) for k in range(1, blocks)]
+    w_in = lax.dynamic_index_in_dim(hidden_weights, here, 0, False)
+    w_out = lax.dynamic_index_in_dim(output_weights, here, 0, True)
+    tiles = sum(min(blocks, b + SPAN_BLOCKS + 1) - b for b in range(blocks))
+    chunk = width // (4 * blocks)
+    pairs = blk * blk
+    partial, acc, loss = pl.pallas_call(
+        functools.partial(head_kernel, blocks, blk, width, slots),
+        out_shape=(
+            jax.ShapeDtypeStruct((2, 2, blocks, chunk, hidden), jnp.float32),
+            jax.ShapeDtypeStruct((blocks, blk, width), jnp.float32),
+            jax.ShapeDtypeStruct((blocks, blk, LANES), jnp.float32),
+        ),
+        scratch_shapes=[
+            pltpu.VMEM((blocks, blk, 2 * width), jnp.float32),
+            pltpu.VMEM((blocks, blk, LANES), bf16),
+            pltpu.VMEM((tiles, pairs, width), bf16),
+            pltpu.VMEM((tiles, pairs, width), jnp.float32),
+            pltpu.VMEM((tiles, pairs, hidden), jnp.float32),
+            pltpu.VMEM((tiles, pairs, LANES), jnp.float32),
+            pltpu.VMEM((width, hidden), jnp.float32),
+        ],
+        compiler_params=pltpu.CompilerParams(vmem_limit_bytes=48 * 2**20),
+        name="head",
+    )(*pieces, acceptor_pos, dist_table, w_in, w_out)
+    acc = acc + swapped(acc, "tis", 1)
+    partial = partial[0] + swapped(partial[1], "rep", 1)
+    partial = partial[0] + swapped(partial[1].astype(bf16), "rep", 2).astype(jnp.float32)
+    send = jnp.concatenate([partial, acc, loss], axis=2)
+    arrived = [send[0]] + [swapped(send[k], "ctx", k) for k in range(1, blocks)]
+    return pl.pallas_call(
+        functools.partial(finish_kernel, blocks, width, hidden),
+        out_shape=(
+            jax.ShapeDtypeStruct((1, blk, tissues), jnp.float32),
+            jax.ShapeDtypeStruct((tissues, chunk, hidden), jnp.float32),
+            jax.ShapeDtypeStruct((1, blk, width), jnp.float32),
+        ),
+        name="finish",
+    )(*arrived)
+
+
+def on_device(*args):
+    donor_feat, acceptor_feat, _, _, pair_mask, _, _, hidden_weights, _ = args
+    blocks = lax.axis_size("ctx")
+    tissues, width, hidden = hidden_weights.shape
+    blk = donor_feat.shape[1]
+    fits = (
+        donor_feat.shape[0] == 1
+        and tissues == blocks == 4
+        and lax.axis_size("rep") == 4
+        and lax.axis_size("tis") == 2
+        and acceptor_feat.shape[1] == blk == 16
+        and width == 256
+        and hidden % LANES == 0
+        and pair_mask.shape[2] + 2 + tissues <= LANES
+    )
+    return shared(*args) if fits else general(*args)
 
 
 def solution(mesh):

time: 134 us -> 38.6 us (0.29)
  waiting for transfers between devices: 44.1 us -> 9.42 us
  matrix products: 22.2 us -> 0 us
  other arithmetic: 15.5 us -> 0.87 us
  between operations: 14.4 us -> 0.74 us
  Pallas kernels: 0 us -> 8.93 us
  blocking collectives: 8.77 us -> 0 us
  starting transfers between devices: 21.4 us -> 13.3 us
  local copies, waits for them, and re-layouts: 7.15 us -> 4.85 us
    reduce_scatter x1 -> x0, waiting for transfers between devices: 26 us -> none  [on_device(): lax.psum_scatter(stacked, ('ctx', 'rep'), scatter_dimension=0, tiled=True)]
    dot_general x17 -> x0, matrix products: 22.2 us -> none  [the longest x4 7.73 us: on_device(): hid = jnp.dot(flat, w_in, preferred_element_type=jnp.float32)]
    pallas_call x0 -> x2, Pallas kernels: none -> 8.93 us  [the longest x1 7.35 us: shared(): pl.pallas_call(functools.partial(head_kernel, blocks, blk, width, slots),...]
    psum x1 -> x0, blocking collectives: 8.77 us -> none  [on_device(): grad_acceptor = lax.psum(carried, 'tis')]
    ppermute x8 -> x9, waiting for transfers between devices: 18 us -> 9.42 us  [swapped(): lax.ppermute(value, axis, [(i, i ^ bits) for i in range(lax.axis_size(axi...]
    convert_element_type x5 -> x3, other arithmetic: 9.16 us -> 0.79 us  [the longest x1 0.78 us: shared(): targets[0].astype(bf16)]
    ppermute x8 -> x9, starting transfers between devices: 21.4 us -> 13.3 us  [swapped(): lax.ppermute(value, axis, [(i, i ^ bits) for i in range(lax.axis_size(axi...]
    gather x4 -> x0, local copies, waits for them, and re-layouts: 2.65 us -> none  [on_device(): jnp.take_along_axis(logits, jnp.minimum(goal, slots - 1)[..., None], axis...]
  transfers between devices with their start and end apart: 9 -> 9, of which waited for: 8 -> 6; matrix products, arithmetic and copies ran while one was open for 9% -> 0% of each run, Pallas kernels for 0% -> 0%
where the time goes in v1:
time: 38.6 us; the launch traced here: 38.1 us
  starting transfers between devices  13.3 us (34%)
  waiting for transfers between devices  9.42 us (24%)
  Pallas kernels  8.93 us (23%)
  local copies, waits for them, and re-layouts  4.85 us (13%)
  other arithmetic  0.87 us (2%)
  between operations  0.74 us (2%)
    ppermute x9, starting transfers between devices, swapped(): lax.ppermute(value, axis, [(i, i ^ bits) for i in range(lax.axis_size(axi...  13.3 us
    ppermute x9, waiting for transfers between devices, swapped(): lax.ppermute(value, axis, [(i, i ^ bits) for i in range(lax.axis_size(axi...  9.42 us
    pallas_call x1, Pallas kernels, shared(): pl.pallas_call(functools.partial(head_kernel, blocks, blk, width, slots),...  7.35 us
    unnamed x22, local copies, waits for them, and re-layouts  2.43 us
    pallas_call x1, Pallas kernels, shared(): pl.pallas_call(functools.partial(finish_kernel, blocks, width, hidden), o...  1.58 us
    pallas_call x1, local copies, waits for them, and re-layouts, shared(): pl.pallas_call(functools.partial(finish_kernel, blocks, width, hidden), o...  1.35 us
    convert_element_type x1, other arithmetic, shared(): targets[0].astype(bf16)  0.78 us
  transfers between devices with their start and end apart: 9, of which 6 were waited for; matrix products, arithmetic and copies ran while one was open for 0% of the time, Pallas kernels for 0%

profile of v1, /device:TPU:0, one launch (start us, length us, event | category | flops | bytes accessed | tf_op | source)
XLA Modules:
  0.0 38.1 jit_solution(10360051206573427278)
XLA Ops:
  0.6 0.0 copy-start
  0.6 0.0 copy-start.10
  0.7 0.8 %convert_bitcast_fusion.1 = bf16[16,4]{0,1:T(4,128)(2,1)S(1)} fusion(s32[1,16,4]{1,2,0:T(4,128)} %param.14), kind=kLoop, calls=%fused_computation.13 | loop fusion | flops 64 | bytes 384 | tf_op jit(solution)/shard_map/convert_element_type | solution.py:319
  1.4 0.0 copy-done.10
  1.4 0.0 copy-start.8
  1.5 0.1 copy.14
  1.6 0.1 copy.13
  1.6 0.1 copy.12
  1.7 0.4 %copy-done.8 = s32[1,16,80]{2,1,0:T(8,128)S(1)} copy-done((s32[1,16,80]{2,1,0:T(8,128)S(1)}, s32[1,16,80]{2,1,0:T(8,128)}, u32[]{:S(2)}) %copy-start.8) | copy-done | bytes 5144
  2.1 0.0 copy-start.6
  2.1 0.0 copy-start.7
  2.2 0.7 %copy-done.6 = bf16[1,16,256]{2,1,0:T(8,128)(2,1)S(1)} copy-done((bf16[1,16,256]{2,1,0:T(8,128)(2,1)S(1)}, bf16[1,16,256]{2,1,0:T(8,128)(2,1)}, u32[]{:S(2)}) %copy-start.6) | copy-done | bytes 8216
  2.8 0.0 copy-done.7
  2.9 0.1 concatenate.6.refs_0_
  3.0 5.1 %collective-permute-start.2 = (bf16[16,640]{1,0:T(8,128)(2,1)S(1)}, bf16[16,640]{1,0:T(8,128)(2,1)S(1)}, u32[]{:S(2)}, u32[]{:S(2)}) collective-permute-start(bf16[16,640]{1,0:T(8,128)(2,1)S(1)} %concatenate.6.refs_0_), channel_id=1, source_target_pairs={{0,24},{8,16},{16,8},{24,0},{1,25},{9,17},{17,9},{25,1},{2,26},{10... | collective-permute-start | bytes 61448 | tf_op jit(solution)/shard_map/ppermute | solution.py:24
  8.0 0.0 collective-permute-start.1
  8.0 0.6 %collective-permute-start = (bf16[16,640]{1,0:T(8,128)(2,1)S(1)}, bf16[16,640]{1,0:T(8,128)(2,1)S(1)}, u32[]{:S(2)}, u32[]{:S(2)}) collective-permute-start(bf16[16,640]{1,0:T(8,128)(2,1)S(1)} %concatenate.6.refs_0_), channel_id=1, source_target_pairs={{0,8},{8,0},{16,24},{24,16},{1,9},{9,1},{17,25},{25,17},{2,10},{10... | collective-permute-start | bytes 61448 | tf_op jit(solution)/shard_map/ppermute | solution.py:24
  8.7 0.0 copy-done
  8.7 0.0 copy-start.9
  8.7 0.7 %copy-done.9 = bf16[4,512]{1,0:T(4,128)(2,1)S(1)} copy-done((bf16[4,512]{1,0:T(4,128)(2,1)S(1)}, bf16[4,512]{1,0:T(4,128)(2,1)}, u32[]{:S(2)}) %copy-start.9) | copy-done | bytes 4120
  9.4 0.0 copy-start.2
  9.4 0.4 %collective-permute-done.2.refs_3_ = bf16[16,640]{1,0:T(8,128)(2,1)S(1)} collective-permute-done((bf16[16,640]{1,0:T(8,128)(2,1)S(1)}, bf16[16,640]{1,0:T(8,128)(2,1)S(1)}, u32[]{:S(2)}, u32[]{:S(2)}) %collective-permute-start.2) | collective-permute-done | bytes 20512 | tf_op jit(solution)/shard_map/ppermute | solution.py:24
  9.8 2.9 %collective-permute-done.1.refs_2_ = bf16[16,640]{1,0:T(8,128)(2,1)S(1)} collective-permute-done((bf16[16,640]{1,0:T(8,128)(2,1)S(1)}, bf16[16,640]{1,0:T(8,128)(2,1)S(1)}, u32[]{:S(2)}, u32[]{:S(2)}) %collective-permute-start.1) | collective-permute-done | bytes 20512 | tf_op jit(solution)/shard_map/ppermute | solution.py:24
  12.7 0.0 collective-permute-done.refs_1_
  12.7 0.0 copy-done.1
  12.7 0.0 copy-done.2
  12.7 7.3 %head.1 = (f32[2,2,4,16,512]{4,3,2,1,0:T(8,128)S(1)}, f32[4,16,256]{2,1,0:T(8,128)S(1)}, f32[4,16,128]{2,1,0:T(8,128)S(1)}) custom-call(bf16[16,640]{1,0:T(8,128)(2,1)S(1)} %concatenate.6.refs_0_, bf16[16,640]{1,0:T(8,128)(2,1)S(1)} %collective-permute-done.refs_1_, bf16[16,640]{1,0:T(8,128)(2,1)S(1)} %collective-permute-done.1.refs_2_, ...), custom_call_target="tpu_custom_call" | custom-call | tf_op jit(solution)/shard_map/head/pallas_call | solution.py:330
  20.1 0.1 collective-permute-start.3
  20.2 1.6 %collective-permute-start.5 = (f32[4,16,256]{2,1,0:T(8,128)S(1)}, f32[4,16,256]{2,1,0:T(8,128)S(1)}, u32[]{:S(2)}, u32[]{:S(2)}) collective-permute-start(f32[4,16,256]{2,1,0:T(8,128)S(1)} %get-tuple-element.7), channel_id=1, source_target_pairs={{0,4},{4,0},{1,5},{5,1},{2,6},{6,2},{3,7},{7,3},{8,12},{12,8},{9,1... | collective-permute-start | bytes 196616 | tf_op jit(solution)/shard_map/ppermute | solution.py:24
  21.8 0.0 collective-permute-done.3
  21.8 1.6 %collective-permute-start.4 = (bf16[4,16,512]{2,1,0:T(8,128)(2,1)S(1)}, bf16[4,16,512]{2,1,0:T(8,128)(2,1)S(1)}, u32[]{:S(2)}, u32[]{:S(2)}) collective-permute-start(bf16[4,16,512]{2,1,0:T(8,128)(2,1)S(1)} %fusion.1), channel_id=1, source_target_pairs={{0,2},{1,3},{2,0},{3,1},{4,6},{5,7},{6,4},{7,5},{8,10},{9,11},{10,... | collective-permute-start | bytes 196616 | tf_op jit(solution)/shard_map/ppermute | solution.py:24
  23.4 1.3 %collective-permute-done.5 = f32[4,16,256]{2,1,0:T(8,128)S(1)} collective-permute-done((f32[4,16,256]{2,1,0:T(8,128)S(1)}, f32[4,16,256]{2,1,0:T(8,128)S(1)}, u32[]{:S(2)}, u32[]{:S(2)}) %collective-permute-start.5) | collective-permute-done | bytes 65568 | tf_op jit(solution)/shard_map/ppermute | solution.py:24
  24.7 1.5 %collective-permute-done.4 = bf16[4,16,512]{2,1,0:T(8,128)(2,1)S(1)} collective-permute-done((bf16[4,16,512]{2,1,0:T(8,128)(2,1)S(1)}, bf16[4,16,512]{2,1,0:T(8,128)(2,1)S(1)}, u32[]{:S(2)}, u32[]{:S(2)}) %collective-permute-start.4) | collective-permute-done | bytes 65568 | tf_op jit(solution)/shard_map/ppermute | solution.py:24
  26.2 0.6 %slice_bitcast_fusion.2 = (f32[16,896]{1,0:T(8,128)S(1)}, f32[16,896]{1,0:T(8,128)S(1)}, f32[16,896]{1,0:T(8,128)S(1)}, f32[16,896]{1,0:T(8,128)}) fusion(f32[4,16,896]{2,1,0:T(8,128)S(1)} %pad_maximum_fusion), kind=kLoop, calls=%fused_computation.8 | loop fusion | bytes 458752 | tf_op jit(solution)/shard_map/squeeze | solution.py:353
  26.8 1.5 %collective-permute-start.8 = (f32[16,896]{1,0:T(8,128)S(1)}, f32[16,896]{1,0:T(8,128)S(1)}, u32[]{:S(2)}, u32[]{:S(2)}) collective-permute-start(f32[16,896]{1,0:T(8,128)S(1)} %get-tuple-element.12), channel_id=1, source_target_pairs={{0,24},{8,16},{16,8},{24,0},{1,25},{9,17},{17,9},{25,1},{2,26},{10... | collective-permute-start | bytes 172040 | tf_op jit(solution)/shard_map/ppermute | solution.py:24
  28.3 0.6 %collective-permute-start.7 = (f32[16,896]{1,0:T(8,128)S(1)}, f32[16,896]{1,0:T(8,128)S(1)}, u32[]{:S(2)}, u32[]{:S(2)}) collective-permute-start(f32[16,896]{1,0:T(8,128)S(1)} %get-tuple-element.13), channel_id=1, source_target_pairs={{0,16},{8,24},{16,0},{24,8},{1,17},{9,25},{17,1},{25,9},{2,18},{10... | collective-permute-start | bytes 172040 | tf_op jit(solution)/shard_map/ppermute | solution.py:24
  28.9 2.4 %collective-permute-start.6 = (f32[16,896]{1,0:T(8,128)S(1)}, f32[16,896]{1,0:T(8,128)S(1)}, u32[]{:S(2)}, u32[]{:S(2)}) collective-permute-start(f32[16,896]{1,0:T(8,128)S(1)} %get-tuple-element.14), channel_id=1, source_target_pairs={{0,8},{8,0},{16,24},{24,16},{1,9},{9,1},{17,25},{25,17},{2,10},{10... | collective-permute-start | bytes 172040 | tf_op jit(solution)/shard_map/ppermute | solution.py:24
  31.2 1.7 %collective-permute-done.8.refs_3_ = f32[16,896]{1,0:T(8,128)S(1)} collective-permute-done((f32[16,896]{1,0:T(8,128)S(1)}, f32[16,896]{1,0:T(8,128)S(1)}, u32[]{:S(2)}, u32[]{:S(2)}) %collective-permute-start.8) | collective-permute-done | bytes 57376 | tf_op jit(solution)/shard_map/ppermute | solution.py:24
  33.0 0.0 copy-start.3
  33.0 1.6 %collective-permute-done.7.refs_2_ = f32[16,896]{1,0:T(8,128)S(1)} collective-permute-done((f32[16,896]{1,0:T(8,128)S(1)}, f32[16,896]{1,0:T(8,128)S(1)}, u32[]{:S(2)}, u32[]{:S(2)}) %collective-permute-start.7) | collective-permute-done | bytes 57376 | tf_op jit(solution)/shard_map/ppermute | solution.py:24
  34.5 0.0 copy-start.4
  34.5 0.0 collective-permute-done.6.refs_1_
  34.5 0.0 copy-start.5
  34.6 0.0 copy-done.3
  34.6 0.6 %copy-done.4 = f32[16,896]{1,0:T(8,128)} copy-done((f32[16,896]{1,0:T(8,128)}, f32[16,896]{1,0:T(8,128)S(1)}, u32[]{:S(2)}) %copy-start.4) | copy-done | bytes 57368
  35.2 0.0 copy-done.5
  35.2 1.6 %finish.1 = (f32[1,16,4]{2,1,0:T(8,128)}, f32[4,16,512]{2,1,0:T(8,128)}, f32[1,16,256]{2,1,0:T(8,128)}) custom-call(f32[16,896]{1,0:T(8,128)} %get-tuple-element.15.refs_0_, f32[16,896]{1,0:T(8,128)} %copy-done.5, f32[16,896]{1,0:T(8,128)} %copy-done.4, f32[16,896]{1,0:T(8,128)} %copy-done.3), custom_call_target="tpu_custom_call" | custom-call | tf_op jit(solution)/shard_map/finish/pallas_call | solution.py:354
  36.8 1.3 %copy.15 = f32[1,16,4]{1,2,0:T(4,128)} copy(f32[1,16,4]{2,1,0:T(8,128)} %get-tuple-element.9) | data formatting | bytes 512 | tf_op jit(solution)/shard_map/finish/pallas_call | solution.py:354
  (12 shorter events, 0.1 us)
Async XLA Ops:
  0.6 8.0 %copy-start = (bf16[4,256,512]{2,1,0:T(8,128)(2,1)S(1)}, bf16[4,256,512]{2,1,0:T(8,128)(2,1)}, u32[]{:S(2)}) copy-start(bf16[4,256,512]{2,1,0:T(8,128)(2,1)} %param.16) | copy-start | bytes 3145732
  0.6 0.8 %copy-start.10 = (s32[1,16]{1,0:T(1,128)S(1)}, s32[1,16]{1,0:T(1,128)}, u32[]{:S(2)}) copy-start(s32[1,16]{1,0:T(1,128)} %param.11) | copy-start | bytes 196
  1.4 0.7 %copy-start.8 = (s32[1,16,80]{2,1,0:T(8,128)S(1)}, s32[1,16,80]{2,1,0:T(8,128)}, u32[]{:S(2)}) copy-start(s32[1,16,80]{2,1,0:T(8,128)} %param.13) | copy-start | bytes 15364
  2.1 0.7 %copy-start.6 = (bf16[1,16,256]{2,1,0:T(8,128)(2,1)S(1)}, bf16[1,16,256]{2,1,0:T(8,128)(2,1)}, u32[]{:S(2)}) copy-start(bf16[1,16,256]{2,1,0:T(8,128)(2,1)} %param.9) | copy-start | bytes 24580
  2.1 0.7 %copy-start.7 = (bf16[1,16,256]{2,1,0:T(8,128)(2,1)S(1)}, bf16[1,16,256]{2,1,0:T(8,128)(2,1)}, u32[]{:S(2)}) copy-start(bf16[1,16,256]{2,1,0:T(8,128)(2,1)} %param.10) | copy-start | bytes 24580
  3.0 6.8 %collective-permute-start.2 = (bf16[16,640]{1,0:T(8,128)(2,1)S(1)}, bf16[16,640]{1,0:T(8,128)(2,1)S(1)}, u32[]{:S(2)}, u32[]{:S(2)}) collective-permute-start(bf16[16,640]{1,0:T(8,128)(2,1)S(1)} %concatenate.6.refs_0_), channel_id=1, source_target_pairs={{0,24},{8,16},{16,8},{24,0},{1,25},{9,17},{17,9},{25,1},{2,26},{10... | collective-permute-start | bytes 61448 | tf_op jit(solution)/shard_map/ppermute | solution.py:24
  8.0 4.7 %collective-permute-start.1 = (bf16[16,640]{1,0:T(8,128)(2,1)S(1)}, bf16[16,640]{1,0:T(8,128)(2,1)S(1)}, u32[]{:S(2)}, u32[]{:S(2)}) collective-permute-start(bf16[16,640]{1,0:T(8,128)(2,1)S(1)} %concatenate.6.refs_0_), channel_id=1, source_target_pairs={{0,16},{8,24},{16,0},{24,8},{1,17},{9,25},{17,1},{25,9},{2,18},{10... | collective-permute-start | bytes 61448 | tf_op jit(solution)/shard_map/ppermute | solution.py:24
  8.0 4.7 %collective-permute-start = (bf16[16,640]{1,0:T(8,128)(2,1)S(1)}, bf16[16,640]{1,0:T(8,128)(2,1)S(1)}, u32[]{:S(2)}, u32[]{:S(2)}) collective-permute-start(bf16[16,640]{1,0:T(8,128)(2,1)S(1)} %concatenate.6.refs_0_), channel_id=1, source_target_pairs={{0,8},{8,0},{16,24},{24,16},{1,9},{9,1},{17,25},{25,17},{2,10},{10... | collective-permute-start | bytes 61448 | tf_op jit(solution)/shard_map/ppermute | solution.py:24
  8.7 0.7 %copy-start.9 = (bf16[4,512]{1,0:T(4,128)(2,1)S(1)}, bf16[4,512]{1,0:T(4,128)(2,1)}, u32[]{:S(2)}) copy-start(bf16[4,512]{1,0:T(4,128)(2,1)} %param.17) | copy-start | bytes 12292
  8.7 4.0 %copy-start.1 = (bf16[128,256]{1,0:T(8,128)(2,1)S(1)}, bf16[128,256]{1,0:T(8,128)(2,1)}, u32[]{:S(2)}) copy-start(bf16[128,256]{1,0:T(8,128)(2,1)} %refs_5_.1) | copy-start | bytes 196612
  9.4 3.4 %copy-start.2 = (s32[1,64]{1,0:T(1,128)S(1)}, s32[1,64]{1,0:T(1,128)}, u32[]{:S(2)}) copy-start(s32[1,64]{1,0:T(1,128)} %refs_4_.1) | copy-start | bytes 772
  20.1 1.7 %collective-permute-start.3 = (f32[2,4,16,512]{3,2,1,0:T(8,128)S(1)}, f32[2,4,16,512]{3,2,1,0:T(8,128)S(1)}, u32[]{:S(2)}, u32[]{:S(2)}) collective-permute-start(f32[2,4,16,512]{3,2,1,0:T(8,128)S(1)} %slice_bitcast_fusion), channel_id=1, source_target_pairs={{0,1},{1,0},{2,3},{3,2},{4,5},{5,4},{6,7},{7,6},{8,9},{9,8},{10,11... | collective-permute-start | bytes 786440 | tf_op jit(solution)/shard_map/ppermute | solution.py:24
  20.2 4.5 %collective-permute-start.5 = (f32[4,16,256]{2,1,0:T(8,128)S(1)}, f32[4,16,256]{2,1,0:T(8,128)S(1)}, u32[]{:S(2)}, u32[]{:S(2)}) collective-permute-start(f32[4,16,256]{2,1,0:T(8,128)S(1)} %get-tuple-element.7), channel_id=1, source_target_pairs={{0,4},{4,0},{1,5},{5,1},{2,6},{6,2},{3,7},{7,3},{8,12},{12,8},{9,1... | collective-permute-start | bytes 196616 | tf_op jit(solution)/shard_map/ppermute | solution.py:24
  21.8 4.3 %collective-permute-start.4 = (bf16[4,16,512]{2,1,0:T(8,128)(2,1)S(1)}, bf16[4,16,512]{2,1,0:T(8,128)(2,1)S(1)}, u32[]{:S(2)}, u32[]{:S(2)}) collective-permute-start(bf16[4,16,512]{2,1,0:T(8,128)(2,1)S(1)} %fusion.1), channel_id=1, source_target_pairs={{0,2},{1,3},{2,0},{3,1},{4,6},{5,7},{6,4},{7,5},{8,10},{9,11},{10,... | collective-permute-start | bytes 196616 | tf_op jit(solution)/shard_map/ppermute | solution.py:24
  26.8 6.1 %collective-permute-start.8 = (f32[16,896]{1,0:T(8,128)S(1)}, f32[16,896]{1,0:T(8,128)S(1)}, u32[]{:S(2)}, u32[]{:S(2)}) collective-permute-start(f32[16,896]{1,0:T(8,128)S(1)} %get-tuple-element.12), channel_id=1, source_target_pairs={{0,24},{8,16},{16,8},{24,0},{1,25},{9,17},{17,9},{25,1},{2,26},{10... | collective-permute-start | bytes 172040 | tf_op jit(solution)/shard_map/ppermute | solution.py:24
  28.3 6.3 %collective-permute-start.7 = (f32[16,896]{1,0:T(8,128)S(1)}, f32[16,896]{1,0:T(8,128)S(1)}, u32[]{:S(2)}, u32[]{:S(2)}) collective-permute-start(f32[16,896]{1,0:T(8,128)S(1)} %get-tuple-element.13), channel_id=1, source_target_pairs={{0,16},{8,24},{16,0},{24,8},{1,17},{9,25},{17,1},{25,9},{2,18},{10... | collective-permute-start | bytes 172040 | tf_op jit(solution)/shard_map/ppermute | solution.py:24
  28.9 5.7 %collective-permute-start.6 = (f32[16,896]{1,0:T(8,128)S(1)}, f32[16,896]{1,0:T(8,128)S(1)}, u32[]{:S(2)}, u32[]{:S(2)}) collective-permute-start(f32[16,896]{1,0:T(8,128)S(1)} %get-tuple-element.14), channel_id=1, source_target_pairs={{0,8},{8,0},{16,24},{24,16},{1,9},{9,1},{17,25},{25,17},{2,10},{10... | collective-permute-start | bytes 172040 | tf_op jit(solution)/shard_map/ppermute | solution.py:24
  33.0 1.6 %copy-start.3 = (f32[16,896]{1,0:T(8,128)}, f32[16,896]{1,0:T(8,128)S(1)}, u32[]{:S(2)}) copy-start(f32[16,896]{1,0:T(8,128)S(1)} %collective-permute-done.8.refs_3_) | copy-start | bytes 172036
  34.5 0.6 %copy-start.4 = (f32[16,896]{1,0:T(8,128)}, f32[16,896]{1,0:T(8,128)S(1)}, u32[]{:S(2)}) copy-start(f32[16,896]{1,0:T(8,128)S(1)} %collective-permute-done.7.refs_2_) | copy-start | bytes 172036
  34.5 0.6 %copy-start.5 = (f32[16,896]{1,0:T(8,128)}, f32[16,896]{1,0:T(8,128)S(1)}, u32[]{:S(2)}) copy-start(f32[16,896]{1,0:T(8,128)S(1)} %collective-permute-done.6.refs_1_) | copy-start | bytes 172036

commit v2 on v0

--- a/solution.py
+++ b/solution.py
@@ -1,12 +1,17 @@
+import functools
+
 import jax
 import jax.numpy as jnp
 from jax import lax
+from jax.experimental import pallas as pl
+from jax.experimental.pallas import tpu as pltpu
 from jax.sharding import PartitionSpec as P
 
 BLOCK_BP = 65536
 SPAN_BLOCKS = 4
 BIN_BP = 2048
 BINS = 128
+LANES = 128
 
 
 def passed_along(value, axis, steps):
@@ -15,12 +20,16 @@
     return lax.ppermute(value, axis, [(source, source + steps) for source in range(first, last)])
 
 
+def swapped(value, axis, bits):
+    return lax.ppermute(value, axis, [(i, i ^ bits) for i in range(lax.axis_size(axis))])
+
+
 def silu_grad(values):
     sig = jax.nn.sigmoid(values)
     return sig * (1.0 + values * (1.0 - sig))
 
 
-def on_device(
+def general(
     donor_feat,
     acceptor_feat,
     donor_pos,
@@ -38,10 +47,12 @@
     slots = reach * acc_blk
     here = lax.axis_index("ctx")
     pieces = [acceptor_feat]
-    current = acceptor_feat
     for offset in range(1, reach):
-        current = passed_along(current, "ctx", -1)
-        pieces.append(current)
+        pieces.append(
+            passed_along(acceptor_feat, "ctx", -offset)
+            if offset < blocks
+            else jnp.zeros_like(acceptor_feat)
+        )
     window = jnp.stack(pieces, axis=1).reshape(seq_dev, slots, width)
     pos_pad = jnp.concatenate(
         [acceptor_pos, jnp.zeros((seq_dev, SPAN_BLOCKS * acc_blk), jnp.int32)], axis=1
@@ -81,13 +92,10 @@
         top = jnp.maximum(jnp.max(masked, axis=-1), 0.0)
         expo = jnp.exp(masked - top[..., None])
         total = jnp.sum(expo, axis=-1) + jnp.exp(-top)
-        picked = jnp.take_along_axis(logits, jnp.minimum(goal, slots - 1)[..., None], axis=-1)[
-            ..., 0
-        ]
-        picked = jnp.where(goal == slots, 0.0, picked)
+        onehot = goal[..., None] == slot_ids
+        picked = jnp.sum(jnp.where(onehot, logits, 0.0), axis=-1)
         losses.append(top + jnp.log(total) - picked)
-        onehot = (goal[..., None] == slot_ids).astype(jnp.float32)
-        grad_logits = expo / total[..., None] - onehot
+        grad_logits = expo / total[..., None] - onehot.astype(jnp.float32)
         grad_act = grad_logits.reshape(-1)[:, None] * w_out.astype(jnp.float32)[None, :]
         grad_hid = (grad_act * silu_grad(hid)).astype(jnp.bfloat16)
         grad_pair = grad_pair + lax.dot_general(
@@ -104,12 +112,325 @@
     )
     grad_pre = grad_pair.reshape(seq_dev, don_blk, slots, width) * silu_grad(pre)
     contrib = jnp.sum(grad_pre, axis=1).reshape(seq_dev, reach, acc_blk, width)
-    carried = contrib[:, reach - 1]
-    for offset in range(reach - 2, -1, -1):
-        carried = passed_along(carried, "ctx", 1) + contrib[:, offset]
+    carried = contrib[:, 0]
+    for offset in range(1, min(reach, blocks)):
+        carried = carried + passed_along(contrib[:, offset], "ctx", offset)
     grad_acceptor = lax.psum(carried, "tis")
     donor_loss = jnp.stack(losses, axis=-1)
     return (donor_loss, grad_hidden, grad_acceptor)
+
+
+def halved(value):
+    return (value.astype(jnp.float32) * 0.5).astype(value.dtype)
+
+
+def silu_parts(half):
+    turn = jnp.tanh(half)
+    tilted = half * turn
+    return half + tilted, (1.0 + turn) * ((1.0 + half) - tilted)
+
+
+def ones_dot(left, right):
+    return jnp.dot(left, right, preferred_element_type=jnp.float32)
+
+
+def tiles_of(blocks):
+    return [(b, a) for b in range(blocks) for a in range(b, min(blocks, b + SPAN_BLOCKS + 1))]
+
+
+def head_kernel(blocks, blk, width, *refs):
+    packed = refs[:blocks]
+    (table_ref, w_ref, wo_ref) = refs[blocks : blocks + 3]
+    (gh_ref, loss_ref, grad_s, dpre_s) = refs[blocks + 3 : blocks + 7]
+    (source, aux, picks_s, pair_s, act_s, dhid_s, gh_s) = refs[blocks + 7 :]
+    here = lax.axis_index("ctx")
+    rep = lax.axis_index("rep")
+    cross = lax.div(rep, 2)
+    core = lax.rem(rep, 2)
+    f32, bf16 = jnp.float32, jnp.bfloat16
+    hidden = w_ref.shape[1]
+    pairs = blk * blk
+    sites = blocks * blk
+    tiles = tiles_of(blocks)
+
+    source[:BINS, :] = table_ref[...]
+    for k in range(blocks):
+        start = pl.multiple_of((here ^ k) * blk, blk)
+        piece = packed[k][...].astype(bf16)
+        source[pl.ds(BINS + start, blk), :] = halved(piece[:, :width])
+        source[pl.ds(BINS + sites + start, blk), :] = halved(piece[:, width : 2 * width])
+        aux[pl.ds(start, blk), :] = piece[:, 2 * width :]
+
+    w_half = w_ref[...]
+    w_out = wo_ref[...]
+    w_rows = jnp.broadcast_to(w_out, (LANES, hidden)).astype(bf16)
+    w_out = w_out * 0.5
+    ones = jnp.ones((LANES, LANES), bf16)
+    lane3 = lax.broadcasted_iota(jnp.int32, (blk, blk, LANES), 2)
+    row3 = lax.broadcasted_iota(jnp.int32, (blk, blk, LANES), 1)
+    don3 = lax.broadcasted_iota(jnp.int32, (blk, blk, LANES), 0)
+    lane_f = lax.broadcasted_iota(jnp.int32, (pairs, LANES), 1).astype(f32)
+    from_donor = [
+        jnp.where(lane3 == don3 + b * blk, 1.0, 0.0).astype(bf16).reshape(pairs, LANES)
+        for b in range(blocks)
+    ]
+    from_acceptor = [
+        jnp.where(lane3 == row3 + (sites + a * blk), 1.0, 0.0).astype(bf16).reshape(pairs, LANES)
+        for a in range(blocks)
+    ]
+    slot_of = [lane3 == row3 + a * blk for a in range(blocks)]
+    twice_of = [pick | (lane3 == row3 + (sites + a * blk)) for a, pick in enumerate(slot_of)]
+    lanes = lax.broadcasted_iota(jnp.int32, (blk, LANES), 1)
+    codes = [aux[b * blk : (b + 1) * blk, :].astype(f32) for b in range(blocks)]
+    for tile, (b, a) in enumerate(tiles):
+        code = jnp.where(slot_of[a], codes[b][:, None, :], 0.0).astype(bf16)
+        code = ones_dot(code.reshape(pairs, LANES), ones)
+        picks_s[tile] = jnp.where(code == lane_f, 1.0, 0.0).astype(bf16)
+    for tile, (b, a) in enumerate(tiles):
+        picks = jnp.concatenate([picks_s[tile], from_donor[b] + from_acceptor[a]], axis=1)
+        value, slope = silu_parts(ones_dot(picks, source[...]))
+        pair_s[tile] = value.astype(bf16)
+        dpre_s[tile] = slope
+    for tile in range(len(tiles)):
+        value, slope = silu_parts(ones_dot(pair_s[tile], w_half))
+        act_s[tile] = value.astype(bf16)
+        dhid_s[tile] = slope * w_out
+    spread_out = [jnp.zeros((blk, blk, LANES), f32)] * blocks
+    for tile, (b, a) in enumerate(tiles):
+        logit = lax.dot_general(
+            act_s[tile], w_rows, (((1,), (1,)), ((), ())), preferred_element_type=f32
+        )
+        spread_out[b] = jnp.where(slot_of[a], logit.reshape(blk, blk, LANES), spread_out[b])
+    grads = []
+    for b in range(blocks):
+        logit = jnp.sum(spread_out[b], axis=1)
+        valid = (codes[b] >= 0.0) & (lanes < sites)
+        goal = jnp.sum(jnp.where(lanes == sites + here, codes[b], 0.0), axis=1, keepdims=True)
+        chosen = lanes == goal.astype(jnp.int32)
+        masked = jnp.where(valid, logit, -jnp.inf)
+        top = jnp.maximum(jnp.max(masked, axis=1, keepdims=True), 0.0)
+        expo = jnp.exp(masked - top)
+        total = jnp.sum(expo, axis=1, keepdims=True) + jnp.exp(-top)
+        picked = jnp.sum(jnp.where(chosen, logit, 0.0), axis=1, keepdims=True)
+        loss_ref[b ^ here] = jnp.broadcast_to(top + jnp.log(total) - picked, (blk, LANES))
+        grad = expo / total - jnp.where(chosen, 1.0, 0.0)
+        high = grad.astype(bf16).astype(f32)
+        grads.append(high + pltpu.roll(grad - high, sites, 1))
+    for tile, (b, a) in enumerate(tiles):
+        rows = jnp.where(twice_of[a], grads[b][:, None, :], 0.0).astype(bf16)
+        rows = ones_dot(rows.reshape(pairs, LANES), ones)
+        rows = jnp.concatenate([rows] * (hidden // LANES), axis=1)
+        grad_s[tile] = (rows * dhid_s[tile]).astype(bf16)
+    count = len(tiles) * pairs
+    gh_s[...] = lax.dot_general(
+        pair_s[...].reshape(count, width),
+        grad_s[...].reshape(count, hidden),
+        (((0,), (0,)), ((), ())),
+        preferred_element_type=f32,
+    )
+    chunk = gh_ref.shape[3]
+    for c in range(blocks):
+        for x in range(2):
+            for y in range(2):
+                start = ((c * 2 + x) * 2 + y) * chunk
+                gh_ref[y ^ core, x ^ cross, c ^ here] = gh_s[start : start + chunk, :]
+
+
+def finish_kernel(parts, width, hidden, *refs):
+    pieces = refs[:parts]
+    (loss_ref, gh_ref, acc_ref) = refs[parts:]
+    here = lax.axis_index("ctx")
+    blk = pieces[0].shape[0]
+    total = None
+    diagonal = lax.broadcasted_iota(jnp.int32, (blk, LANES), 0) == lax.broadcasted_iota(
+        jnp.int32, (blk, LANES), 1
+    )
+    for k in range(parts):
+        owner = here ^ k
+        gh_ref[owner] = pieces[k][:, :hidden]
+        acc = pieces[k][:, hidden : hidden + width]
+        total = acc if total is None else total + acc
+        row = jnp.sum(
+            jnp.where(diagonal, pieces[k][:, hidden + width :], 0.0), axis=0, keepdims=True
+        )
+        loss_ref[0, pl.ds(owner, 1), :] = row[:, :blk]
+    acc_ref[0] = total
+
+
+def pack_kernel(
+    blocks, pos_ref, goal_ref, apos_ref, donor_hbm, acceptor_hbm, mask_hbm, out_ref, mask_ref, sems
+):
+    here = lax.axis_index("ctx")
+    f32, bf16 = jnp.float32, jnp.bfloat16
+    _, blk, width = donor_hbm.shape
+    copies = [
+        pltpu.make_async_copy(mask_hbm, mask_ref, sems.at[0]),
+        pltpu.make_async_copy(donor_hbm.at[0], out_ref.at[:, :width], sems.at[1]),
+        pltpu.make_async_copy(acceptor_hbm.at[0], out_ref.at[:, width : 2 * width], sems.at[2]),
+    ]
+    for copy in copies:
+        copy.start()
+    tissues = goal_ref.shape[1]
+    slots = mask_ref.shape[2]
+    sites = blocks * blk
+    lanes = lax.broadcasted_iota(jnp.int32, (blk, LANES), 1)
+    rows = lax.broadcasted_iota(jnp.int32, (blk, LANES), 0)
+    dpos = jnp.zeros((blk, LANES), jnp.int32)
+    goal = jnp.zeros((blk, LANES), jnp.int32)
+    for i in range(blk):
+        dpos = jnp.where(rows == i, pos_ref[0, i], dpos)
+        for t in range(tissues):
+            goal = jnp.where((rows == i) & (lanes == sites + t), goal_ref[0, t, i], goal)
+    apos = jnp.zeros((1, LANES), jnp.int32)
+    line = lax.broadcasted_iota(jnp.int32, (1, LANES), 1)
+    for j in range(sites):
+        apos = jnp.where(line == j, apos_ref[0, j], apos)
+    dist = (lanes // blk - here) * BLOCK_BP + apos - dpos
+    goal = jnp.where(goal == slots, -1, goal + here * blk)
+    spot = lax.broadcasted_iota(jnp.int32, (LANES, LANES), 0)
+    onto = lax.broadcasted_iota(jnp.int32, (LANES, LANES), 1)
+    shift = jnp.where((onto == spot + here * blk) & (spot < slots), 1.0, 0.0).astype(bf16)
+    copies[0].wait()
+    mask = jnp.concatenate(
+        [mask_ref[0], jnp.zeros((blk, LANES - slots), jnp.int32)], axis=1
+    )
+    mask = ones_dot(mask.astype(f32).astype(bf16), shift)
+    valid = (mask > 0.5) & (dist > 0) & (dist <= SPAN_BLOCKS * BLOCK_BP) & (lanes < sites)
+    code = jnp.where(valid, jnp.clip((dist - 1) // BIN_BP, 0, BINS - 1), -1)
+    code = jnp.where(lanes < sites, code, goal)
+    out_ref[:, 2 * width :] = code.astype(f32).astype(bf16)
+    copies[1].wait()
+    copies[2].wait()
+
+
+def acceptor_kernel(blocks, blk, grad_ref, w_ref, slope_ref, out_ref):
+    here = lax.axis_index("ctx")
+    width = w_ref.shape[0]
+    w = w_ref[...]
+    total = [None] * blocks
+    for tile, (_, a) in enumerate(tiles_of(blocks)):
+        grad_pair = lax.dot_general(
+            grad_ref[tile], w, (((1,), (1,)), ((), ())), preferred_element_type=jnp.float32
+        )
+        part = jnp.sum((grad_pair * slope_ref[tile]).reshape(blk, blk, width), axis=0)
+        total[a] = part if total[a] is None else total[a] + part
+    for a in range(blocks):
+        out_ref[a ^ here] = total[a]
+
+
+def shared(
+    donor_feat,
+    acceptor_feat,
+    donor_pos,
+    acceptor_pos,
+    pair_mask,
+    targets,
+    dist_table,
+    hidden_weights,
+    output_weights,
+):
+    _, blk, width = donor_feat.shape
+    blocks = lax.axis_size("ctx")
+    tissues, _, hidden = hidden_weights.shape
+    bf16 = jnp.bfloat16
+    f32 = jnp.float32
+    anywhere = pl.BlockSpec(memory_space=pl.ANY)
+    smem = pl.BlockSpec(memory_space=pltpu.SMEM)
+    packed = pl.pallas_call(
+        functools.partial(pack_kernel, blocks),
+        in_specs=[smem] * 3 + [anywhere] * 3,
+        out_specs=pl.BlockSpec(memory_space=pltpu.VMEM),
+        out_shape=jax.ShapeDtypeStruct((blk, 2 * width + LANES), bf16),
+        scratch_shapes=[
+            pltpu.VMEM(pair_mask.shape, jnp.int32),
+            pltpu.SemaphoreType.DMA((3,)),
+        ],
+        compiler_params=pltpu.CompilerParams(vmem_limit_bytes=60 * 2**20),
+        name="pack",
+    )(
+        donor_pos,
+        jnp.transpose(targets, (0, 2, 1)),
+        acceptor_pos,
+        donor_feat,
+        acceptor_feat,
+        pair_mask,
+    )
+    here = lax.axis_index("ctx")
+    table = halved(dist_table)
+    w_in = halved(lax.dynamic_index_in_dim(hidden_weights, here, 0, False))
+    w_out = lax.dynamic_index_in_dim(output_weights, here, 0, True).astype(f32)
+    pieces = [packed.astype(f32)] + [swapped(packed, "ctx", k) for k in range(1, blocks)]
+    tiles = len(tiles_of(blocks))
+    chunk = width // (4 * blocks)
+    pairs = blk * blk
+    partial, loss, grad, slope = pl.pallas_call(
+        functools.partial(head_kernel, blocks, blk, width),
+        out_shape=(
+            jax.ShapeDtypeStruct((2, 2, blocks, chunk, hidden), f32),
+            jax.ShapeDtypeStruct((blocks, blk, LANES), f32),
+            jax.ShapeDtypeStruct((tiles, pairs, hidden), bf16),
+            jax.ShapeDtypeStruct((tiles, pairs, width), f32),
+        ),
+        scratch_shapes=[
+            pltpu.VMEM((BINS + 2 * blocks * blk, width), bf16),
+            pltpu.VMEM((blocks * blk, LANES), bf16),
+            pltpu.VMEM((tiles, pairs, BINS), bf16),
+            pltpu.VMEM((tiles, pairs, width), bf16),
+            pltpu.VMEM((tiles, pairs, hidden), bf16),
+            pltpu.VMEM((tiles, pairs, hidden), f32),
+            pltpu.VMEM((width, hidden), f32),
+        ],
+        compiler_params=pltpu.CompilerParams(vmem_limit_bytes=32 * 2**20),
+        name="head",
+    )(*pieces, table, w_in, w_out)
+    kept, sent = partial[0], swapped(partial[1], "rep", 1)
+    acc = pl.pallas_call(
+        functools.partial(acceptor_kernel, blocks, blk),
+        out_shape=jax.ShapeDtypeStruct((blocks, blk, width), f32),
+        compiler_params=pltpu.CompilerParams(vmem_limit_bytes=16 * 2**20),
+        cost_estimate=pl.CostEstimate(
+            flops=2 * tiles * pairs * width * hidden,
+            bytes_accessed=tiles * pairs * (2 * hidden + 4 * width),
+            transcendentals=0,
+        ),
+        name="acceptors",
+    )(grad, w_in, slope)
+    partial = kept + sent
+    sent = swapped(partial[1].astype(bf16), "rep", 2)
+    acc = acc + swapped(acc, "tis", 1)
+    partial = partial[0] + sent.astype(jnp.float32)
+    send = jnp.concatenate([partial, acc, loss], axis=2)
+    arrived = [send[0]] + [swapped(send[k], "ctx", k) for k in range(1, blocks)]
+    donor_loss, grad_hidden, grad_acceptor = pl.pallas_call(
+        functools.partial(finish_kernel, blocks, width, hidden),
+        out_shape=(
+            jax.ShapeDtypeStruct((1, tissues, blk), jnp.float32),
+            jax.ShapeDtypeStruct((tissues, chunk, hidden), jnp.float32),
+            jax.ShapeDtypeStruct((1, blk, width), jnp.float32),
+        ),
+        compiler_params=pltpu.CompilerParams(vmem_limit_bytes=8 * 2**20),
+        name="finish",
+    )(*arrived)
+    return (jnp.transpose(donor_loss, (0, 2, 1)), grad_hidden, grad_acceptor)
+
+
+def on_device(*args):
+    donor_feat, acceptor_feat, _, _, pair_mask, _, _, hidden_weights, _ = args
+    blocks = lax.axis_size("ctx")
+    tissues, width, hidden = hidden_weights.shape
+    blk = donor_feat.shape[1]
+    fits = (
+        donor_feat.shape[0] == 1
+        and tissues == blocks == 4
+        and lax.axis_size("rep") == 4
+        and lax.axis_size("tis") == 2
+        and acceptor_feat.shape[1] == blk == 16
+        and width == 256
+        and hidden % LANES == 0
+        and pair_mask.shape[2] == (SPAN_BLOCKS + 1) * blk
+        and BINS == LANES == 2 * blocks * blk
+    )
+    return shared(*args) if fits else general(*args)
 
 
 def solution(mesh):

time: 134 us -> 33.4 us (0.25)
  waiting for transfers between devices: 44.1 us -> 7.45 us
  matrix products: 22.2 us -> 0 us
  between operations: 14.4 us -> 0.72 us
  other arithmetic: 15.5 us -> 3.37 us
  blocking collectives: 8.77 us -> 0 us
  Pallas kernels: 0 us -> 8.02 us
  starting transfers between devices: 21.4 us -> 13.4 us
  local copies, waits for them, and re-layouts: 7.15 us -> 0.05 us
    reduce_scatter x1 -> x0, waiting for transfers between devices: 26 us -> none  [on_device(): lax.psum_scatter(stacked, ('ctx', 'rep'), scatter_dimension=0, tiled=True)]
    dot_general x17 -> x0, matrix products: 22.2 us -> none  [the longest x4 7.73 us: on_device(): hid = jnp.dot(flat, w_in, preferred_element_type=jnp.float32)]
    ppermute x8 -> x9, waiting for transfers between devices: 18 us -> 7.45 us  [swapped(): lax.ppermute(value, axis, [(i, i ^ bits) for i in range(lax.axis_size(axi...]
    psum x1 -> x0, blocking collectives: 8.77 us -> none  [on_device(): grad_acceptor = lax.psum(carried, 'tis')]
    pallas_call x0 -> x4, Pallas kernels: none -> 8.02 us  [the longest x1 4.29 us: shared(): pl.pallas_call(functools.partial(head_kernel, blocks, blk, width), out_sh...]
    ppermute x8 -> x9, starting transfers between devices: 21.4 us -> 13.4 us  [swapped(): lax.ppermute(value, axis, [(i, i ^ bits) for i in range(lax.axis_size(axi...]
    convert_element_type x5 -> x4, other arithmetic: 9.16 us -> 3.28 us  [the longest x2 1.85 us: halved(): return (value.astype(jnp.float32) * 0.5).astype(value.dtype)]
    unnamed x28 -> x0, local copies, waits for them, and re-layouts: 3.33 us -> none
  transfers between devices with their start and end apart: 9 -> 9, of which waited for: 8 -> 5; matrix products, arithmetic and copies ran while one was open for 9% -> 10% of each run, Pallas kernels for 0% -> 3%
where the time goes in v2:
time: 33.4 us; the launch traced here: 33 us
  starting transfers between devices  13.4 us (40%)
  Pallas kernels  8.02 us (24%)
  waiting for transfers between devices  7.45 us (22%)
  other arithmetic  3.37 us (10%)
  between operations  0.72 us (2%)
    ppermute x9, starting transfers between devices, swapped(): lax.ppermute(value, axis, [(i, i ^ bits) for i in range(lax.axis_size(axi...  13.4 us
    ppermute x9, waiting for transfers between devices, swapped(): lax.ppermute(value, axis, [(i, i ^ bits) for i in range(lax.axis_size(axi...  7.45 us
    pallas_call x1, Pallas kernels, shared(): pl.pallas_call(functools.partial(head_kernel, blocks, blk, width), out_sh...  4.29 us
    pallas_call x1, Pallas kernels, shared(): pl.pallas_call(functools.partial(pack_kernel, blocks), in_specs=[smem] *...  2.17 us
    convert_element_type x2, other arithmetic, halved(): return (value.astype(jnp.float32) * 0.5).astype(value.dtype)  1.85 us
    pallas_call x1, Pallas kernels, shared(): pl.pallas_call(functools.partial(acceptor_kernel, blocks, blk), out_shape...  0.88 us
    convert_element_type x1, other arithmetic, shared(): packed.astype(f32)  0.73 us
    convert_element_type x1, other arithmetic, shared(): w_out = lax.dynamic_index_in_dim(output_weights, here, 0, True).astype(f32)  0.7 us
  transfers between devices with their start and end apart: 9, of which 5 were waited for; matrix products, arithmetic and copies ran while one was open for 10% of the time, Pallas kernels for 3%

profile of v2, /device:TPU:0, one launch (start us, length us, event | category | flops | bytes accessed | tf_op | source)
XLA Modules:
  0.0 33.0 jit_solution(14361133525535013047)
XLA Ops:
  0.6 2.2 %pack.1 = bf16[16,640]{1,0:T(8,128)(2,1)} custom-call(s32[1,16]{1,0:T(1,128)} %pos_ref.1, s32[1,4,16]{2,1,0:T(4,128)} %bitcast.22, s32[1,64]{1,0:T(1,128)} %apos_ref.1, bf16[1,16,256]{2,1,0:T(8,128)(2,1)} %donor_hbm.1, bf16[1,16,256]{2,1,0:T(8,128)(2,1)} %acceptor_hbm.1, s32[1,16,80]{2,1,0:T(8,128)} %mask_hbm.1), custom_call_target="tpu_custom_call" | custom-call | tf_op jit(solution)/shard_map/pack/pallas_call | solution.py:339
  2.8 5.1 %collective-permute-start.2 = (bf16[16,640]{1,0:T(8,128)(2,1)}, bf16[16,640]{1,0:T(8,128)(2,1)S(1)}, u32[]{:S(2)}, u32[]{:S(2)}) collective-permute-start(bf16[16,640]{1,0:T(8,128)(2,1)} %pack.1), channel_id=1, source_target_pairs={{0,24},{8,16},{16,8},{24,0},{1,25},{9,17},{17,9},{25,1},{2,26},{10... | collective-permute-start | bytes 61448 | tf_op jit(solution)/shard_map/ppermute | solution.py:24
  7.9 0.0 collective-permute-start.1
  7.9 0.6 %collective-permute-start = (bf16[16,640]{1,0:T(8,128)(2,1)}, bf16[16,640]{1,0:T(8,128)(2,1)S(1)}, u32[]{:S(2)}, u32[]{:S(2)}) collective-permute-start(bf16[16,640]{1,0:T(8,128)(2,1)} %pack.1), channel_id=1, source_target_pairs={{0,8},{8,0},{16,24},{24,16},{1,9},{9,1},{17,25},{25,17},{2,10},{10... | collective-permute-start | bytes 61448 | tf_op jit(solution)/shard_map/ppermute | solution.py:24
  8.6 0.9 %multiply_convert_fusion.1.refs_4_ = bf16[128,256]{1,0:T(8,128)(2,1)S(1)} fusion(bf16[128,256]{1,0:T(8,128)(2,1)} %param.15), kind=kLoop, calls=%fused_computation.8 | loop fusion | flops 98304 | bytes 131072 | tf_op jit(solution)/shard_map/convert_element_type | solution.py:124
  9.4 1.0 %fusion.refs_5_.w_ref = bf16[256,512]{1,0:T(8,128)(2,1)S(1)} fusion(bf16[4,256,512]{2,1,0:T(8,128)(2,1)} %param.16, s32[]{:T(128)S(6)} %select_n.6), kind=kLoop, calls=%fused_computation.1 | loop fusion | flops 393216 | bytes 524292 | tf_op jit(solution)/shard_map/convert_element_type | solution.py:124
  10.4 0.7 %dynamic-slice_convert_fusion.refs_6_ = f32[1,512]{1,0:T(1,128)S(1)} fusion(bf16[4,512]{1,0:T(4,128)(2,1)} %param.17, s32[]{:T(128)S(6)} %select_n.6), kind=kLoop, calls=%fused_computation.14 | loop fusion | flops 512 | bytes 3076 | tf_op jit(solution)/shard_map/convert_element_type | solution.py:361
  11.1 0.7 %convert_element_type.28.refs_0_ = f32[16,640]{1,0:T(8,128)S(1)} convert(bf16[16,640]{1,0:T(8,128)(2,1)} %pack.1) | non-fusion elementwise | flops 10240 | bytes 61440 | tf_op jit(solution)/shard_map/convert_element_type | solution.py:362
  11.9 0.0 collective-permute-done.2.refs_3_
  11.9 1.0 %collective-permute-done.1.refs_2_ = bf16[16,640]{1,0:T(8,128)(2,1)S(1)} collective-permute-done((bf16[16,640]{1,0:T(8,128)(2,1)}, bf16[16,640]{1,0:T(8,128)(2,1)S(1)}, u32[]{:S(2)}, u32[]{:S(2)}) %collective-permute-start.1) | collective-permute-done | bytes 20512 | tf_op jit(solution)/shard_map/ppermute | solution.py:24
  12.8 0.0 collective-permute-done.refs_1_
  12.8 4.3 %head.1 = (f32[2,2,4,16,512]{4,3,2,1,0:T(8,128)S(1)}, f32[4,16,128]{2,1,0:T(8,128)S(1)}, bf16[10,256,512]{2,1,0:T(8,128)(2,1)S(1)}, f32[10,256,256]{2,1,0:T(8,128)S(1)}) custom-call(f32[16,640]{1,0:T(8,128)S(1)} %convert_element_type.28.refs_0_, bf16[16,640]{1,0:T(8,128)(2,1)S(1)} %collective-permute-done.refs_1_, ...), custom_call_target="tpu_custom_call" | custom-call | tf_op jit(solution)/shard_map/head/pallas_call | solution.py:366
  17.1 0.1 collective-permute-start.3
  17.2 0.9 %acceptors.1 = f32[4,16,256]{2,1,0:T(8,128)S(1)} custom-call(bf16[10,256,512]{2,1,0:T(8,128)(2,1)S(1)} %get-tuple-element.11.grad_ref, bf16[256,512]{1,0:T(8,128)(2,1)S(1)} %fusion.refs_5_.w_ref, f32[10,256,256]{2,1,0:T(8,128)S(1)} %get-tuple-element.12.slope_ref), custom_call_target="tpu_custom_call" | custom-call | flops 671088640 | bytes 5242880 | tf_op jit(solution)/shard_map/acceptors/pallas_call | solution.py:387
  18.1 1.6 %collective-permute-start.5 = (f32[4,16,256]{2,1,0:T(8,128)S(1)}, f32[4,16,256]{2,1,0:T(8,128)S(1)}, u32[]{:S(2)}, u32[]{:S(2)}) collective-permute-start(f32[4,16,256]{2,1,0:T(8,128)S(1)} %acceptors.1), channel_id=1, source_target_pairs={{0,4},{4,0},{1,5},{5,1},{2,6},{6,2},{3,7},{7,3},{8,12},{12,8},{9,1... | collective-permute-start | bytes 196616 | tf_op jit(solution)/shard_map/ppermute | solution.py:24
  19.7 0.0 collective-permute-done.3
  19.8 1.6 %collective-permute-start.4 = (bf16[4,16,512]{2,1,0:T(8,128)(2,1)S(1)}, bf16[4,16,512]{2,1,0:T(8,128)(2,1)S(1)}, u32[]{:S(2)}, u32[]{:S(2)}) collective-permute-start(bf16[4,16,512]{2,1,0:T(8,128)(2,1)S(1)} %fusion.2), channel_id=1, source_target_pairs={{0,2},{1,3},{2,0},{3,1},{4,6},{5,7},{6,4},{7,5},{8,10},{9,11},{10,... | collective-permute-start | bytes 196616 | tf_op jit(solution)/shard_map/ppermute | solution.py:24
  21.3 1.3 %collective-permute-done.5 = f32[4,16,256]{2,1,0:T(8,128)S(1)} collective-permute-done((f32[4,16,256]{2,1,0:T(8,128)S(1)}, f32[4,16,256]{2,1,0:T(8,128)S(1)}, u32[]{:S(2)}, u32[]{:S(2)}) %collective-permute-start.5) | collective-permute-done | bytes 65568 | tf_op jit(solution)/shard_map/ppermute | solution.py:24
  22.7 1.4 %collective-permute-done.4 = bf16[4,16,512]{2,1,0:T(8,128)(2,1)S(1)} collective-permute-done((bf16[4,16,512]{2,1,0:T(8,128)(2,1)S(1)}, bf16[4,16,512]{2,1,0:T(8,128)(2,1)S(1)}, u32[]{:S(2)}, u32[]{:S(2)}) %collective-permute-start.4) | collective-permute-done | bytes 65568 | tf_op jit(solution)/shard_map/ppermute | solution.py:24
  24.2 2.9 %collective-permute-start.8 = (f32[16,896]{1,0:T(8,128)S(1)}, f32[16,896]{1,0:T(8,128)S(1)}, u32[]{:S(2)}, u32[]{:S(2)}) collective-permute-start(f32[16,896]{1,0:T(8,128)S(1)} %get-tuple-element.17), channel_id=1, source_target_pairs={{0,24},{8,16},{16,8},{24,0},{1,25},{9,17},{17,9},{25,1},{2,26},{10... | collective-permute-start | bytes 172040 | tf_op jit(solution)/shard_map/ppermute | solution.py:24
  27.1 0.0 collective-permute-start.7
  27.1 1.6 %collective-permute-start.6 = (f32[16,896]{1,0:T(8,128)S(1)}, f32[16,896]{1,0:T(8,128)S(1)}, u32[]{:S(2)}, u32[]{:S(2)}) collective-permute-start(f32[16,896]{1,0:T(8,128)S(1)} %get-tuple-element.19), channel_id=1, source_target_pairs={{0,8},{8,0},{16,24},{24,16},{1,9},{9,1},{17,25},{25,17},{2,10},{10... | collective-permute-start | bytes 172040 | tf_op jit(solution)/shard_map/ppermute | solution.py:24
  28.6 1.6 %collective-permute-done.8.refs_3_ = f32[16,896]{1,0:T(8,128)S(1)} collective-permute-done((f32[16,896]{1,0:T(8,128)S(1)}, f32[16,896]{1,0:T(8,128)S(1)}, u32[]{:S(2)}, u32[]{:S(2)}) %collective-permute-start.8) | collective-permute-done | bytes 57376 | tf_op jit(solution)/shard_map/ppermute | solution.py:24
  30.2 2.1 %collective-permute-done.7.refs_2_ = f32[16,896]{1,0:T(8,128)S(1)} collective-permute-done((f32[16,896]{1,0:T(8,128)S(1)}, f32[16,896]{1,0:T(8,128)S(1)}, u32[]{:S(2)}, u32[]{:S(2)}) %collective-permute-start.7) | collective-permute-done | bytes 57376 | tf_op jit(solution)/shard_map/ppermute | solution.py:24
  32.3 0.0 collective-permute-done.6.refs_1_
  32.3 0.7 %finish.1 = (f32[1,4,16]{2,1,0:T(4,128)}, f32[4,16,512]{2,1,0:T(8,128)}, f32[1,16,256]{2,1,0:T(8,128)}) custom-call(f32[16,896]{1,0:T(8,128)S(1)} %get-tuple-element.20.refs_0_, f32[16,896]{1,0:T(8,128)S(1)} %collective-permute-done.6.refs_1_, f32[16,896]{1,0:T(8,128)S(1)} %collective-permute-done.7.refs_2_, f32[16,896]{1,0:T(8,128)S(1)} %collective-permute-done.8.refs_3_), custom_call_target="tpu_custom_call" | custom-call | tf_op jit(solution)/shard_map/finish/pallas_call | solution.py:404
  (7 shorter events, 0.1 us)
Async XLA Ops:
  2.8 9.1 %collective-permute-start.2 = (bf16[16,640]{1,0:T(8,128)(2,1)}, bf16[16,640]{1,0:T(8,128)(2,1)S(1)}, u32[]{:S(2)}, u32[]{:S(2)}) collective-permute-start(bf16[16,640]{1,0:T(8,128)(2,1)} %pack.1), channel_id=1, source_target_pairs={{0,24},{8,16},{16,8},{24,0},{1,25},{9,17},{17,9},{25,1},{2,26},{10... | collective-permute-start | bytes 61448 | tf_op jit(solution)/shard_map/ppermute | solution.py:24
  7.9 4.9 %collective-permute-start.1 = (bf16[16,640]{1,0:T(8,128)(2,1)}, bf16[16,640]{1,0:T(8,128)(2,1)S(1)}, u32[]{:S(2)}, u32[]{:S(2)}) collective-permute-start(bf16[16,640]{1,0:T(8,128)(2,1)} %pack.1), channel_id=1, source_target_pairs={{0,16},{8,24},{16,0},{24,8},{1,17},{9,25},{17,1},{25,9},{2,18},{10... | collective-permute-start | bytes 61448 | tf_op jit(solution)/shard_map/ppermute | solution.py:24
  7.9 4.9 %collective-permute-start = (bf16[16,640]{1,0:T(8,128)(2,1)}, bf16[16,640]{1,0:T(8,128)(2,1)S(1)}, u32[]{:S(2)}, u32[]{:S(2)}) collective-permute-start(bf16[16,640]{1,0:T(8,128)(2,1)} %pack.1), channel_id=1, source_target_pairs={{0,8},{8,0},{16,24},{24,16},{1,9},{9,1},{17,25},{25,17},{2,10},{10... | collective-permute-start | bytes 61448 | tf_op jit(solution)/shard_map/ppermute | solution.py:24
  17.1 2.6 %collective-permute-start.3 = (f32[2,4,16,512]{3,2,1,0:T(8,128)S(1)}, f32[2,4,16,512]{3,2,1,0:T(8,128)S(1)}, u32[]{:S(2)}, u32[]{:S(2)}) collective-permute-start(f32[2,4,16,512]{3,2,1,0:T(8,128)S(1)} %slice_bitcast_fusion), channel_id=1, source_target_pairs={{0,1},{1,0},{2,3},{3,2},{4,5},{5,4},{6,7},{7,6},{8,9},{9,8},{10,11... | collective-permute-start | bytes 786440 | tf_op jit(solution)/shard_map/ppermute | solution.py:24
  18.1 4.6 %collective-permute-start.5 = (f32[4,16,256]{2,1,0:T(8,128)S(1)}, f32[4,16,256]{2,1,0:T(8,128)S(1)}, u32[]{:S(2)}, u32[]{:S(2)}) collective-permute-start(f32[4,16,256]{2,1,0:T(8,128)S(1)} %acceptors.1), channel_id=1, source_target_pairs={{0,4},{4,0},{1,5},{5,1},{2,6},{6,2},{3,7},{7,3},{8,12},{12,8},{9,1... | collective-permute-start | bytes 196616 | tf_op jit(solution)/shard_map/ppermute | solution.py:24
  19.8 4.3 %collective-permute-start.4 = (bf16[4,16,512]{2,1,0:T(8,128)(2,1)S(1)}, bf16[4,16,512]{2,1,0:T(8,128)(2,1)S(1)}, u32[]{:S(2)}, u32[]{:S(2)}) collective-permute-start(bf16[4,16,512]{2,1,0:T(8,128)(2,1)S(1)} %fusion.2), channel_id=1, source_target_pairs={{0,2},{1,3},{2,0},{3,1},{4,6},{5,7},{6,4},{7,5},{8,10},{9,11},{10,... | collective-permute-start | bytes 196616 | tf_op jit(solution)/shard_map/ppermute | solution.py:24
  24.2 6.0 %collective-permute-start.8 = (f32[16,896]{1,0:T(8,128)S(1)}, f32[16,896]{1,0:T(8,128)S(1)}, u32[]{:S(2)}, u32[]{:S(2)}) collective-permute-start(f32[16,896]{1,0:T(8,128)S(1)} %get-tuple-element.17), channel_id=1, source_target_pairs={{0,24},{8,16},{16,8},{24,0},{1,25},{9,17},{17,9},{25,1},{2,26},{10... | collective-permute-start | bytes 172040 | tf_op jit(solution)/shard_map/ppermute | solution.py:24
  27.1 5.3 %collective-permute-start.7 = (f32[16,896]{1,0:T(8,128)S(1)}, f32[16,896]{1,0:T(8,128)S(1)}, u32[]{:S(2)}, u32[]{:S(2)}) collective-permute-start(f32[16,896]{1,0:T(8,128)S(1)} %get-tuple-element.18), channel_id=1, source_target_pairs={{0,16},{8,24},{16,0},{24,8},{1,17},{9,25},{17,1},{25,9},{2,18},{10... | collective-permute-start | bytes 172040 | tf_op jit(solution)/shard_map/ppermute | solution.py:24
  27.1 5.3 %collective-permute-start.6 = (f32[16,896]{1,0:T(8,128)S(1)}, f32[16,896]{1,0:T(8,128)S(1)}, u32[]{:S(2)}, u32[]{:S(2)}) collective-permute-start(f32[16,896]{1,0:T(8,128)S(1)} %get-tuple-element.19), channel_id=1, source_target_pairs={{0,8},{8,0},{16,24},{24,16},{1,9},{9,1},{17,25},{25,17},{2,10},{10... | collective-permute-start | bytes 172040 | tf_op jit(solution)/shard_map/ppermute | solution.py:24

commit v3 on v2

--- a/solution.py
+++ b/solution.py
@@ -12,6 +12,9 @@
 BIN_BP = 2048
 BINS = 128
 LANES = 128
+GATHER_ORDER = (1, 3, 2)
+RETURN_ORDER = (1, 3, 2)
+LAGS = (10, 12, 13)
 
 
 def passed_along(value, axis, steps):
@@ -139,32 +142,41 @@
 
 
 def head_kernel(blocks, blk, width, *refs):
-    packed = refs[:blocks]
-    (table_ref, w_ref, wo_ref) = refs[blocks : blocks + 3]
-    (gh_ref, loss_ref, grad_s, dpre_s) = refs[blocks + 3 : blocks + 7]
-    (source, aux, picks_s, pair_s, act_s, dhid_s, gh_s) = refs[blocks + 7 :]
+    (base_ref, w_ref) = refs[:2]
+    packed = refs[2 : blocks + 1]
+    (gh_ref, loss_ref, grad_s, dpre_s) = refs[blocks + 1 : blocks + 5]
+    (source, aux, picks_s, pair_s, act_s, dhid_s, gh_s) = refs[blocks + 5 :]
     here = lax.axis_index("ctx")
     rep = lax.axis_index("rep")
     cross = lax.div(rep, 2)
     core = lax.rem(rep, 2)
     f32, bf16 = jnp.float32, jnp.bfloat16
-    hidden = w_ref.shape[1]
+    hidden = gh_s.shape[1]
     pairs = blk * blk
     sites = blocks * blk
     tiles = tiles_of(blocks)
-
-    source[:BINS, :] = table_ref[...]
-    for k in range(blocks):
+    parts = hidden // width
+
+    source[:BINS, :] = base_ref[:BINS, :]
+    for i, k in enumerate((0,) + GATHER_ORDER):
         start = pl.multiple_of((here ^ k) * blk, blk)
-        piece = packed[k][...].astype(bf16)
-        source[pl.ds(BINS + start, blk), :] = halved(piece[:, :width])
-        source[pl.ds(BINS + sites + start, blk), :] = halved(piece[:, width : 2 * width])
-        aux[pl.ds(start, blk), :] = piece[:, 2 * width :]
+        if k == 0:
+            donors = base_ref[BINS : BINS + blk, :]
+            acceptors = base_ref[BINS + blk : BINS + 2 * blk, :]
+            codes = base_ref[BINS + 2 * blk : BINS + 3 * blk, :LANES]
+            codes = (codes.astype(f32) * 2.0).astype(bf16)
+        else:
+            donors = halved(packed[i - 1][:, :width])
+            acceptors = halved(packed[i - 1][:, width : 2 * width])
+            codes = packed[i - 1][:, 2 * width :]
+        source[pl.ds(BINS + start, blk), :] = donors
+        source[pl.ds(BINS + sites + start, blk), :] = acceptors
+        aux[pl.ds(start, blk), :] = codes
 
     w_half = w_ref[...]
-    w_out = wo_ref[...]
-    w_rows = jnp.broadcast_to(w_out, (LANES, hidden)).astype(bf16)
-    w_out = w_out * 0.5
+    w_out = base_ref[BINS + 3 * blk : BINS + 4 * blk, :].astype(f32)
+    w_out = jnp.concatenate([w_out[p : p + 1, :] for p in range(parts)], axis=1)
+    w_rows = jnp.broadcast_to(w_out * 2.0, (LANES, hidden)).astype(bf16)
     ones = jnp.ones((LANES, LANES), bf16)
     lane3 = lax.broadcasted_iota(jnp.int32, (blk, blk, LANES), 2)
     row3 = lax.broadcasted_iota(jnp.int32, (blk, blk, LANES), 1)
@@ -182,25 +194,38 @@
     twice_of = [pick | (lane3 == row3 + (sites + a * blk)) for a, pick in enumerate(slot_of)]
     lanes = lax.broadcasted_iota(jnp.int32, (blk, LANES), 1)
     codes = [aux[b * blk : (b + 1) * blk, :].astype(f32) for b in range(blocks)]
-    for tile, (b, a) in enumerate(tiles):
+    spread_out = [jnp.zeros((blk, blk, LANES), f32)] * blocks
+
+    def bins_of(tile):
+        b, a = tiles[tile]
         code = jnp.where(slot_of[a], codes[b][:, None, :], 0.0).astype(bf16)
         code = ones_dot(code.reshape(pairs, LANES), ones)
         picks_s[tile] = jnp.where(code == lane_f, 1.0, 0.0).astype(bf16)
-    for tile, (b, a) in enumerate(tiles):
+
+    def pair_of(tile):
+        b, a = tiles[tile]
         picks = jnp.concatenate([picks_s[tile], from_donor[b] + from_acceptor[a]], axis=1)
         value, slope = silu_parts(ones_dot(picks, source[...]))
         pair_s[tile] = value.astype(bf16)
         dpre_s[tile] = slope
-    for tile in range(len(tiles)):
+
+    def hidden_of(tile):
         value, slope = silu_parts(ones_dot(pair_s[tile], w_half))
         act_s[tile] = value.astype(bf16)
         dhid_s[tile] = slope * w_out
-    spread_out = [jnp.zeros((blk, blk, LANES), f32)] * blocks
-    for tile, (b, a) in enumerate(tiles):
+
+    def logits_of(tile):
+        b, a = tiles[tile]
         logit = lax.dot_general(
             act_s[tile], w_rows, (((1,), (1,)), ((), ())), preferred_element_type=f32
         )
         spread_out[b] = jnp.where(slot_of[a], logit.reshape(blk, blk, LANES), spread_out[b])
+
+    stages = [(bins_of, 0), (pair_of, LAGS[0]), (hidden_of, LAGS[1]), (logits_of, LAGS[2])]
+    for step in range(len(tiles) + stages[-1][1]):
+        for stage, lag in stages:
+            if 0 <= step - lag < len(tiles):
+                stage(step - lag)
     grads = []
     for b in range(blocks):
         logit = jnp.sum(spread_out[b], axis=1)
@@ -216,24 +241,30 @@
         grad = expo / total - jnp.where(chosen, 1.0, 0.0)
         high = grad.astype(bf16).astype(f32)
         grads.append(high + pltpu.roll(grad - high, sites, 1))
+    def gradient_of(start, stop):
+        count = (stop - start) * pairs
+        return lax.dot_general(
+            pair_s[start:stop].reshape(count, width),
+            grad_s[start:stop].reshape(count, hidden),
+            (((0,), (0,)), ((), ())),
+            preferred_element_type=f32,
+        )
+
+    middle = len(tiles) // 2
     for tile, (b, a) in enumerate(tiles):
         rows = jnp.where(twice_of[a], grads[b][:, None, :], 0.0).astype(bf16)
         rows = ones_dot(rows.reshape(pairs, LANES), ones)
         rows = jnp.concatenate([rows] * (hidden // LANES), axis=1)
         grad_s[tile] = (rows * dhid_s[tile]).astype(bf16)
-    count = len(tiles) * pairs
-    gh_s[...] = lax.dot_general(
-        pair_s[...].reshape(count, width),
-        grad_s[...].reshape(count, hidden),
-        (((0,), (0,)), ((), ())),
-        preferred_element_type=f32,
-    )
+        if tile == middle:
+            gh_s[...] = gradient_of(0, middle)
+    total = gh_s[...] + gradient_of(middle, len(tiles))
     chunk = gh_ref.shape[3]
     for c in range(blocks):
         for x in range(2):
             for y in range(2):
                 start = ((c * 2 + x) * 2 + y) * chunk
-                gh_ref[y ^ core, x ^ cross, c ^ here] = gh_s[start : start + chunk, :]
+                gh_ref[y ^ core, x ^ cross, c ^ here] = total[start : start + chunk, :]
 
 
 def finish_kernel(parts, width, hidden, *refs):
@@ -245,38 +276,79 @@
     diagonal = lax.broadcasted_iota(jnp.int32, (blk, LANES), 0) == lax.broadcasted_iota(
         jnp.int32, (blk, LANES), 1
     )
-    for k in range(parts):
+    for piece, k in zip(pieces, (0,) + RETURN_ORDER):
         owner = here ^ k
-        gh_ref[owner] = pieces[k][:, :hidden]
-        acc = pieces[k][:, hidden : hidden + width]
+        gh_ref[owner] = piece[:, :hidden]
+        acc = piece[:, hidden : hidden + width]
         total = acc if total is None else total + acc
         row = jnp.sum(
-            jnp.where(diagonal, pieces[k][:, hidden + width :], 0.0), axis=0, keepdims=True
+            jnp.where(diagonal, piece[:, hidden + width :], 0.0), axis=0, keepdims=True
         )
         loss_ref[0, pl.ds(owner, 1), :] = row[:, :blk]
     acc_ref[0] = total
 
 
 def pack_kernel(
-    blocks, pos_ref, goal_ref, apos_ref, donor_hbm, acceptor_hbm, mask_hbm, out_ref, mask_ref, sems
+    blocks,
+    pos_hbm,
+    goal_hbm,
+    apos_hbm,
+    mask_hbm,
+    donor_hbm,
+    acceptor_hbm,
+    wo_hbm,
+    table_hbm,
+    out_hbm,
+    base_hbm,
+    pos_ref,
+    goal_ref,
+    apos_ref,
+    mask_ref,
+    wo_ref,
+    aux_ref,
+    base_ref,
+    sems,
 ):
     here = lax.axis_index("ctx")
     f32, bf16 = jnp.float32, jnp.bfloat16
     _, blk, width = donor_hbm.shape
+    loads = [
+        (donor_hbm.at[0], base_ref.at[BINS : BINS + blk]),
+        (acceptor_hbm.at[0], base_ref.at[BINS + blk : BINS + 2 * blk]),
+        (mask_hbm, mask_ref),
+        (pos_hbm, pos_ref),
+        (goal_hbm, goal_ref),
+        (apos_hbm, apos_ref),
+        (wo_hbm, wo_ref),
+        (table_hbm, base_ref.at[:BINS]),
+    ]
+    stores = [
+        (base_ref.at[BINS : BINS + blk], out_hbm.at[:, :width]),
+        (base_ref.at[BINS + blk : BINS + 2 * blk], out_hbm.at[:, width : 2 * width]),
+        (aux_ref, out_hbm.at[:, 2 * width :]),
+        (base_ref, base_hbm),
+    ]
     copies = [
-        pltpu.make_async_copy(mask_hbm, mask_ref, sems.at[0]),
-        pltpu.make_async_copy(donor_hbm.at[0], out_ref.at[:, :width], sems.at[1]),
-        pltpu.make_async_copy(acceptor_hbm.at[0], out_ref.at[:, width : 2 * width], sems.at[2]),
+        pltpu.make_async_copy(src, dst, sems.at[i]) for i, (src, dst) in enumerate(loads + stores)
     ]
-    for copy in copies:
+    stores = copies[len(loads) :]
+    loads = copies[: len(loads)]
+    for copy in loads:
         copy.start()
     tissues = goal_ref.shape[1]
     slots = mask_ref.shape[2]
     sites = blocks * blk
     lanes = lax.broadcasted_iota(jnp.int32, (blk, LANES), 1)
     rows = lax.broadcasted_iota(jnp.int32, (blk, LANES), 0)
+    spot = lax.broadcasted_iota(jnp.int32, (LANES, LANES), 0)
+    onto = lax.broadcasted_iota(jnp.int32, (LANES, LANES), 1)
+    shift = jnp.where((onto == spot + here * blk) & (spot < slots), 1.0, 0.0).astype(bf16)
     dpos = jnp.zeros((blk, LANES), jnp.int32)
     goal = jnp.zeros((blk, LANES), jnp.int32)
+    for copy in loads:
+        copy.wait()
+    for copy in stores[:2]:
+        copy.start()
     for i in range(blk):
         dpos = jnp.where(rows == i, pos_ref[0, i], dpos)
         for t in range(tissues):
@@ -287,10 +359,6 @@
         apos = jnp.where(line == j, apos_ref[0, j], apos)
     dist = (lanes // blk - here) * BLOCK_BP + apos - dpos
     goal = jnp.where(goal == slots, -1, goal + here * blk)
-    spot = lax.broadcasted_iota(jnp.int32, (LANES, LANES), 0)
-    onto = lax.broadcasted_iota(jnp.int32, (LANES, LANES), 1)
-    shift = jnp.where((onto == spot + here * blk) & (spot < slots), 1.0, 0.0).astype(bf16)
-    copies[0].wait()
     mask = jnp.concatenate(
         [mask_ref[0], jnp.zeros((blk, LANES - slots), jnp.int32)], axis=1
     )
@@ -298,15 +366,30 @@
     valid = (mask > 0.5) & (dist > 0) & (dist <= SPAN_BLOCKS * BLOCK_BP) & (lanes < sites)
     code = jnp.where(valid, jnp.clip((dist - 1) // BIN_BP, 0, BINS - 1), -1)
     code = jnp.where(lanes < sites, code, goal)
-    out_ref[:, 2 * width :] = code.astype(f32).astype(bf16)
-    copies[1].wait()
-    copies[2].wait()
+    code = code.astype(f32).astype(bf16)
+    aux_ref[...] = code
+    stores[2].start()
+    wo_all = wo_ref[...].astype(f32)
+    pick = lax.broadcasted_iota(jnp.int32, wo_all.shape, 0) == here
+    row = jnp.sum(jnp.where(pick, wo_all, 0.0), axis=0, keepdims=True)
+    start = BINS + 2 * blk
+    base_ref[start : start + blk, :LANES] = code
+    base_ref[start : start + blk, LANES:] = jnp.zeros((blk, width - LANES), bf16)
+    parts = [row[:, i * width : (i + 1) * width] for i in range(row.shape[1] // width)]
+    ids = lax.broadcasted_iota(jnp.int32, (blk, width), 0)
+    rows = jnp.zeros((blk, width), f32)
+    for i, part in enumerate(parts):
+        rows = jnp.where(ids == i, part, rows)
+    base_ref[start + blk : start + 2 * blk, :] = rows.astype(bf16)
+    stores[3].start()
+    for copy in stores:
+        copy.wait()
 
 
 def acceptor_kernel(blocks, blk, grad_ref, w_ref, slope_ref, out_ref):
     here = lax.axis_index("ctx")
-    width = w_ref.shape[0]
     w = w_ref[...]
+    width = w.shape[0]
     total = [None] * blocks
     for tile, (_, a) in enumerate(tiles_of(blocks)):
         grad_pair = lax.dot_general(
@@ -335,15 +418,23 @@
     bf16 = jnp.bfloat16
     f32 = jnp.float32
     anywhere = pl.BlockSpec(memory_space=pl.ANY)
-    smem = pl.BlockSpec(memory_space=pltpu.SMEM)
-    packed = pl.pallas_call(
+    packed, base = pl.pallas_call(
         functools.partial(pack_kernel, blocks),
-        in_specs=[smem] * 3 + [anywhere] * 3,
-        out_specs=pl.BlockSpec(memory_space=pltpu.VMEM),
-        out_shape=jax.ShapeDtypeStruct((blk, 2 * width + LANES), bf16),
+        in_specs=[anywhere] * 8,
+        out_specs=[anywhere] * 2,
+        out_shape=(
+            jax.ShapeDtypeStruct((blk, 2 * width + LANES), bf16),
+            jax.ShapeDtypeStruct((BINS + 4 * blk, width), bf16),
+        ),
         scratch_shapes=[
+            pltpu.SMEM(donor_pos.shape, jnp.int32),
+            pltpu.SMEM((1, tissues, blk), jnp.int32),
+            pltpu.SMEM(acceptor_pos.shape, jnp.int32),
             pltpu.VMEM(pair_mask.shape, jnp.int32),
-            pltpu.SemaphoreType.DMA((3,)),
+            pltpu.VMEM((tissues, hidden), bf16),
+            pltpu.VMEM((blk, LANES), bf16),
+            pltpu.VMEM((BINS + 4 * blk, width), bf16),
+            pltpu.SemaphoreType.DMA((12,)),
         ],
         compiler_params=pltpu.CompilerParams(vmem_limit_bytes=60 * 2**20),
         name="pack",
@@ -351,15 +442,15 @@
         donor_pos,
         jnp.transpose(targets, (0, 2, 1)),
         acceptor_pos,
+        pair_mask,
         donor_feat,
         acceptor_feat,
-        pair_mask,
-    )
-    here = lax.axis_index("ctx")
-    table = halved(dist_table)
-    w_in = halved(lax.dynamic_index_in_dim(hidden_weights, here, 0, False))
-    w_out = lax.dynamic_index_in_dim(output_weights, here, 0, True).astype(f32)
-    pieces = [packed.astype(f32)] + [swapped(packed, "ctx", k) for k in range(1, blocks)]
+        output_weights,
+        dist_table,
+    )
+    base = halved(base)
+    w_in = halved(lax.dynamic_index_in_dim(hidden_weights, lax.axis_index("ctx"), 0, False))
+    pieces = [swapped(packed, "ctx", k) for k in GATHER_ORDER]
     tiles = len(tiles_of(blocks))
     chunk = width // (4 * blocks)
     pairs = blk * blk
@@ -382,7 +473,7 @@
         ],
         compiler_params=pltpu.CompilerParams(vmem_limit_bytes=32 * 2**20),
         name="head",
-    )(*pieces, table, w_in, w_out)
+    )(base, w_in, *pieces)
     kept, sent = partial[0], swapped(partial[1], "rep", 1)
     acc = pl.pallas_call(
         functools.partial(acceptor_kernel, blocks, blk),
@@ -400,7 +491,7 @@
     acc = acc + swapped(acc, "tis", 1)
     partial = partial[0] + sent.astype(jnp.float32)
     send = jnp.concatenate([partial, acc, loss], axis=2)
-    arrived = [send[0]] + [swapped(send[k], "ctx", k) for k in range(1, blocks)]
+    arrived = [send[0]] + [swapped(send[k], "ctx", k) for k in RETURN_ORDER]
     donor_loss, grad_hidden, grad_acceptor = pl.pallas_call(
         functools.partial(finish_kernel, blocks, width, hidden),
         out_shape=(
@@ -426,7 +517,7 @@
         and lax.axis_size("tis") == 2
         and acceptor_feat.shape[1] == blk == 16
         and width == 256
-        and hidden % LANES == 0
+        and hidden % width == 0
         and pair_mask.shape[2] == (SPAN_BLOCKS + 1) * blk
         and BINS == LANES == 2 * blocks * blk
     )

time: 33.4 us -> 31.7 us (0.949)
  other arithmetic: 3.37 us -> 2 us
  waiting for transfers between devices: 7.45 us -> 8.77 us
  starting transfers between devices: 13.4 us -> 12.5 us
  Pallas kernels: 8.02 us -> 7.43 us
    convert_element_type x2 -> x0, other arithmetic: 1.43 us -> none  [the longest x1 0.73 us: shared(): packed.astype(f32)]
    ppermute x9, waiting for transfers between devices: 7.45 us -> 8.77 us  [swapped(): lax.ppermute(value, axis, [(i, i ^ bits) for i in range(lax.axis_size(axi...]
    ppermute x9, starting transfers between devices: 13.4 us -> 12.5 us  [swapped(): lax.ppermute(value, axis, [(i, i ^ bits) for i in range(lax.axis_size(axi...]
    pallas_call x1, Pallas kernels: 2.17 us -> 1.78 us  [shared(): pl.pallas_call(functools.partial(pack_kernel, blocks), in_specs=[anywhere...]
  transfers between devices with their start and end apart: 9 -> 9, of which waited for: 5 -> 5; matrix products, arithmetic and copies ran while one was open for 10% -> 6% of each run, Pallas kernels for 3% -> 3%
where the time goes in v3:
time: 31.7 us; the launch traced here: 31.4 us
  starting transfers between devices  12.5 us (39%)
  waiting for transfers between devices  8.77 us (28%)
  Pallas kernels  7.43 us (23%)
  other arithmetic  2 us (6%)
  between operations  0.73 us (2%)
    ppermute x9, starting transfers between devices, swapped(): lax.ppermute(value, axis, [(i, i ^ bits) for i in range(lax.axis_size(axi...  12.5 us
    ppermute x9, waiting for transfers between devices, swapped(): lax.ppermute(value, axis, [(i, i ^ bits) for i in range(lax.axis_size(axi...  8.77 us
    pallas_call x1, Pallas kernels, shared(): pl.pallas_call(functools.partial(head_kernel, blocks, blk, width), out_sh...  4.04 us
    convert_element_type x2, other arithmetic, halved(): return (value.astype(jnp.float32) * 0.5).astype(value.dtype)  1.91 us
    pallas_call x1, Pallas kernels, shared(): pl.pallas_call(functools.partial(pack_kernel, blocks), in_specs=[anywhere...  1.78 us
    pallas_call x1, Pallas kernels, shared(): pl.pallas_call(functools.partial(acceptor_kernel, blocks, blk), out_shape...  0.92 us
    pallas_call x1, Pallas kernels, shared(): pl.pallas_call(functools.partial(finish_kernel, blocks, width, hidden), o...  0.68 us
  transfers between devices with their start and end apart: 9, of which 5 were waited for; matrix products, arithmetic and copies ran while one was open for 6% of the time, Pallas kernels for 3%

profile of v3, /device:TPU:0, one launch (start us, length us, event | category | flops | bytes accessed | tf_op | source)
XLA Modules:
  0.0 31.4 jit_solution(12264345752504988762)
XLA Ops:
  0.6 1.8 %pack.1 = (bf16[16,640]{1,0:T(8,128)(2,1)}, bf16[192,256]{1,0:T(8,128)(2,1)}) custom-call(s32[1,16]{1,0:T(1,128)} %pos_hbm.1, s32[1,4,16]{2,1,0:T(4,128)} %bitcast.22, s32[1,64]{1,0:T(1,128)} %apos_hbm.1, s32[1,16,80]{2,1,0:T(8,128)} %mask_hbm.1, bf16[1,16,256]{2,1,0:T(8,128)(2,1)} %donor_hbm.1, bf16[1,16,256]{2,1,0:T(8,128)(2,1)} %acceptor_hbm.1, ...), custom_call_target="tpu_custom_call" | custom-call | tf_op jit(solution)/shard_map/pack/pallas_call | solution.py:421
  2.4 4.1 %collective-permute-start.2 = (bf16[16,640]{1,0:T(8,128)(2,1)}, bf16[16,640]{1,0:T(8,128)(2,1)S(1)}, u32[]{:S(2)}, u32[]{:S(2)}) collective-permute-start(bf16[16,640]{1,0:T(8,128)(2,1)} %get-tuple-element.13), channel_id=1, source_target_pairs={{0,16},{8,24},{16,0},{24,8},{1,17},{9,25},{17,1},{25,9},{2,18},{10... | collective-permute-start | bytes 61448 | tf_op jit(solution)/shard_map/ppermute | solution.py:27
  6.5 1.3 %collective-permute-start.1 = (bf16[16,640]{1,0:T(8,128)(2,1)}, bf16[16,640]{1,0:T(8,128)(2,1)S(1)}, u32[]{:S(2)}, u32[]{:S(2)}) collective-permute-start(bf16[16,640]{1,0:T(8,128)(2,1)} %get-tuple-element.13), channel_id=1, source_target_pairs={{0,24},{8,16},{16,8},{24,0},{1,25},{9,17},{17,9},{25,1},{2,26},{10... | collective-permute-start | bytes 61448 | tf_op jit(solution)/shard_map/ppermute | solution.py:27
  7.9 0.2 collective-permute-start
  8.1 0.9 %multiply_convert_fusion.1.refs_0_ = bf16[192,256]{1,0:T(8,128)(2,1)S(1)} fusion(bf16[192,256]{1,0:T(8,128)(2,1)} %get-tuple-element.12), kind=kLoop, calls=%fused_computation.5 | loop fusion | flops 147456 | bytes 196608 | tf_op jit(solution)/shard_map/convert_element_type | solution.py:127
  9.0 1.0 %fusion.refs_1_.w_ref = bf16[256,512]{1,0:T(8,128)(2,1)S(1)} fusion(bf16[4,256,512]{2,1,0:T(8,128)(2,1)} %param.16, s32[]{:T(128)S(6)} %select_n.4), kind=kLoop, calls=%fused_computation.1 | loop fusion | flops 393216 | bytes 524292 | tf_op jit(solution)/shard_map/convert_element_type | solution.py:127
  10.0 0.0 collective-permute-done.2.refs_4_
  10.0 2.3 %collective-permute-done.1.refs_3_ = bf16[16,640]{1,0:T(8,128)(2,1)S(1)} collective-permute-done((bf16[16,640]{1,0:T(8,128)(2,1)}, bf16[16,640]{1,0:T(8,128)(2,1)S(1)}, u32[]{:S(2)}, u32[]{:S(2)}) %collective-permute-start.1) | collective-permute-done | bytes 20512 | tf_op jit(solution)/shard_map/ppermute | solution.py:27
  12.3 0.0 collective-permute-done.refs_2_
  12.3 4.0 %head.1 = (f32[2,2,4,16,512]{4,3,2,1,0:T(8,128)S(1)}, f32[4,16,128]{2,1,0:T(8,128)S(1)}, bf16[10,256,512]{2,1,0:T(8,128)(2,1)S(1)}, f32[10,256,256]{2,1,0:T(8,128)S(1)}) custom-call(bf16[192,256]{1,0:T(8,128)(2,1)S(1)} %multiply_convert_fusion.1.refs_0_, bf16[256,512]{1,0:T(8,128)(2,1)S(1)} %fusion.refs_1_.w_ref, ...), custom_call_target="tpu_custom_call" | custom-call | tf_op jit(solution)/shard_map/head/pallas_call | solution.py:457
  16.4 0.1 collective-permute-start.3
  16.5 0.9 %acceptors.1 = f32[4,16,256]{2,1,0:T(8,128)S(1)} custom-call(bf16[10,256,512]{2,1,0:T(8,128)(2,1)S(1)} %get-tuple-element.15.grad_ref, bf16[256,512]{1,0:T(8,128)(2,1)S(1)} %fusion.refs_1_.w_ref, f32[10,256,256]{2,1,0:T(8,128)S(1)} %get-tuple-element.16.slope_ref), custom_call_target="tpu_custom_call" | custom-call | flops 671088640 | bytes 5242880 | tf_op jit(solution)/shard_map/acceptors/pallas_call | solution.py:478
  17.4 1.6 %collective-permute-start.5 = (f32[4,16,256]{2,1,0:T(8,128)S(1)}, f32[4,16,256]{2,1,0:T(8,128)S(1)}, u32[]{:S(2)}, u32[]{:S(2)}) collective-permute-start(f32[4,16,256]{2,1,0:T(8,128)S(1)} %acceptors.1), channel_id=1, source_target_pairs={{0,4},{4,0},{1,5},{5,1},{2,6},{6,2},{3,7},{7,3},{8,12},{12,8},{9,1... | collective-permute-start | bytes 196616 | tf_op jit(solution)/shard_map/ppermute | solution.py:27
  19.0 0.0 collective-permute-done.3
  19.1 1.6 %collective-permute-start.4 = (bf16[4,16,512]{2,1,0:T(8,128)(2,1)S(1)}, bf16[4,16,512]{2,1,0:T(8,128)(2,1)S(1)}, u32[]{:S(2)}, u32[]{:S(2)}) collective-permute-start(bf16[4,16,512]{2,1,0:T(8,128)(2,1)S(1)} %fusion.2), channel_id=1, source_target_pairs={{0,2},{1,3},{2,0},{3,1},{4,6},{5,7},{6,4},{7,5},{8,10},{9,11},{10,... | collective-permute-start | bytes 196616 | tf_op jit(solution)/shard_map/ppermute | solution.py:27
  20.6 1.3 %collective-permute-done.5 = f32[4,16,256]{2,1,0:T(8,128)S(1)} collective-permute-done((f32[4,16,256]{2,1,0:T(8,128)S(1)}, f32[4,16,256]{2,1,0:T(8,128)S(1)}, u32[]{:S(2)}, u32[]{:S(2)}) %collective-permute-start.5) | collective-permute-done | bytes 65568 | tf_op jit(solution)/shard_map/ppermute | solution.py:27
  22.0 1.4 %collective-permute-done.4 = bf16[4,16,512]{2,1,0:T(8,128)(2,1)S(1)} collective-permute-done((bf16[4,16,512]{2,1,0:T(8,128)(2,1)S(1)}, bf16[4,16,512]{2,1,0:T(8,128)(2,1)S(1)}, u32[]{:S(2)}, u32[]{:S(2)}) %collective-permute-start.4) | collective-permute-done | bytes 65568 | tf_op jit(solution)/shard_map/ppermute | solution.py:27
  23.5 1.3 %collective-permute-start.8 = (f32[16,896]{1,0:T(8,128)S(1)}, f32[16,896]{1,0:T(8,128)S(1)}, u32[]{:S(2)}, u32[]{:S(2)}) collective-permute-start(f32[16,896]{1,0:T(8,128)S(1)} %get-tuple-element.21), channel_id=1, source_target_pairs={{0,16},{8,24},{16,0},{24,8},{1,17},{9,25},{17,1},{25,9},{2,18},{10... | collective-permute-start | bytes 172040 | tf_op jit(solution)/shard_map/ppermute | solution.py:27
  24.8 0.9 %collective-permute-start.7 = (f32[16,896]{1,0:T(8,128)S(1)}, f32[16,896]{1,0:T(8,128)S(1)}, u32[]{:S(2)}, u32[]{:S(2)}) collective-permute-start(f32[16,896]{1,0:T(8,128)S(1)} %get-tuple-element.22), channel_id=1, source_target_pairs={{0,24},{8,16},{16,8},{24,0},{1,25},{9,17},{17,9},{25,1},{2,26},{10... | collective-permute-start | bytes 172040 | tf_op jit(solution)/shard_map/ppermute | solution.py:27
  25.7 1.3 %collective-permute-start.6 = (f32[16,896]{1,0:T(8,128)S(1)}, f32[16,896]{1,0:T(8,128)S(1)}, u32[]{:S(2)}, u32[]{:S(2)}) collective-permute-start(f32[16,896]{1,0:T(8,128)S(1)} %get-tuple-element.23), channel_id=1, source_target_pairs={{0,8},{8,0},{16,24},{24,16},{1,9},{9,1},{17,25},{25,17},{2,10},{10... | collective-permute-start | bytes 172040 | tf_op jit(solution)/shard_map/ppermute | solution.py:27
  27.0 2.4 %collective-permute-done.8.refs_3_ = f32[16,896]{1,0:T(8,128)S(1)} collective-permute-done((f32[16,896]{1,0:T(8,128)S(1)}, f32[16,896]{1,0:T(8,128)S(1)}, u32[]{:S(2)}, u32[]{:S(2)}) %collective-permute-start.8) | collective-permute-done | bytes 57376 | tf_op jit(solution)/shard_map/ppermute | solution.py:27
  29.4 1.3 %collective-permute-done.7.refs_2_ = f32[16,896]{1,0:T(8,128)S(1)} collective-permute-done((f32[16,896]{1,0:T(8,128)S(1)}, f32[16,896]{1,0:T(8,128)S(1)}, u32[]{:S(2)}, u32[]{:S(2)}) %collective-permute-start.7) | collective-permute-done | bytes 57376 | tf_op jit(solution)/shard_map/ppermute | solution.py:27
  30.7 0.0 collective-permute-done.6.refs_1_
  30.7 0.7 %finish.1 = (f32[1,4,16]{2,1,0:T(4,128)}, f32[4,16,512]{2,1,0:T(8,128)}, f32[1,16,256]{2,1,0:T(8,128)}) custom-call(f32[16,896]{1,0:T(8,128)S(1)} %get-tuple-element.24.refs_0_, f32[16,896]{1,0:T(8,128)S(1)} %collective-permute-done.6.refs_1_, f32[16,896]{1,0:T(8,128)S(1)} %collective-permute-done.7.refs_2_, f32[16,896]{1,0:T(8,128)S(1)} %collective-permute-done.8.refs_3_), custom_call_target="tpu_custom_call" | custom-call | tf_op jit(solution)/shard_map/finish/pallas_call | solution.py:495
  (7 shorter events, 0.1 us)
Async XLA Ops:
  2.4 7.6 %collective-permute-start.2 = (bf16[16,640]{1,0:T(8,128)(2,1)}, bf16[16,640]{1,0:T(8,128)(2,1)S(1)}, u32[]{:S(2)}, u32[]{:S(2)}) collective-permute-start(bf16[16,640]{1,0:T(8,128)(2,1)} %get-tuple-element.13), channel_id=1, source_target_pairs={{0,16},{8,24},{16,0},{24,8},{1,17},{9,25},{17,1},{25,9},{2,18},{10... | collective-permute-start | bytes 61448 | tf_op jit(solution)/shard_map/ppermute | solution.py:27
  6.5 5.8 %collective-permute-start.1 = (bf16[16,640]{1,0:T(8,128)(2,1)}, bf16[16,640]{1,0:T(8,128)(2,1)S(1)}, u32[]{:S(2)}, u32[]{:S(2)}) collective-permute-start(bf16[16,640]{1,0:T(8,128)(2,1)} %get-tuple-element.13), channel_id=1, source_target_pairs={{0,24},{8,16},{16,8},{24,0},{1,25},{9,17},{17,9},{25,1},{2,26},{10... | collective-permute-start | bytes 61448 | tf_op jit(solution)/shard_map/ppermute | solution.py:27
  7.9 4.4 %collective-permute-start = (bf16[16,640]{1,0:T(8,128)(2,1)}, bf16[16,640]{1,0:T(8,128)(2,1)S(1)}, u32[]{:S(2)}, u32[]{:S(2)}) collective-permute-start(bf16[16,640]{1,0:T(8,128)(2,1)} %get-tuple-element.13), channel_id=1, source_target_pairs={{0,8},{8,0},{16,24},{24,16},{1,9},{9,1},{17,25},{25,17},{2,10},{10... | collective-permute-start | bytes 61448 | tf_op jit(solution)/shard_map/ppermute | solution.py:27
  16.4 2.6 %collective-permute-start.3 = (f32[2,4,16,512]{3,2,1,0:T(8,128)S(1)}, f32[2,4,16,512]{3,2,1,0:T(8,128)S(1)}, u32[]{:S(2)}, u32[]{:S(2)}) collective-permute-start(f32[2,4,16,512]{3,2,1,0:T(8,128)S(1)} %slice_bitcast_fusion), channel_id=1, source_target_pairs={{0,1},{1,0},{2,3},{3,2},{4,5},{5,4},{6,7},{7,6},{8,9},{9,8},{10,11... | collective-permute-start | bytes 786440 | tf_op jit(solution)/shard_map/ppermute | solution.py:27
  17.4 4.6 %collective-permute-start.5 = (f32[4,16,256]{2,1,0:T(8,128)S(1)}, f32[4,16,256]{2,1,0:T(8,128)S(1)}, u32[]{:S(2)}, u32[]{:S(2)}) collective-permute-start(f32[4,16,256]{2,1,0:T(8,128)S(1)} %acceptors.1), channel_id=1, source_target_pairs={{0,4},{4,0},{1,5},{5,1},{2,6},{6,2},{3,7},{7,3},{8,12},{12,8},{9,1... | collective-permute-start | bytes 196616 | tf_op jit(solution)/shard_map/ppermute | solution.py:27
  19.1 4.3 %collective-permute-start.4 = (bf16[4,16,512]{2,1,0:T(8,128)(2,1)S(1)}, bf16[4,16,512]{2,1,0:T(8,128)(2,1)S(1)}, u32[]{:S(2)}, u32[]{:S(2)}) collective-permute-start(bf16[4,16,512]{2,1,0:T(8,128)(2,1)S(1)} %fusion.2), channel_id=1, source_target_pairs={{0,2},{1,3},{2,0},{3,1},{4,6},{5,7},{6,4},{7,5},{8,10},{9,11},{10,... | collective-permute-start | bytes 196616 | tf_op jit(solution)/shard_map/ppermute | solution.py:27
  23.5 6.0 %collective-permute-start.8 = (f32[16,896]{1,0:T(8,128)S(1)}, f32[16,896]{1,0:T(8,128)S(1)}, u32[]{:S(2)}, u32[]{:S(2)}) collective-permute-start(f32[16,896]{1,0:T(8,128)S(1)} %get-tuple-element.21), channel_id=1, source_target_pairs={{0,16},{8,24},{16,0},{24,8},{1,17},{9,25},{17,1},{25,9},{2,18},{10... | collective-permute-start | bytes 172040 | tf_op jit(solution)/shard_map/ppermute | solution.py:27
  24.8 6.0 %collective-permute-start.7 = (f32[16,896]{1,0:T(8,128)S(1)}, f32[16,896]{1,0:T(8,128)S(1)}, u32[]{:S(2)}, u32[]{:S(2)}) collective-permute-start(f32[16,896]{1,0:T(8,128)S(1)} %get-tuple-element.22), channel_id=1, source_target_pairs={{0,24},{8,16},{16,8},{24,0},{1,25},{9,17},{17,9},{25,1},{2,26},{10... | collective-permute-start | bytes 172040 | tf_op jit(solution)/shard_map/ppermute | solution.py:27
  25.7 5.1 %collective-permute-start.6 = (f32[16,896]{1,0:T(8,128)S(1)}, f32[16,896]{1,0:T(8,128)S(1)}, u32[]{:S(2)}, u32[]{:S(2)}) collective-permute-start(f32[16,896]{1,0:T(8,128)S(1)} %get-tuple-element.23), channel_id=1, source_target_pairs={{0,8},{8,0},{16,24},{24,16},{1,9},{9,1},{17,25},{25,17},{2,10},{10... | collective-permute-start | bytes 172040 | tf_op jit(solution)/shard_map/ppermute | solution.py:27

commit v4 on v2

--- a/solution.py
+++ b/solution.py
@@ -12,6 +12,9 @@
 BIN_BP = 2048
 BINS = 128
 LANES = 128
+GATHER_ORDER = (1, 3, 2)
+RETURN_ORDER = (1, 3, 2)
+LAGS = (10, 12, 13)
 
 
 def passed_along(value, axis, steps):
@@ -139,32 +142,63 @@
 
 
 def head_kernel(blocks, blk, width, *refs):
-    packed = refs[:blocks]
-    (table_ref, w_ref, wo_ref) = refs[blocks : blocks + 3]
-    (gh_ref, loss_ref, grad_s, dpre_s) = refs[blocks + 3 : blocks + 7]
-    (source, aux, picks_s, pair_s, act_s, dhid_s, gh_s) = refs[blocks + 7 :]
+    (base_ref, w_ref) = refs[:2]
+    packed = refs[2 : blocks + 2]
+    (gh_ref, loss_ref, grad_s, dpre_s) = refs[blocks + 2 : blocks + 6]
+    (source, aux, picks_s, pair_s, act_s, dhid_s, gh_s) = refs[blocks + 6 :]
     here = lax.axis_index("ctx")
     rep = lax.axis_index("rep")
     cross = lax.div(rep, 2)
     core = lax.rem(rep, 2)
     f32, bf16 = jnp.float32, jnp.bfloat16
-    hidden = w_ref.shape[1]
+    hidden = gh_s.shape[1]
     pairs = blk * blk
     sites = blocks * blk
+    slots = (SPAN_BLOCKS + 1) * blk
     tiles = tiles_of(blocks)
 
-    source[:BINS, :] = table_ref[...]
-    for k in range(blocks):
+    source[:BINS, :] = base_ref[:BINS, :]
+    for piece, k in zip(packed, (0,) + GATHER_ORDER):
         start = pl.multiple_of((here ^ k) * blk, blk)
-        piece = packed[k][...].astype(bf16)
-        source[pl.ds(BINS + start, blk), :] = halved(piece[:, :width])
-        source[pl.ds(BINS + sites + start, blk), :] = halved(piece[:, width : 2 * width])
-        aux[pl.ds(start, blk), :] = piece[:, 2 * width :]
+        source[pl.ds(BINS + start, blk), :] = halved(piece[:blk, :])
+        source[pl.ds(BINS + sites + start, blk), :] = halved(piece[blk : 2 * blk, :])
+        aux[pl.ds(start, blk), :] = piece[2 * blk :, :]
+
+    lanes = lax.broadcasted_iota(jnp.int32, (blk, LANES), 1)
+    ids = lax.broadcasted_iota(jnp.int32, (blk, LANES), 0)
+    codes = []
+    aims = []
+    for b in range(blocks):
+        extra = aux[b * blk : (b + 1) * blk, :].astype(f32)
+        rows = extra[:, LANES:]
+
+        def column(row):
+            return jnp.sum(jnp.where(lanes == ids, row, 0.0), axis=1, keepdims=True)
+
+        dpos = column(rows[:1, :] * 256.0 + rows[1:2, :])
+        apos = rows[2:3, :] * 256.0 + rows[3:4, :]
+        aim = column(
+            jnp.sum(jnp.where(ids == here + 4, rows, 0.0), axis=0, keepdims=True)
+        ).astype(jnp.int32)
+        mask = pltpu.roll(extra[:, :LANES], b * blk, 1) if b else extra[:, :LANES]
+        dist = (lanes // blk - b) * BLOCK_BP + (apos - dpos).astype(jnp.int32)
+        valid = (mask > 0.5) & (dist > 0) & (dist <= SPAN_BLOCKS * BLOCK_BP) & (lanes < sites)
+        code = jnp.where(valid, jnp.clip((dist - 1) // BIN_BP, 0, BINS - 1), -1)
+        codes.append(code.astype(f32))
+        aims.append(jnp.where(aim == slots, -1, aim + b * blk))
 
     w_half = w_ref[...]
-    w_out = wo_ref[...]
-    w_rows = jnp.broadcast_to(w_out, (LANES, hidden)).astype(bf16)
-    w_out = w_out * 0.5
+    w_out = base_ref[BINS:, :].astype(f32)
+    tissues = blocks
+    ids = lax.broadcasted_iota(jnp.int32, w_out.shape, 0)
+    w_out = jnp.concatenate(
+        [
+            jnp.sum(jnp.where(ids == here + part * tissues, w_out, 0.0), axis=0, keepdims=True)
+            for part in range(hidden // width)
+        ],
+        axis=1,
+    )
+    w_rows = jnp.broadcast_to(w_out * 2.0, (LANES, hidden)).astype(bf16)
     ones = jnp.ones((LANES, LANES), bf16)
     lane3 = lax.broadcasted_iota(jnp.int32, (blk, blk, LANES), 2)
     row3 = lax.broadcasted_iota(jnp.int32, (blk, blk, LANES), 1)
@@ -180,34 +214,43 @@
     ]
     slot_of = [lane3 == row3 + a * blk for a in range(blocks)]
     twice_of = [pick | (lane3 == row3 + (sites + a * blk)) for a, pick in enumerate(slot_of)]
-    lanes = lax.broadcasted_iota(jnp.int32, (blk, LANES), 1)
-    codes = [aux[b * blk : (b + 1) * blk, :].astype(f32) for b in range(blocks)]
-    for tile, (b, a) in enumerate(tiles):
+    spread_out = [jnp.zeros((blk, blk, LANES), f32)] * blocks
+
+    def bins_of(tile):
+        b, a = tiles[tile]
         code = jnp.where(slot_of[a], codes[b][:, None, :], 0.0).astype(bf16)
         code = ones_dot(code.reshape(pairs, LANES), ones)
         picks_s[tile] = jnp.where(code == lane_f, 1.0, 0.0).astype(bf16)
-    for tile, (b, a) in enumerate(tiles):
+
+    def pair_of(tile):
+        b, a = tiles[tile]
         picks = jnp.concatenate([picks_s[tile], from_donor[b] + from_acceptor[a]], axis=1)
         value, slope = silu_parts(ones_dot(picks, source[...]))
         pair_s[tile] = value.astype(bf16)
         dpre_s[tile] = slope
-    for tile in range(len(tiles)):
+
+    def hidden_of(tile):
         value, slope = silu_parts(ones_dot(pair_s[tile], w_half))
         act_s[tile] = value.astype(bf16)
         dhid_s[tile] = slope * w_out
-    spread_out = [jnp.zeros((blk, blk, LANES), f32)] * blocks
-    for tile, (b, a) in enumerate(tiles):
+
+    def logits_of(tile):
+        b, a = tiles[tile]
         logit = lax.dot_general(
             act_s[tile], w_rows, (((1,), (1,)), ((), ())), preferred_element_type=f32
         )
         spread_out[b] = jnp.where(slot_of[a], logit.reshape(blk, blk, LANES), spread_out[b])
+
+    stages = [(bins_of, 0), (pair_of, LAGS[0]), (hidden_of, LAGS[1]), (logits_of, LAGS[2])]
+    for step in range(len(tiles) + stages[-1][1]):
+        for stage, lag in stages:
+            if 0 <= step - lag < len(tiles):
+                stage(step - lag)
     grads = []
     for b in range(blocks):
         logit = jnp.sum(spread_out[b], axis=1)
-        valid = (codes[b] >= 0.0) & (lanes < sites)
-        goal = jnp.sum(jnp.where(lanes == sites + here, codes[b], 0.0), axis=1, keepdims=True)
-        chosen = lanes == goal.astype(jnp.int32)
-        masked = jnp.where(valid, logit, -jnp.inf)
+        chosen = lanes == aims[b]
+        masked = jnp.where(codes[b] >= 0.0, logit, -jnp.inf)
         top = jnp.maximum(jnp.max(masked, axis=1, keepdims=True), 0.0)
         expo = jnp.exp(masked - top)
         total = jnp.sum(expo, axis=1, keepdims=True) + jnp.exp(-top)
@@ -216,24 +259,30 @@
         grad = expo / total - jnp.where(chosen, 1.0, 0.0)
         high = grad.astype(bf16).astype(f32)
         grads.append(high + pltpu.roll(grad - high, sites, 1))
+    def gradient_of(start, stop):
+        count = (stop - start) * pairs
+        return lax.dot_general(
+            pair_s[start:stop].reshape(count, width),
+            grad_s[start:stop].reshape(count, hidden),
+            (((0,), (0,)), ((), ())),
+            preferred_element_type=f32,
+        )
+
+    middle = len(tiles) // 2
     for tile, (b, a) in enumerate(tiles):
         rows = jnp.where(twice_of[a], grads[b][:, None, :], 0.0).astype(bf16)
         rows = ones_dot(rows.reshape(pairs, LANES), ones)
         rows = jnp.concatenate([rows] * (hidden // LANES), axis=1)
         grad_s[tile] = (rows * dhid_s[tile]).astype(bf16)
-    count = len(tiles) * pairs
-    gh_s[...] = lax.dot_general(
-        pair_s[...].reshape(count, width),
-        grad_s[...].reshape(count, hidden),
-        (((0,), (0,)), ((), ())),
-        preferred_element_type=f32,
-    )
+        if tile == middle:
+            gh_s[...] = gradient_of(0, middle)
+    total = gh_s[...] + gradient_of(middle, len(tiles))
     chunk = gh_ref.shape[3]
     for c in range(blocks):
         for x in range(2):
             for y in range(2):
                 start = ((c * 2 + x) * 2 + y) * chunk
-                gh_ref[y ^ core, x ^ cross, c ^ here] = gh_s[start : start + chunk, :]
+                gh_ref[y ^ core, x ^ cross, c ^ here] = total[start : start + chunk, :]
 
 
 def finish_kernel(parts, width, hidden, *refs):
@@ -245,68 +294,22 @@
     diagonal = lax.broadcasted_iota(jnp.int32, (blk, LANES), 0) == lax.broadcasted_iota(
         jnp.int32, (blk, LANES), 1
     )
-    for k in range(parts):
+    for piece, k in zip(pieces, (0,) + RETURN_ORDER):
         owner = here ^ k
-        gh_ref[owner] = pieces[k][:, :hidden]
-        acc = pieces[k][:, hidden : hidden + width]
+        gh_ref[owner] = piece[:, :hidden]
+        acc = piece[:, hidden : hidden + width]
         total = acc if total is None else total + acc
         row = jnp.sum(
-            jnp.where(diagonal, pieces[k][:, hidden + width :], 0.0), axis=0, keepdims=True
+            jnp.where(diagonal, piece[:, hidden + width :], 0.0), axis=0, keepdims=True
         )
         loss_ref[0, pl.ds(owner, 1), :] = row[:, :blk]
     acc_ref[0] = total
 
 
-def pack_kernel(
-    blocks, pos_ref, goal_ref, apos_ref, donor_hbm, acceptor_hbm, mask_hbm, out_ref, mask_ref, sems
-):
-    here = lax.axis_index("ctx")
-    f32, bf16 = jnp.float32, jnp.bfloat16
-    _, blk, width = donor_hbm.shape
-    copies = [
-        pltpu.make_async_copy(mask_hbm, mask_ref, sems.at[0]),
-        pltpu.make_async_copy(donor_hbm.at[0], out_ref.at[:, :width], sems.at[1]),
-        pltpu.make_async_copy(acceptor_hbm.at[0], out_ref.at[:, width : 2 * width], sems.at[2]),
-    ]
-    for copy in copies:
-        copy.start()
-    tissues = goal_ref.shape[1]
-    slots = mask_ref.shape[2]
-    sites = blocks * blk
-    lanes = lax.broadcasted_iota(jnp.int32, (blk, LANES), 1)
-    rows = lax.broadcasted_iota(jnp.int32, (blk, LANES), 0)
-    dpos = jnp.zeros((blk, LANES), jnp.int32)
-    goal = jnp.zeros((blk, LANES), jnp.int32)
-    for i in range(blk):
-        dpos = jnp.where(rows == i, pos_ref[0, i], dpos)
-        for t in range(tissues):
-            goal = jnp.where((rows == i) & (lanes == sites + t), goal_ref[0, t, i], goal)
-    apos = jnp.zeros((1, LANES), jnp.int32)
-    line = lax.broadcasted_iota(jnp.int32, (1, LANES), 1)
-    for j in range(sites):
-        apos = jnp.where(line == j, apos_ref[0, j], apos)
-    dist = (lanes // blk - here) * BLOCK_BP + apos - dpos
-    goal = jnp.where(goal == slots, -1, goal + here * blk)
-    spot = lax.broadcasted_iota(jnp.int32, (LANES, LANES), 0)
-    onto = lax.broadcasted_iota(jnp.int32, (LANES, LANES), 1)
-    shift = jnp.where((onto == spot + here * blk) & (spot < slots), 1.0, 0.0).astype(bf16)
-    copies[0].wait()
-    mask = jnp.concatenate(
-        [mask_ref[0], jnp.zeros((blk, LANES - slots), jnp.int32)], axis=1
-    )
-    mask = ones_dot(mask.astype(f32).astype(bf16), shift)
-    valid = (mask > 0.5) & (dist > 0) & (dist <= SPAN_BLOCKS * BLOCK_BP) & (lanes < sites)
-    code = jnp.where(valid, jnp.clip((dist - 1) // BIN_BP, 0, BINS - 1), -1)
-    code = jnp.where(lanes < sites, code, goal)
-    out_ref[:, 2 * width :] = code.astype(f32).astype(bf16)
-    copies[1].wait()
-    copies[2].wait()
-
-
 def acceptor_kernel(blocks, blk, grad_ref, w_ref, slope_ref, out_ref):
     here = lax.axis_index("ctx")
-    width = w_ref.shape[0]
     w = w_ref[...]
+    width = w.shape[0]
     total = [None] * blocks
     for tile, (_, a) in enumerate(tiles_of(blocks)):
         grad_pair = lax.dot_general(
@@ -334,32 +337,40 @@
     tissues, _, hidden = hidden_weights.shape
     bf16 = jnp.bfloat16
     f32 = jnp.float32
-    anywhere = pl.BlockSpec(memory_space=pl.ANY)
-    smem = pl.BlockSpec(memory_space=pltpu.SMEM)
-    packed = pl.pallas_call(
-        functools.partial(pack_kernel, blocks),
-        in_specs=[smem] * 3 + [anywhere] * 3,
-        out_specs=pl.BlockSpec(memory_space=pltpu.VMEM),
-        out_shape=jax.ShapeDtypeStruct((blk, 2 * width + LANES), bf16),
-        scratch_shapes=[
-            pltpu.VMEM(pair_mask.shape, jnp.int32),
-            pltpu.SemaphoreType.DMA((3,)),
-        ],
-        compiler_params=pltpu.CompilerParams(vmem_limit_bytes=60 * 2**20),
-        name="pack",
-    )(
-        donor_pos,
-        jnp.transpose(targets, (0, 2, 1)),
-        acceptor_pos,
-        donor_feat,
-        acceptor_feat,
-        pair_mask,
-    )
-    here = lax.axis_index("ctx")
-    table = halved(dist_table)
-    w_in = halved(lax.dynamic_index_in_dim(hidden_weights, here, 0, False))
-    w_out = lax.dynamic_index_in_dim(output_weights, here, 0, True).astype(f32)
-    pieces = [packed.astype(f32)] + [swapped(packed, "ctx", k) for k in range(1, blocks)]
+    def placed(value, rows, row, lane=0):
+        height, extent = value.shape
+        room = ((row, rows - row - height, 0), (lane, width - lane - extent, 0))
+        return lax.pad(value, jnp.zeros((), value.dtype), room)
+
+    rows = 3 * blk
+    last = 2 * blk
+    whole = sum(
+        placed(value, rows, row, lane)
+        for value, row, lane in (
+            (pair_mask[0], last, 0),
+            (donor_pos, last, LANES),
+            (donor_pos, last + 1, LANES),
+            (acceptor_pos, last + 2, LANES),
+            (acceptor_pos, last + 3, LANES),
+            (jnp.transpose(targets, (0, 2, 1))[0], last + 4, LANES),
+        )
+    )
+    row = lax.broadcasted_iota(jnp.int32, whole.shape, 0)
+    lane = lax.broadcasted_iota(jnp.int32, whole.shape, 1)
+    high = (lane >= LANES) & ((row == last) | (row == last + 2))
+    whole = jnp.where(high, whole >> 8, whole & 255).astype(f32)
+    sites = placed(donor_feat[0], rows, 0) + placed(acceptor_feat[0], rows, blk)
+    packed = (sites.astype(f32) + whole).astype(bf16)
+    base = 0.5 * sum(
+        placed(value, BINS + blk, row, lane)
+        for value, row, lane in (
+            (dist_table, 0, 0),
+            (output_weights, BINS, 0),
+            (output_weights, BINS + tissues, -width),
+        )
+    )
+    w_in = halved(lax.dynamic_index_in_dim(hidden_weights, lax.axis_index("ctx"), 0, False))
+    pieces = [swapped(packed, "ctx", k) for k in GATHER_ORDER]
     tiles = len(tiles_of(blocks))
     chunk = width // (4 * blocks)
     pairs = blk * blk
@@ -373,7 +384,7 @@
         ),
         scratch_shapes=[
             pltpu.VMEM((BINS + 2 * blocks * blk, width), bf16),
-            pltpu.VMEM((blocks * blk, LANES), bf16),
+            pltpu.VMEM((blocks * blk, width), bf16),
             pltpu.VMEM((tiles, pairs, BINS), bf16),
             pltpu.VMEM((tiles, pairs, width), bf16),
             pltpu.VMEM((tiles, pairs, hidden), bf16),
@@ -382,7 +393,7 @@
         ],
         compiler_params=pltpu.CompilerParams(vmem_limit_bytes=32 * 2**20),
         name="head",
-    )(*pieces, table, w_in, w_out)
+    )(base, w_in, packed, *pieces)
     kept, sent = partial[0], swapped(partial[1], "rep", 1)
     acc = pl.pallas_call(
         functools.partial(acceptor_kernel, blocks, blk),
@@ -400,7 +411,7 @@
     acc = acc + swapped(acc, "tis", 1)
     partial = partial[0] + sent.astype(jnp.float32)
     send = jnp.concatenate([partial, acc, loss], axis=2)
-    arrived = [send[0]] + [swapped(send[k], "ctx", k) for k in range(1, blocks)]
+    arrived = [send[0]] + [swapped(send[k], "ctx", k) for k in RETURN_ORDER]
     donor_loss, grad_hidden, grad_acceptor = pl.pallas_call(
         functools.partial(finish_kernel, blocks, width, hidden),
         out_shape=(
@@ -426,7 +437,7 @@
         and lax.axis_size("tis") == 2
         and acceptor_feat.shape[1] == blk == 16
         and width == 256
-        and hidden % LANES == 0
+        and hidden == 2 * width
         and pair_mask.shape[2] == (SPAN_BLOCKS + 1) * blk
         and BINS == LANES == 2 * blocks * blk
     )

time: 33.4 us -> 30.6 us (0.916)
  Pallas kernels: 8.02 us -> 5.6 us
  waiting for transfers between devices: 7.45 us -> 8.63 us
  starting transfers between devices: 13.4 us -> 12.4 us
  other arithmetic: 3.37 us -> 2.88 us
    pallas_call x1 -> x0, Pallas kernels: 2.17 us -> none  [shared(): pl.pallas_call(functools.partial(pack_kernel, blocks), in_specs=[smem] *...]
    ppermute x9, waiting for transfers between devices: 7.45 us -> 8.63 us  [swapped(): lax.ppermute(value, axis, [(i, i ^ bits) for i in range(lax.axis_size(axi...]
    ppermute x9, starting transfers between devices: 13.4 us -> 12.4 us  [swapped(): lax.ppermute(value, axis, [(i, i ^ bits) for i in range(lax.axis_size(axi...]
    mul x0 -> x1, other arithmetic: none -> 0.9 us  [shared(): 0.5 * sum((placed(value, BINS + blk, row, lane) for value, row, lane in (...]
    convert_element_type x2 -> x1, other arithmetic: 1.85 us -> 0.99 us  [halved(): return (value.astype(jnp.float32) * 0.5).astype(value.dtype)]
    convert_element_type x2 -> x1, other arithmetic: 1.43 us -> 0.89 us  [shared(): packed = (sites.astype(f32) + whole).astype(bf16)]
  transfers between devices with their start and end apart: 9 -> 9, of which waited for: 5 -> 5; matrix products, arithmetic and copies ran while one was open for 10% -> 6% of each run, Pallas kernels for 3% -> 3%
where the time goes in v4:
time: 30.6 us; the launch traced here: 30.3 us
  starting transfers between devices  12.4 us (41%)
  waiting for transfers between devices  8.63 us (28%)
  Pallas kernels  5.6 us (18%)
  other arithmetic  2.88 us (9%)
  between operations  0.73 us (2%)
    ppermute x9, starting transfers between devices, swapped(): lax.ppermute(value, axis, [(i, i ^ bits) for i in range(lax.axis_size(axi...  12.4 us
    ppermute x9, waiting for transfers between devices, swapped(): lax.ppermute(value, axis, [(i, i ^ bits) for i in range(lax.axis_size(axi...  8.63 us
    pallas_call x1, Pallas kernels, shared(): pl.pallas_call(functools.partial(head_kernel, blocks, blk, width), out_sh...  4.04 us
    convert_element_type x1, other arithmetic, halved(): return (value.astype(jnp.float32) * 0.5).astype(value.dtype)  0.99 us
    mul x1, other arithmetic, shared(): 0.5 * sum((placed(value, BINS + blk, row, lane) for value, row, lane in (...  0.9 us
    convert_element_type x1, other arithmetic, shared(): packed = (sites.astype(f32) + whole).astype(bf16)  0.89 us
    pallas_call x1, Pallas kernels, shared(): pl.pallas_call(functools.partial(acceptor_kernel, blocks, blk), out_shape...  0.88 us
    pallas_call x1, Pallas kernels, shared(): pl.pallas_call(functools.partial(finish_kernel, blocks, width, hidden), o...  0.68 us
  transfers between devices with their start and end apart: 9, of which 5 were waited for; matrix products, arithmetic and copies ran while one was open for 6% of the time, Pallas kernels for 3%

profile of v4, /device:TPU:0, one launch (start us, length us, event | category | flops | bytes accessed | tf_op | source)
XLA Modules:
  0.0 30.3 jit_solution(11527734204553162463)
XLA Ops:
  0.7 0.9 %add_convert_fusion.refs_2_ = bf16[48,256]{1,0:T(8,128)(2,1)S(1)} fusion(s32[4,16]{1,0:T(4,128)} %bitcast.30, s32[1,64]{1,0:T(1,128)} %param.12, s32[1,16]{1,0:T(1,128)} %param.11, s32[16,80]{1,0:T(8,128)} %bitcast.27, bf16[16,256]{1,0:T(8,128)(2,1)} %bitcast.28, bf16[16,256]{1,0:T(8,128)(2,1)} %bitcast.29, pred[256]{0:T(512)(128)(4,1)S(1)} %iota_compare_fusion, ...), kind=kLoop, calls=%fused_computation.18 | loop fusion | flops 196608 | bytes 46960 | tf_op jit(solution)/shard_map/convert_element_type | solution.py:363
  1.5 4.1 %collective-permute-start.2 = (bf16[48,256]{1,0:T(8,128)(2,1)S(1)}, bf16[48,256]{1,0:T(8,128)(2,1)S(1)}, u32[]{:S(2)}, u32[]{:S(2)}) collective-permute-start(bf16[48,256]{1,0:T(8,128)(2,1)S(1)} %add_convert_fusion.refs_2_), channel_id=1, source_target_pairs={{0,16},{8,24},{16,0},{24,8},{1,17},{9,25},{17,1},{25,9},{2,18},{10... | collective-permute-start | bytes 73736 | tf_op jit(solution)/shard_map/ppermute | solution.py:27
  5.6 1.3 %collective-permute-start.1 = (bf16[48,256]{1,0:T(8,128)(2,1)S(1)}, bf16[48,256]{1,0:T(8,128)(2,1)S(1)}, u32[]{:S(2)}, u32[]{:S(2)}) collective-permute-start(bf16[48,256]{1,0:T(8,128)(2,1)S(1)} %add_convert_fusion.refs_2_), channel_id=1, source_target_pairs={{0,24},{8,16},{16,8},{24,0},{1,25},{9,17},{17,9},{25,1},{2,26},{10... | collective-permute-start | bytes 73736 | tf_op jit(solution)/shard_map/ppermute | solution.py:27
  7.0 0.2 collective-permute-start
  7.2 1.0 %fusion.refs_1_.w_ref = bf16[256,512]{1,0:T(8,128)(2,1)S(1)} fusion(bf16[4,256,512]{2,1,0:T(8,128)(2,1)} %param.16, s32[]{:T(128)S(6)} %select_n.8), kind=kLoop, calls=%fused_computation.1 | loop fusion | flops 393216 | bytes 524292 | tf_op jit(solution)/shard_map/convert_element_type | solution.py:127
  8.2 0.9 %fusion.4.refs_0_ = bf16[144,256]{1,0:T(8,128)(2,1)S(1)} fusion(bf16[4,512]{1,0:T(4,128)(2,1)} %param.17, bf16[128,256]{1,0:T(8,128)(2,1)} %param.15), kind=kLoop, calls=%fused_computation.12 | loop fusion | flops 294912 | bytes 143360 | tf_op jit(solution)/shard_map/mul | solution.py:364
  9.1 0.0 collective-permute-done.2.refs_5_
  9.1 2.1 %collective-permute-done.1.refs_4_ = bf16[48,256]{1,0:T(8,128)(2,1)S(1)} collective-permute-done((bf16[48,256]{1,0:T(8,128)(2,1)S(1)}, bf16[48,256]{1,0:T(8,128)(2,1)S(1)}, u32[]{:S(2)}, u32[]{:S(2)}) %collective-permute-start.1) | collective-permute-done | bytes 24608 | tf_op jit(solution)/shard_map/ppermute | solution.py:27
  11.2 0.0 collective-permute-done.refs_3_
  11.2 4.0 %head.1 = (f32[2,2,4,16,512]{4,3,2,1,0:T(8,128)S(1)}, f32[4,16,128]{2,1,0:T(8,128)S(1)}, bf16[10,256,512]{2,1,0:T(8,128)(2,1)S(1)}, f32[10,256,256]{2,1,0:T(8,128)S(1)}) custom-call(bf16[144,256]{1,0:T(8,128)(2,1)S(1)} %fusion.4.refs_0_, bf16[256,512]{1,0:T(8,128)(2,1)S(1)} %fusion.refs_1_.w_ref, bf16[48,256]{1,0:T(8,128)(2,1)S(1)} %add_convert_fusion.refs_2_, ...), custom_call_target="tpu_custom_call" | custom-call | tf_op jit(solution)/shard_map/head/pallas_call | solution.py:377
  15.3 0.1 collective-permute-start.3
  15.4 0.9 %acceptors.1 = f32[4,16,256]{2,1,0:T(8,128)S(1)} custom-call(bf16[10,256,512]{2,1,0:T(8,128)(2,1)S(1)} %get-tuple-element.11.grad_ref, bf16[256,512]{1,0:T(8,128)(2,1)S(1)} %fusion.refs_1_.w_ref, f32[10,256,256]{2,1,0:T(8,128)S(1)} %get-tuple-element.12.slope_ref), custom_call_target="tpu_custom_call" | custom-call | flops 671088640 | bytes 5242880 | tf_op jit(solution)/shard_map/acceptors/pallas_call | solution.py:398
  16.3 1.6 %collective-permute-start.5 = (f32[4,16,256]{2,1,0:T(8,128)S(1)}, f32[4,16,256]{2,1,0:T(8,128)S(1)}, u32[]{:S(2)}, u32[]{:S(2)}) collective-permute-start(f32[4,16,256]{2,1,0:T(8,128)S(1)} %acceptors.1), channel_id=1, source_target_pairs={{0,4},{4,0},{1,5},{5,1},{2,6},{6,2},{3,7},{7,3},{8,12},{12,8},{9,1... | collective-permute-start | bytes 196616 | tf_op jit(solution)/shard_map/ppermute | solution.py:27
  17.9 0.0 collective-permute-done.3
  17.9 1.6 %collective-permute-start.4 = (bf16[4,16,512]{2,1,0:T(8,128)(2,1)S(1)}, bf16[4,16,512]{2,1,0:T(8,128)(2,1)S(1)}, u32[]{:S(2)}, u32[]{:S(2)}) collective-permute-start(bf16[4,16,512]{2,1,0:T(8,128)(2,1)S(1)} %fusion.5), channel_id=1, source_target_pairs={{0,2},{1,3},{2,0},{3,1},{4,6},{5,7},{6,4},{7,5},{8,10},{9,11},{10,... | collective-permute-start | bytes 196616 | tf_op jit(solution)/shard_map/ppermute | solution.py:27
  19.5 1.3 %collective-permute-done.5 = f32[4,16,256]{2,1,0:T(8,128)S(1)} collective-permute-done((f32[4,16,256]{2,1,0:T(8,128)S(1)}, f32[4,16,256]{2,1,0:T(8,128)S(1)}, u32[]{:S(2)}, u32[]{:S(2)}) %collective-permute-start.5) | collective-permute-done | bytes 65568 | tf_op jit(solution)/shard_map/ppermute | solution.py:27
  20.9 1.4 %collective-permute-done.4 = bf16[4,16,512]{2,1,0:T(8,128)(2,1)S(1)} collective-permute-done((bf16[4,16,512]{2,1,0:T(8,128)(2,1)S(1)}, bf16[4,16,512]{2,1,0:T(8,128)(2,1)S(1)}, u32[]{:S(2)}, u32[]{:S(2)}) %collective-permute-start.4) | collective-permute-done | bytes 65568 | tf_op jit(solution)/shard_map/ppermute | solution.py:27
  22.3 1.3 %collective-permute-start.8 = (f32[16,896]{1,0:T(8,128)S(1)}, f32[16,896]{1,0:T(8,128)S(1)}, u32[]{:S(2)}, u32[]{:S(2)}) collective-permute-start(f32[16,896]{1,0:T(8,128)S(1)} %get-tuple-element.17), channel_id=1, source_target_pairs={{0,16},{8,24},{16,0},{24,8},{1,17},{9,25},{17,1},{25,9},{2,18},{10... | collective-permute-start | bytes 172040 | tf_op jit(solution)/shard_map/ppermute | solution.py:27
  23.6 0.9 %collective-permute-start.7 = (f32[16,896]{1,0:T(8,128)S(1)}, f32[16,896]{1,0:T(8,128)S(1)}, u32[]{:S(2)}, u32[]{:S(2)}) collective-permute-start(f32[16,896]{1,0:T(8,128)S(1)} %get-tuple-element.18), channel_id=1, source_target_pairs={{0,24},{8,16},{16,8},{24,0},{1,25},{9,17},{17,9},{25,1},{2,26},{10... | collective-permute-start | bytes 172040 | tf_op jit(solution)/shard_map/ppermute | solution.py:27
  24.6 1.3 %collective-permute-start.6 = (f32[16,896]{1,0:T(8,128)S(1)}, f32[16,896]{1,0:T(8,128)S(1)}, u32[]{:S(2)}, u32[]{:S(2)}) collective-permute-start(f32[16,896]{1,0:T(8,128)S(1)} %get-tuple-element.19), channel_id=1, source_target_pairs={{0,8},{8,0},{16,24},{24,16},{1,9},{9,1},{17,25},{25,17},{2,10},{10... | collective-permute-start | bytes 172040 | tf_op jit(solution)/shard_map/ppermute | solution.py:27
  25.9 2.4 %collective-permute-done.8.refs_3_ = f32[16,896]{1,0:T(8,128)S(1)} collective-permute-done((f32[16,896]{1,0:T(8,128)S(1)}, f32[16,896]{1,0:T(8,128)S(1)}, u32[]{:S(2)}, u32[]{:S(2)}) %collective-permute-start.8) | collective-permute-done | bytes 57376 | tf_op jit(solution)/shard_map/ppermute | solution.py:27
  28.3 1.3 %collective-permute-done.7.refs_2_ = f32[16,896]{1,0:T(8,128)S(1)} collective-permute-done((f32[16,896]{1,0:T(8,128)S(1)}, f32[16,896]{1,0:T(8,128)S(1)}, u32[]{:S(2)}, u32[]{:S(2)}) %collective-permute-start.7) | collective-permute-done | bytes 57376 | tf_op jit(solution)/shard_map/ppermute | solution.py:27
  29.6 0.0 collective-permute-done.6.refs_1_
  29.6 0.7 %finish.1 = (f32[1,4,16]{2,1,0:T(4,128)}, f32[4,16,512]{2,1,0:T(8,128)}, f32[1,16,256]{2,1,0:T(8,128)}) custom-call(f32[16,896]{1,0:T(8,128)S(1)} %get-tuple-element.20.refs_0_, f32[16,896]{1,0:T(8,128)S(1)} %collective-permute-done.6.refs_1_, f32[16,896]{1,0:T(8,128)S(1)} %collective-permute-done.7.refs_2_, f32[16,896]{1,0:T(8,128)S(1)} %collective-permute-done.8.refs_3_), custom_call_target="tpu_custom_call" | custom-call | tf_op jit(solution)/shard_map/finish/pallas_call | solution.py:415
  (9 shorter events, 0.1 us)
Async XLA Ops:
  1.5 7.5 %collective-permute-start.2 = (bf16[48,256]{1,0:T(8,128)(2,1)S(1)}, bf16[48,256]{1,0:T(8,128)(2,1)S(1)}, u32[]{:S(2)}, u32[]{:S(2)}) collective-permute-start(bf16[48,256]{1,0:T(8,128)(2,1)S(1)} %add_convert_fusion.refs_2_), channel_id=1, source_target_pairs={{0,16},{8,24},{16,0},{24,8},{1,17},{9,25},{17,1},{25,9},{2,18},{10... | collective-permute-start | bytes 73736 | tf_op jit(solution)/shard_map/ppermute | solution.py:27
  5.6 5.6 %collective-permute-start.1 = (bf16[48,256]{1,0:T(8,128)(2,1)S(1)}, bf16[48,256]{1,0:T(8,128)(2,1)S(1)}, u32[]{:S(2)}, u32[]{:S(2)}) collective-permute-start(bf16[48,256]{1,0:T(8,128)(2,1)S(1)} %add_convert_fusion.refs_2_), channel_id=1, source_target_pairs={{0,24},{8,16},{16,8},{24,0},{1,25},{9,17},{17,9},{25,1},{2,26},{10... | collective-permute-start | bytes 73736 | tf_op jit(solution)/shard_map/ppermute | solution.py:27
  7.0 4.3 %collective-permute-start = (bf16[48,256]{1,0:T(8,128)(2,1)S(1)}, bf16[48,256]{1,0:T(8,128)(2,1)S(1)}, u32[]{:S(2)}, u32[]{:S(2)}) collective-permute-start(bf16[48,256]{1,0:T(8,128)(2,1)S(1)} %add_convert_fusion.refs_2_), channel_id=1, source_target_pairs={{0,8},{8,0},{16,24},{24,16},{1,9},{9,1},{17,25},{25,17},{2,10},{10... | collective-permute-start | bytes 73736 | tf_op jit(solution)/shard_map/ppermute | solution.py:27
  15.3 2.6 %collective-permute-start.3 = (f32[2,4,16,512]{3,2,1,0:T(8,128)S(1)}, f32[2,4,16,512]{3,2,1,0:T(8,128)S(1)}, u32[]{:S(2)}, u32[]{:S(2)}) collective-permute-start(f32[2,4,16,512]{3,2,1,0:T(8,128)S(1)} %slice_bitcast_fusion), channel_id=1, source_target_pairs={{0,1},{1,0},{2,3},{3,2},{4,5},{5,4},{6,7},{7,6},{8,9},{9,8},{10,11... | collective-permute-start | bytes 786440 | tf_op jit(solution)/shard_map/ppermute | solution.py:27
  16.3 4.6 %collective-permute-start.5 = (f32[4,16,256]{2,1,0:T(8,128)S(1)}, f32[4,16,256]{2,1,0:T(8,128)S(1)}, u32[]{:S(2)}, u32[]{:S(2)}) collective-permute-start(f32[4,16,256]{2,1,0:T(8,128)S(1)} %acceptors.1), channel_id=1, source_target_pairs={{0,4},{4,0},{1,5},{5,1},{2,6},{6,2},{3,7},{7,3},{8,12},{12,8},{9,1... | collective-permute-start | bytes 196616 | tf_op jit(solution)/shard_map/ppermute | solution.py:27
  17.9 4.3 %collective-permute-start.4 = (bf16[4,16,512]{2,1,0:T(8,128)(2,1)S(1)}, bf16[4,16,512]{2,1,0:T(8,128)(2,1)S(1)}, u32[]{:S(2)}, u32[]{:S(2)}) collective-permute-start(bf16[4,16,512]{2,1,0:T(8,128)(2,1)S(1)} %fusion.5), channel_id=1, source_target_pairs={{0,2},{1,3},{2,0},{3,1},{4,6},{5,7},{6,4},{7,5},{8,10},{9,11},{10,... | collective-permute-start | bytes 196616 | tf_op jit(solution)/shard_map/ppermute | solution.py:27
  22.3 5.9 %collective-permute-start.8 = (f32[16,896]{1,0:T(8,128)S(1)}, f32[16,896]{1,0:T(8,128)S(1)}, u32[]{:S(2)}, u32[]{:S(2)}) collective-permute-start(f32[16,896]{1,0:T(8,128)S(1)} %get-tuple-element.17), channel_id=1, source_target_pairs={{0,16},{8,24},{16,0},{24,8},{1,17},{9,25},{17,1},{25,9},{2,18},{10... | collective-permute-start | bytes 172040 | tf_op jit(solution)/shard_map/ppermute | solution.py:27
  23.6 6.0 %collective-permute-start.7 = (f32[16,896]{1,0:T(8,128)S(1)}, f32[16,896]{1,0:T(8,128)S(1)}, u32[]{:S(2)}, u32[]{:S(2)}) collective-permute-start(f32[16,896]{1,0:T(8,128)S(1)} %get-tuple-element.18), channel_id=1, source_target_pairs={{0,24},{8,16},{16,8},{24,0},{1,25},{9,17},{17,9},{25,1},{2,26},{10... | collective-permute-start | bytes 172040 | tf_op jit(solution)/shard_map/ppermute | solution.py:27
  24.6 5.1 %collective-permute-start.6 = (f32[16,896]{1,0:T(8,128)S(1)}, f32[16,896]{1,0:T(8,128)S(1)}, u32[]{:S(2)}, u32[]{:S(2)}) collective-permute-start(f32[16,896]{1,0:T(8,128)S(1)} %get-tuple-element.19), channel_id=1, source_target_pairs={{0,8},{8,0},{16,24},{24,16},{1,9},{9,1},{17,25},{25,17},{2,10},{10... | collective-permute-start | bytes 172040 | tf_op jit(solution)/shard_map/ppermute | solution.py:27

commit v5 on v4

--- a/solution.py
+++ b/solution.py
@@ -129,8 +129,8 @@
 
 def silu_parts(half):
     turn = jnp.tanh(half)
-    tilted = half * turn
-    return half + tilted, (1.0 + turn) * ((1.0 + half) - tilted)
+    value = half + half * turn
+    return value, 2.0 - (1.0 - value) * (1.0 - turn)
 
 
 def ones_dot(left, right):

time: 30.6 us -> 30.3 us (level)
  transfers between devices with their start and end apart: 9 -> 9, of which waited for: 5 -> 5; matrix products, arithmetic and copies ran while one was open for 6% -> 7% of each run, Pallas kernels for 3% -> 3%
where the time goes in v5:
time: 30.3 us; the launch traced here: 30 us
  starting transfers between devices  12.4 us (41%)
  waiting for transfers between devices  8.63 us (28%)
  Pallas kernels  5.33 us (18%)
  other arithmetic  2.88 us (10%)
  between operations  0.73 us (2%)
    ppermute x9, starting transfers between devices, swapped(): lax.ppermute(value, axis, [(i, i ^ bits) for i in range(lax.axis_size(axi...  12.4 us
    ppermute x9, waiting for transfers between devices, swapped(): lax.ppermute(value, axis, [(i, i ^ bits) for i in range(lax.axis_size(axi...  8.63 us
    pallas_call x1, Pallas kernels, shared(): pl.pallas_call(functools.partial(head_kernel, blocks, blk, width), out_sh...  3.77 us
    convert_element_type x1, other arithmetic, halved(): return (value.astype(jnp.float32) * 0.5).astype(value.dtype)  0.99 us
    mul x1, other arithmetic, shared(): 0.5 * sum((placed(value, BINS + blk, row, lane) for value, row, lane in (...  0.9 us
    convert_element_type x1, other arithmetic, shared(): packed = (sites.astype(f32) + whole).astype(bf16)  0.89 us
    pallas_call x1, Pallas kernels, shared(): pl.pallas_call(functools.partial(acceptor_kernel, blocks, blk), out_shape...  0.88 us
    pallas_call x1, Pallas kernels, shared(): pl.pallas_call(functools.partial(finish_kernel, blocks, width, hidden), o...  0.68 us
  transfers between devices with their start and end apart: 9, of which 5 were waited for; matrix products, arithmetic and copies ran while one was open for 7% of the time, Pallas kernels for 3%

profile of v5, /device:TPU:0, one launch (start us, length us, event | category | flops | bytes accessed | tf_op | source)
XLA Modules:
  0.0 30.0 jit_solution(1363978599614683747)
XLA Ops:
  0.7 0.9 %add_convert_fusion.refs_2_ = bf16[48,256]{1,0:T(8,128)(2,1)S(1)} fusion(s32[4,16]{1,0:T(4,128)} %bitcast.30, s32[1,64]{1,0:T(1,128)} %param.12, s32[1,16]{1,0:T(1,128)} %param.11, s32[16,80]{1,0:T(8,128)} %bitcast.27, bf16[16,256]{1,0:T(8,128)(2,1)} %bitcast.28, bf16[16,256]{1,0:T(8,128)(2,1)} %bitcast.29, pred[256]{0:T(512)(128)(4,1)S(1)} %iota_compare_fusion, ...), kind=kLoop, calls=%fused_computation.18 | loop fusion | flops 196608 | bytes 46960 | tf_op jit(solution)/shard_map/convert_element_type | solution.py:363
  1.5 4.1 %collective-permute-start.2 = (bf16[48,256]{1,0:T(8,128)(2,1)S(1)}, bf16[48,256]{1,0:T(8,128)(2,1)S(1)}, u32[]{:S(2)}, u32[]{:S(2)}) collective-permute-start(bf16[48,256]{1,0:T(8,128)(2,1)S(1)} %add_convert_fusion.refs_2_), channel_id=1, source_target_pairs={{0,16},{8,24},{16,0},{24,8},{1,17},{9,25},{17,1},{25,9},{2,18},{10... | collective-permute-start | bytes 73736 | tf_op jit(solution)/shard_map/ppermute | solution.py:27
  5.6 1.3 %collective-permute-start.1 = (bf16[48,256]{1,0:T(8,128)(2,1)S(1)}, bf16[48,256]{1,0:T(8,128)(2,1)S(1)}, u32[]{:S(2)}, u32[]{:S(2)}) collective-permute-start(bf16[48,256]{1,0:T(8,128)(2,1)S(1)} %add_convert_fusion.refs_2_), channel_id=1, source_target_pairs={{0,24},{8,16},{16,8},{24,0},{1,25},{9,17},{17,9},{25,1},{2,26},{10... | collective-permute-start | bytes 73736 | tf_op jit(solution)/shard_map/ppermute | solution.py:27
  7.0 0.2 collective-permute-start
  7.2 1.0 %fusion.refs_1_.w_ref = bf16[256,512]{1,0:T(8,128)(2,1)S(1)} fusion(bf16[4,256,512]{2,1,0:T(8,128)(2,1)} %param.16, s32[]{:T(128)S(6)} %select_n.8), kind=kLoop, calls=%fused_computation.1 | loop fusion | flops 393216 | bytes 524292 | tf_op jit(solution)/shard_map/convert_element_type | solution.py:127
  8.2 0.9 %fusion.4.refs_0_ = bf16[144,256]{1,0:T(8,128)(2,1)S(1)} fusion(bf16[4,512]{1,0:T(4,128)(2,1)} %param.17, bf16[128,256]{1,0:T(8,128)(2,1)} %param.15), kind=kLoop, calls=%fused_computation.12 | loop fusion | flops 294912 | bytes 143360 | tf_op jit(solution)/shard_map/mul | solution.py:364
  9.1 0.0 collective-permute-done.2.refs_5_
  9.1 2.1 %collective-permute-done.1.refs_4_ = bf16[48,256]{1,0:T(8,128)(2,1)S(1)} collective-permute-done((bf16[48,256]{1,0:T(8,128)(2,1)S(1)}, bf16[48,256]{1,0:T(8,128)(2,1)S(1)}, u32[]{:S(2)}, u32[]{:S(2)}) %collective-permute-start.1) | collective-permute-done | bytes 24608 | tf_op jit(solution)/shard_map/ppermute | solution.py:27
  11.2 0.0 collective-permute-done.refs_3_
  11.2 3.8 %head.1 = (f32[2,2,4,16,512]{4,3,2,1,0:T(8,128)S(1)}, f32[4,16,128]{2,1,0:T(8,128)S(1)}, bf16[10,256,512]{2,1,0:T(8,128)(2,1)S(1)}, f32[10,256,256]{2,1,0:T(8,128)S(1)}) custom-call(bf16[144,256]{1,0:T(8,128)(2,1)S(1)} %fusion.4.refs_0_, bf16[256,512]{1,0:T(8,128)(2,1)S(1)} %fusion.refs_1_.w_ref, bf16[48,256]{1,0:T(8,128)(2,1)S(1)} %add_convert_fusion.refs_2_, ...), custom_call_target="tpu_custom_call" | custom-call | tf_op jit(solution)/shard_map/head/pallas_call | solution.py:377
  15.0 0.1 collective-permute-start.3
  15.1 0.9 %acceptors.1 = f32[4,16,256]{2,1,0:T(8,128)S(1)} custom-call(bf16[10,256,512]{2,1,0:T(8,128)(2,1)S(1)} %get-tuple-element.11.grad_ref, bf16[256,512]{1,0:T(8,128)(2,1)S(1)} %fusion.refs_1_.w_ref, f32[10,256,256]{2,1,0:T(8,128)S(1)} %get-tuple-element.12.slope_ref), custom_call_target="tpu_custom_call" | custom-call | flops 671088640 | bytes 5242880 | tf_op jit(solution)/shard_map/acceptors/pallas_call | solution.py:398
  16.0 1.6 %collective-permute-start.5 = (f32[4,16,256]{2,1,0:T(8,128)S(1)}, f32[4,16,256]{2,1,0:T(8,128)S(1)}, u32[]{:S(2)}, u32[]{:S(2)}) collective-permute-start(f32[4,16,256]{2,1,0:T(8,128)S(1)} %acceptors.1), channel_id=1, source_target_pairs={{0,4},{4,0},{1,5},{5,1},{2,6},{6,2},{3,7},{7,3},{8,12},{12,8},{9,1... | collective-permute-start | bytes 196616 | tf_op jit(solution)/shard_map/ppermute | solution.py:27
  17.6 0.0 collective-permute-done.3
  17.6 1.6 %collective-permute-start.4 = (bf16[4,16,512]{2,1,0:T(8,128)(2,1)S(1)}, bf16[4,16,512]{2,1,0:T(8,128)(2,1)S(1)}, u32[]{:S(2)}, u32[]{:S(2)}) collective-permute-start(bf16[4,16,512]{2,1,0:T(8,128)(2,1)S(1)} %fusion.5), channel_id=1, source_target_pairs={{0,2},{1,3},{2,0},{3,1},{4,6},{5,7},{6,4},{7,5},{8,10},{9,11},{10,... | collective-permute-start | bytes 196616 | tf_op jit(solution)/shard_map/ppermute | solution.py:27
  19.2 1.3 %collective-permute-done.5 = f32[4,16,256]{2,1,0:T(8,128)S(1)} collective-permute-done((f32[4,16,256]{2,1,0:T(8,128)S(1)}, f32[4,16,256]{2,1,0:T(8,128)S(1)}, u32[]{:S(2)}, u32[]{:S(2)}) %collective-permute-start.5) | collective-permute-done | bytes 65568 | tf_op jit(solution)/shard_map/ppermute | solution.py:27
  20.6 1.4 %collective-permute-done.4 = bf16[4,16,512]{2,1,0:T(8,128)(2,1)S(1)} collective-permute-done((bf16[4,16,512]{2,1,0:T(8,128)(2,1)S(1)}, bf16[4,16,512]{2,1,0:T(8,128)(2,1)S(1)}, u32[]{:S(2)}, u32[]{:S(2)}) %collective-permute-start.4) | collective-permute-done | bytes 65568 | tf_op jit(solution)/shard_map/ppermute | solution.py:27
  22.1 1.3 %collective-permute-start.8 = (f32[16,896]{1,0:T(8,128)S(1)}, f32[16,896]{1,0:T(8,128)S(1)}, u32[]{:S(2)}, u32[]{:S(2)}) collective-permute-start(f32[16,896]{1,0:T(8,128)S(1)} %get-tuple-element.17), channel_id=1, source_target_pairs={{0,16},{8,24},{16,0},{24,8},{1,17},{9,25},{17,1},{25,9},{2,18},{10... | collective-permute-start | bytes 172040 | tf_op jit(solution)/shard_map/ppermute | solution.py:27
  23.4 0.9 %collective-permute-start.7 = (f32[16,896]{1,0:T(8,128)S(1)}, f32[16,896]{1,0:T(8,128)S(1)}, u32[]{:S(2)}, u32[]{:S(2)}) collective-permute-start(f32[16,896]{1,0:T(8,128)S(1)} %get-tuple-element.18), channel_id=1, source_target_pairs={{0,24},{8,16},{16,8},{24,0},{1,25},{9,17},{17,9},{25,1},{2,26},{10... | collective-permute-start | bytes 172040 | tf_op jit(solution)/shard_map/ppermute | solution.py:27
  24.3 1.3 %collective-permute-start.6 = (f32[16,896]{1,0:T(8,128)S(1)}, f32[16,896]{1,0:T(8,128)S(1)}, u32[]{:S(2)}, u32[]{:S(2)}) collective-permute-start(f32[16,896]{1,0:T(8,128)S(1)} %get-tuple-element.19), channel_id=1, source_target_pairs={{0,8},{8,0},{16,24},{24,16},{1,9},{9,1},{17,25},{25,17},{2,10},{10... | collective-permute-start | bytes 172040 | tf_op jit(solution)/shard_map/ppermute | solution.py:27
  25.6 2.4 %collective-permute-done.8.refs_3_ = f32[16,896]{1,0:T(8,128)S(1)} collective-permute-done((f32[16,896]{1,0:T(8,128)S(1)}, f32[16,896]{1,0:T(8,128)S(1)}, u32[]{:S(2)}, u32[]{:S(2)}) %collective-permute-start.8) | collective-permute-done | bytes 57376 | tf_op jit(solution)/shard_map/ppermute | solution.py:27
  28.0 1.3 %collective-permute-done.7.refs_2_ = f32[16,896]{1,0:T(8,128)S(1)} collective-permute-done((f32[16,896]{1,0:T(8,128)S(1)}, f32[16,896]{1,0:T(8,128)S(1)}, u32[]{:S(2)}, u32[]{:S(2)}) %collective-permute-start.7) | collective-permute-done | bytes 57376 | tf_op jit(solution)/shard_map/ppermute | solution.py:27
  29.4 0.0 collective-permute-done.6.refs_1_
  29.4 0.7 %finish.1 = (f32[1,4,16]{2,1,0:T(4,128)}, f32[4,16,512]{2,1,0:T(8,128)}, f32[1,16,256]{2,1,0:T(8,128)}) custom-call(f32[16,896]{1,0:T(8,128)S(1)} %get-tuple-element.20.refs_0_, f32[16,896]{1,0:T(8,128)S(1)} %collective-permute-done.6.refs_1_, f32[16,896]{1,0:T(8,128)S(1)} %collective-permute-done.7.refs_2_, f32[16,896]{1,0:T(8,128)S(1)} %collective-permute-done.8.refs_3_), custom_call_target="tpu_custom_call" | custom-call | tf_op jit(solution)/shard_map/finish/pallas_call | solution.py:415
  (9 shorter events, 0.1 us)
Async XLA Ops:
  1.5 7.5 %collective-permute-start.2 = (bf16[48,256]{1,0:T(8,128)(2,1)S(1)}, bf16[48,256]{1,0:T(8,128)(2,1)S(1)}, u32[]{:S(2)}, u32[]{:S(2)}) collective-permute-start(bf16[48,256]{1,0:T(8,128)(2,1)S(1)} %add_convert_fusion.refs_2_), channel_id=1, source_target_pairs={{0,16},{8,24},{16,0},{24,8},{1,17},{9,25},{17,1},{25,9},{2,18},{10... | collective-permute-start | bytes 73736 | tf_op jit(solution)/shard_map/ppermute | solution.py:27
  5.6 5.6 %collective-permute-start.1 = (bf16[48,256]{1,0:T(8,128)(2,1)S(1)}, bf16[48,256]{1,0:T(8,128)(2,1)S(1)}, u32[]{:S(2)}, u32[]{:S(2)}) collective-permute-start(bf16[48,256]{1,0:T(8,128)(2,1)S(1)} %add_convert_fusion.refs_2_), channel_id=1, source_target_pairs={{0,24},{8,16},{16,8},{24,0},{1,25},{9,17},{17,9},{25,1},{2,26},{10... | collective-permute-start | bytes 73736 | tf_op jit(solution)/shard_map/ppermute | solution.py:27
  7.0 4.3 %collective-permute-start = (bf16[48,256]{1,0:T(8,128)(2,1)S(1)}, bf16[48,256]{1,0:T(8,128)(2,1)S(1)}, u32[]{:S(2)}, u32[]{:S(2)}) collective-permute-start(bf16[48,256]{1,0:T(8,128)(2,1)S(1)} %add_convert_fusion.refs_2_), channel_id=1, source_target_pairs={{0,8},{8,0},{16,24},{24,16},{1,9},{9,1},{17,25},{25,17},{2,10},{10... | collective-permute-start | bytes 73736 | tf_op jit(solution)/shard_map/ppermute | solution.py:27
  15.0 2.6 %collective-permute-start.3 = (f32[2,4,16,512]{3,2,1,0:T(8,128)S(1)}, f32[2,4,16,512]{3,2,1,0:T(8,128)S(1)}, u32[]{:S(2)}, u32[]{:S(2)}) collective-permute-start(f32[2,4,16,512]{3,2,1,0:T(8,128)S(1)} %slice_bitcast_fusion), channel_id=1, source_target_pairs={{0,1},{1,0},{2,3},{3,2},{4,5},{5,4},{6,7},{7,6},{8,9},{9,8},{10,11... | collective-permute-start | bytes 786440 | tf_op jit(solution)/shard_map/ppermute | solution.py:27
  16.0 4.6 %collective-permute-start.5 = (f32[4,16,256]{2,1,0:T(8,128)S(1)}, f32[4,16,256]{2,1,0:T(8,128)S(1)}, u32[]{:S(2)}, u32[]{:S(2)}) collective-permute-start(f32[4,16,256]{2,1,0:T(8,128)S(1)} %acceptors.1), channel_id=1, source_target_pairs={{0,4},{4,0},{1,5},{5,1},{2,6},{6,2},{3,7},{7,3},{8,12},{12,8},{9,1... | collective-permute-start | bytes 196616 | tf_op jit(solution)/shard_map/ppermute | solution.py:27
  17.6 4.3 %collective-permute-start.4 = (bf16[4,16,512]{2,1,0:T(8,128)(2,1)S(1)}, bf16[4,16,512]{2,1,0:T(8,128)(2,1)S(1)}, u32[]{:S(2)}, u32[]{:S(2)}) collective-permute-start(bf16[4,16,512]{2,1,0:T(8,128)(2,1)S(1)} %fusion.5), channel_id=1, source_target_pairs={{0,2},{1,3},{2,0},{3,1},{4,6},{5,7},{6,4},{7,5},{8,10},{9,11},{10,... | collective-permute-start | bytes 196616 | tf_op jit(solution)/shard_map/ppermute | solution.py:27
  22.1 6.0 %collective-permute-start.8 = (f32[16,896]{1,0:T(8,128)S(1)}, f32[16,896]{1,0:T(8,128)S(1)}, u32[]{:S(2)}, u32[]{:S(2)}) collective-permute-start(f32[16,896]{1,0:T(8,128)S(1)} %get-tuple-element.17), channel_id=1, source_target_pairs={{0,16},{8,24},{16,0},{24,8},{1,17},{9,25},{17,1},{25,9},{2,18},{10... | collective-permute-start | bytes 172040 | tf_op jit(solution)/shard_map/ppermute | solution.py:27
  23.4 6.0 %collective-permute-start.7 = (f32[16,896]{1,0:T(8,128)S(1)}, f32[16,896]{1,0:T(8,128)S(1)}, u32[]{:S(2)}, u32[]{:S(2)}) collective-permute-start(f32[16,896]{1,0:T(8,128)S(1)} %get-tuple-element.18), channel_id=1, source_target_pairs={{0,24},{8,16},{16,8},{24,0},{1,25},{9,17},{17,9},{25,1},{2,26},{10... | collective-permute-start | bytes 172040 | tf_op jit(solution)/shard_map/ppermute | solution.py:27
  24.3 5.1 %collective-permute-start.6 = (f32[16,896]{1,0:T(8,128)S(1)}, f32[16,896]{1,0:T(8,128)S(1)}, u32[]{:S(2)}, u32[]{:S(2)}) collective-permute-start(f32[16,896]{1,0:T(8,128)S(1)} %get-tuple-element.19), channel_id=1, source_target_pairs={{0,8},{8,0},{16,24},{24,16},{1,9},{9,1},{17,25},{25,17},{2,10},{10... | collective-permute-start | bytes 172040 | tf_op jit(solution)/shard_map/ppermute | solution.py:27

commit v6 on v5

--- a/solution.py
+++ b/solution.py
@@ -166,6 +166,9 @@
 
     lanes = lax.broadcasted_iota(jnp.int32, (blk, LANES), 1)
     ids = lax.broadcasted_iota(jnp.int32, (blk, LANES), 0)
+    spots = base_ref[BINS:, :LANES].astype(f32)
+    apos = spots[2 * blocks : 2 * blocks + 1, :] * 256.0
+    apos = apos + spots[2 * blocks + 1 : 2 * blocks + 2, :]
     codes = []
     aims = []
     for b in range(blocks):
@@ -176,7 +179,6 @@
             return jnp.sum(jnp.where(lanes == ids, row, 0.0), axis=1, keepdims=True)
 
         dpos = column(rows[:1, :] * 256.0 + rows[1:2, :])
-        apos = rows[2:3, :] * 256.0 + rows[3:4, :]
         aim = column(
             jnp.sum(jnp.where(ids == here + 4, rows, 0.0), axis=0, keepdims=True)
         ).astype(jnp.int32)
@@ -190,10 +192,10 @@
     w_half = w_ref[...]
     w_out = base_ref[BINS:, :].astype(f32)
     tissues = blocks
-    ids = lax.broadcasted_iota(jnp.int32, w_out.shape, 0)
+    row_ids = lax.broadcasted_iota(jnp.int32, w_out.shape, 0)
     w_out = jnp.concatenate(
         [
-            jnp.sum(jnp.where(ids == here + part * tissues, w_out, 0.0), axis=0, keepdims=True)
+            jnp.sum(jnp.where(row_ids == here + part * tissues, w_out, 0.0), axis=0, keepdims=True)
             for part in range(hidden // width)
         ],
         axis=1,
@@ -255,7 +257,9 @@
         expo = jnp.exp(masked - top)
         total = jnp.sum(expo, axis=1, keepdims=True) + jnp.exp(-top)
         picked = jnp.sum(jnp.where(chosen, logit, 0.0), axis=1, keepdims=True)
-        loss_ref[b ^ here] = jnp.broadcast_to(top + jnp.log(total) - picked, (blk, LANES))
+        loss = jnp.where(lanes == ids, top + jnp.log(total) - picked, 0.0)
+        loss = jnp.sum(loss, axis=0, keepdims=True)
+        loss_ref[b ^ here] = jnp.broadcast_to(loss, loss_ref.shape[1:])
         grad = expo / total - jnp.where(chosen, 1.0, 0.0)
         high = grad.astype(bf16).astype(f32)
         grads.append(high + pltpu.roll(grad - high, sites, 1))
@@ -289,20 +293,16 @@
     pieces = refs[:parts]
     (loss_ref, gh_ref, acc_ref) = refs[parts:]
     here = lax.axis_index("ctx")
-    blk = pieces[0].shape[0]
+    blk = acc_ref.shape[1]
     total = None
-    diagonal = lax.broadcasted_iota(jnp.int32, (blk, LANES), 0) == lax.broadcasted_iota(
-        jnp.int32, (blk, LANES), 1
-    )
     for piece, k in zip(pieces, (0,) + RETURN_ORDER):
         owner = here ^ k
-        gh_ref[owner] = piece[:, :hidden]
-        acc = piece[:, hidden : hidden + width]
+        groups = (hidden + width) // LANES
+        cuts = [piece[i * blk : (i + 1) * blk, :] for i in range(groups)]
+        gh_ref[owner] = jnp.concatenate(cuts[: hidden // LANES], axis=1)
+        acc = jnp.concatenate(cuts[hidden // LANES :], axis=1)
         total = acc if total is None else total + acc
-        row = jnp.sum(
-            jnp.where(diagonal, piece[:, hidden + width :], 0.0), axis=0, keepdims=True
-        )
-        loss_ref[0, pl.ds(owner, 1), :] = row[:, :blk]
+        loss_ref[0, pl.ds(owner, 1), :] = piece[groups * blk : groups * blk + 1, :blk]
     acc_ref[0] = total
 
 
@@ -350,15 +350,12 @@
             (pair_mask[0], last, 0),
             (donor_pos, last, LANES),
             (donor_pos, last + 1, LANES),
-            (acceptor_pos, last + 2, LANES),
-            (acceptor_pos, last + 3, LANES),
             (jnp.transpose(targets, (0, 2, 1))[0], last + 4, LANES),
         )
     )
     row = lax.broadcasted_iota(jnp.int32, whole.shape, 0)
     lane = lax.broadcasted_iota(jnp.int32, whole.shape, 1)
-    high = (lane >= LANES) & ((row == last) | (row == last + 2))
-    whole = jnp.where(high, whole >> 8, whole & 255).astype(f32)
+    whole = jnp.where((lane >= LANES) & (row == last), whole >> 8, whole & 255).astype(f32)
     sites = placed(donor_feat[0], rows, 0) + placed(acceptor_feat[0], rows, blk)
     packed = (sites.astype(f32) + whole).astype(bf16)
     base = 0.5 * sum(
@@ -369,6 +366,11 @@
             (output_weights, BINS + tissues, -width),
         )
     )
+    spots = placed(acceptor_pos, BINS + blk, BINS + 2 * tissues)
+    spots = spots + placed(acceptor_pos, BINS + blk, BINS + 2 * tissues + 1)
+    row = lax.broadcasted_iota(jnp.int32, spots.shape, 0)
+    spots = jnp.where(row == BINS + 2 * tissues, spots >> 8, spots & 255)
+    base = (base.astype(f32) + spots.astype(f32)).astype(bf16)
     w_in = halved(lax.dynamic_index_in_dim(hidden_weights, lax.axis_index("ctx"), 0, False))
     pieces = [swapped(packed, "ctx", k) for k in GATHER_ORDER]
     tiles = len(tiles_of(blocks))
@@ -378,7 +380,7 @@
         functools.partial(head_kernel, blocks, blk, width),
         out_shape=(
             jax.ShapeDtypeStruct((2, 2, blocks, chunk, hidden), f32),
-            jax.ShapeDtypeStruct((blocks, blk, LANES), f32),
+            jax.ShapeDtypeStruct((blocks, 8, LANES), f32),
             jax.ShapeDtypeStruct((tiles, pairs, hidden), bf16),
             jax.ShapeDtypeStruct((tiles, pairs, width), f32),
         ),
@@ -410,7 +412,8 @@
     sent = swapped(partial[1].astype(bf16), "rep", 2)
     acc = acc + swapped(acc, "tis", 1)
     partial = partial[0] + sent.astype(jnp.float32)
-    send = jnp.concatenate([partial, acc, loss], axis=2)
+    cuts = [part[:, :, i : i + LANES] for part in (partial, acc) for i in range(0, part.shape[2], LANES)]
+    send = jnp.concatenate(cuts + [loss], axis=1)
     arrived = [send[0]] + [swapped(send[k], "ctx", k) for k in RETURN_ORDER]
     donor_loss, grad_hidden, grad_acceptor = pl.pallas_call(
         functools.partial(finish_kernel, blocks, width, hidden),

time: 30.3 us -> 30.3 us (level)
    convert_element_type x0 -> x1, other arithmetic: none -> 0.98 us  [shared(): base = (base.astype(f32) + spots.astype(f32)).astype(bf16)]
    mul x1 -> x0, other arithmetic: 0.9 us -> none  [shared(): 0.5 * sum((placed(value, BINS + blk, row, lane) for value, row, lane in (...]
where the time goes in v6:
time: 30.3 us; the launch traced here: 30 us
  starting transfers between devices  12.4 us (41%)
  waiting for transfers between devices  8.5 us (28%)
  Pallas kernels  5.36 us (18%)
  other arithmetic  2.92 us (10%)
  between operations  0.77 us (3%)
    ppermute x9, starting transfers between devices, swapped(): lax.ppermute(value, axis, [(i, i ^ bits) for i in range(lax.axis_size(axi...  12.4 us
    ppermute x9, waiting for transfers between devices, swapped(): lax.ppermute(value, axis, [(i, i ^ bits) for i in range(lax.axis_size(axi...  8.5 us
    pallas_call x1, Pallas kernels, shared(): pl.pallas_call(functools.partial(head_kernel, blocks, blk, width), out_sh...  3.81 us
    convert_element_type x1, other arithmetic, halved(): return (value.astype(jnp.float32) * 0.5).astype(value.dtype)  0.99 us
    convert_element_type x1, other arithmetic, shared(): base = (base.astype(f32) + spots.astype(f32)).astype(bf16)  0.98 us
    pallas_call x1, Pallas kernels, shared(): pl.pallas_call(functools.partial(acceptor_kernel, blocks, blk), out_shape...  0.88 us
    convert_element_type x1, other arithmetic, shared(): packed = (sites.astype(f32) + whole).astype(bf16)  0.86 us
    pallas_call x1, Pallas kernels, shared(): pl.pallas_call(functools.partial(finish_kernel, blocks, width, hidden), o...  0.68 us
  transfers between devices with their start and end apart: 9, of which 5 were waited for; matrix products, arithmetic and copies ran while one was open for 7% of the time, Pallas kernels for 3%

profile of v6, /device:TPU:0, one launch (start us, length us, event | category | flops | bytes accessed | tf_op | source)
XLA Modules:
  0.0 30.0 jit_solution(8983670921115400311)
XLA Ops:
  0.7 0.9 %add_convert_fusion.1.refs_2_ = bf16[48,256]{1,0:T(8,128)(2,1)S(1)} fusion(s32[4,16]{1,0:T(4,128)} %bitcast.30, s32[1,16]{1,0:T(1,128)} %param.11, s32[16,80]{1,0:T(8,128)} %bitcast.27, bf16[16,256]{1,0:T(8,128)(2,1)} %bitcast.28, bf16[16,256]{1,0:T(8,128)(2,1)} %bitcast.29, pred[256]{0:T(512)(128)(4,1)S(1)} %iota_compare_fusion, ...), kind=kLoop, calls=%fused_computation.18 | loop fusion | flops 172032 | bytes 46704 | tf_op jit(solution)/shard_map/convert_element_type | solution.py:360
  1.5 4.0 %collective-permute-start.2 = (bf16[48,256]{1,0:T(8,128)(2,1)S(1)}, bf16[48,256]{1,0:T(8,128)(2,1)S(1)}, u32[]{:S(2)}, u32[]{:S(2)}) collective-permute-start(bf16[48,256]{1,0:T(8,128)(2,1)S(1)} %add_convert_fusion.1.refs_2_), channel_id=1, source_target_pairs={{0,16},{8,24},{16,0},{24,8},{1,17},{9,25},{17,1},{25,9},{2,18},{10... | collective-permute-start | bytes 73736 | tf_op jit(solution)/shard_map/ppermute | solution.py:27
  5.6 1.3 %collective-permute-start.1 = (bf16[48,256]{1,0:T(8,128)(2,1)S(1)}, bf16[48,256]{1,0:T(8,128)(2,1)S(1)}, u32[]{:S(2)}, u32[]{:S(2)}) collective-permute-start(bf16[48,256]{1,0:T(8,128)(2,1)S(1)} %add_convert_fusion.1.refs_2_), channel_id=1, source_target_pairs={{0,24},{8,16},{16,8},{24,0},{1,25},{9,17},{17,9},{25,1},{2,26},{10... | collective-permute-start | bytes 73736 | tf_op jit(solution)/shard_map/ppermute | solution.py:27
  6.9 0.2 collective-permute-start
  7.1 1.0 %add_convert_fusion.refs_0_ = bf16[144,256]{1,0:T(8,128)(2,1)S(1)} fusion(s32[1,64]{1,0:T(1,128)} %param.12, bf16[4,512]{1,0:T(4,128)(2,1)} %param.17, bf16[128,256]{1,0:T(8,128)(2,1)} %param.15, pred[144]{0:T(512)(128)(4,1)S(1)} %iota_compare_fusion.1), kind=kLoop, calls=%fused_computation.4 | loop fusion | flops 552960 | bytes 143760 | tf_op jit(solution)/shard_map/convert_element_type | solution.py:373
  8.1 1.0 %fusion.refs_1_.w_ref = bf16[256,512]{1,0:T(8,128)(2,1)S(1)} fusion(bf16[4,256,512]{2,1,0:T(8,128)(2,1)} %param.16, s32[]{:T(128)S(6)} %select_n.13), kind=kLoop, calls=%fused_computation.1 | loop fusion | flops 393216 | bytes 524292 | tf_op jit(solution)/shard_map/convert_element_type | solution.py:127
  9.1 0.0 collective-permute-done.2.refs_5_
  9.1 2.0 %collective-permute-done.1.refs_4_ = bf16[48,256]{1,0:T(8,128)(2,1)S(1)} collective-permute-done((bf16[48,256]{1,0:T(8,128)(2,1)S(1)}, bf16[48,256]{1,0:T(8,128)(2,1)S(1)}, u32[]{:S(2)}, u32[]{:S(2)}) %collective-permute-start.1) | collective-permute-done | bytes 24608 | tf_op jit(solution)/shard_map/ppermute | solution.py:27
  11.2 0.0 collective-permute-done.refs_3_
  11.2 3.8 %head.1 = (f32[2,2,4,16,512]{4,3,2,1,0:T(8,128)S(1)}, f32[4,8,128]{2,1,0:T(8,128)S(1)}, bf16[10,256,512]{2,1,0:T(8,128)(2,1)S(1)}, f32[10,256,256]{2,1,0:T(8,128)S(1)}) custom-call(bf16[144,256]{1,0:T(8,128)(2,1)S(1)} %add_convert_fusion.refs_0_, bf16[256,512]{1,0:T(8,128)(2,1)S(1)} %fusion.refs_1_.w_ref, bf16[48,256]{1,0:T(8,128)(2,1)S(1)} %add_convert_fusion.1.refs_2_, ...), custom_call_target="tpu_custom_call" | custom-call | tf_op jit(solution)/shard_map/head/pallas_call | solution.py:379
  15.0 0.1 collective-permute-start.3
  15.1 0.9 %acceptors.1 = f32[4,16,256]{2,1,0:T(8,128)S(1)} custom-call(bf16[10,256,512]{2,1,0:T(8,128)(2,1)S(1)} %get-tuple-element.11.grad_ref, bf16[256,512]{1,0:T(8,128)(2,1)S(1)} %fusion.refs_1_.w_ref, f32[10,256,256]{2,1,0:T(8,128)S(1)} %get-tuple-element.12.slope_ref), custom_call_target="tpu_custom_call" | custom-call | flops 671088640 | bytes 5242880 | tf_op jit(solution)/shard_map/acceptors/pallas_call | solution.py:400
  16.0 1.6 %collective-permute-start.5 = (f32[4,16,256]{2,1,0:T(8,128)S(1)}, f32[4,16,256]{2,1,0:T(8,128)S(1)}, u32[]{:S(2)}, u32[]{:S(2)}) collective-permute-start(f32[4,16,256]{2,1,0:T(8,128)S(1)} %acceptors.1), channel_id=1, source_target_pairs={{0,4},{4,0},{1,5},{5,1},{2,6},{6,2},{3,7},{7,3},{8,12},{12,8},{9,1... | collective-permute-start | bytes 196616 | tf_op jit(solution)/shard_map/ppermute | solution.py:27
  17.6 0.0 collective-permute-done.3
  17.6 1.5 %collective-permute-start.4 = (bf16[4,16,512]{2,1,0:T(8,128)(2,1)S(1)}, bf16[4,16,512]{2,1,0:T(8,128)(2,1)S(1)}, u32[]{:S(2)}, u32[]{:S(2)}) collective-permute-start(bf16[4,16,512]{2,1,0:T(8,128)(2,1)S(1)} %fusion.5), channel_id=1, source_target_pairs={{0,2},{1,3},{2,0},{3,1},{4,6},{5,7},{6,4},{7,5},{8,10},{9,11},{10,... | collective-permute-start | bytes 196616 | tf_op jit(solution)/shard_map/ppermute | solution.py:27
  19.2 1.4 %collective-permute-done.5 = f32[4,16,256]{2,1,0:T(8,128)S(1)} collective-permute-done((f32[4,16,256]{2,1,0:T(8,128)S(1)}, f32[4,16,256]{2,1,0:T(8,128)S(1)}, u32[]{:S(2)}, u32[]{:S(2)}) %collective-permute-start.5) | collective-permute-done | bytes 65568 | tf_op jit(solution)/shard_map/ppermute | solution.py:27
  20.6 1.4 %collective-permute-done.4 = bf16[4,16,512]{2,1,0:T(8,128)(2,1)S(1)} collective-permute-done((bf16[4,16,512]{2,1,0:T(8,128)(2,1)S(1)}, bf16[4,16,512]{2,1,0:T(8,128)(2,1)S(1)}, u32[]{:S(2)}, u32[]{:S(2)}) %collective-permute-start.4) | collective-permute-done | bytes 65568 | tf_op jit(solution)/shard_map/ppermute | solution.py:27
  22.1 1.3 %collective-permute-start.8 = (f32[104,128]{1,0:T(8,128)S(1)}, f32[104,128]{1,0:T(8,128)S(1)}, u32[]{:S(2)}, u32[]{:S(2)}) collective-permute-start(f32[104,128]{1,0:T(8,128)S(1)} %get-tuple-element.17), channel_id=1, source_target_pairs={{0,16},{8,24},{16,0},{24,8},{1,17},{9,25},{17,1},{25,9},{2,18},{10... | collective-permute-start | bytes 159752 | tf_op jit(solution)/shard_map/ppermute | solution.py:27
  23.4 1.0 %collective-permute-start.7 = (f32[104,128]{1,0:T(8,128)S(1)}, f32[104,128]{1,0:T(8,128)S(1)}, u32[]{:S(2)}, u32[]{:S(2)}) collective-permute-start(f32[104,128]{1,0:T(8,128)S(1)} %get-tuple-element.18), channel_id=1, source_target_pairs={{0,24},{8,16},{16,8},{24,0},{1,25},{9,17},{17,9},{25,1},{2,26},{10... | collective-permute-start | bytes 159752 | tf_op jit(solution)/shard_map/ppermute | solution.py:27
  24.4 1.3 %collective-permute-start.6 = (f32[104,128]{1,0:T(8,128)S(1)}, f32[104,128]{1,0:T(8,128)S(1)}, u32[]{:S(2)}, u32[]{:S(2)}) collective-permute-start(f32[104,128]{1,0:T(8,128)S(1)} %get-tuple-element.19), channel_id=1, source_target_pairs={{0,8},{8,0},{16,24},{24,16},{1,9},{9,1},{17,25},{25,17},{2,10},{10... | collective-permute-start | bytes 159752 | tf_op jit(solution)/shard_map/ppermute | solution.py:27
  25.7 2.2 %collective-permute-done.8.refs_3_ = f32[104,128]{1,0:T(8,128)S(1)} collective-permute-done((f32[104,128]{1,0:T(8,128)S(1)}, f32[104,128]{1,0:T(8,128)S(1)}, u32[]{:S(2)}, u32[]{:S(2)}) %collective-permute-start.8) | collective-permute-done | bytes 53280 | tf_op jit(solution)/shard_map/ppermute | solution.py:27
  27.9 1.5 %collective-permute-done.7.refs_2_ = f32[104,128]{1,0:T(8,128)S(1)} collective-permute-done((f32[104,128]{1,0:T(8,128)S(1)}, f32[104,128]{1,0:T(8,128)S(1)}, u32[]{:S(2)}, u32[]{:S(2)}) %collective-permute-start.7) | collective-permute-done | bytes 53280 | tf_op jit(solution)/shard_map/ppermute | solution.py:27
  29.3 0.0 collective-permute-done.6.refs_1_
  29.3 0.7 %finish.1 = (f32[1,4,16]{2,1,0:T(4,128)}, f32[4,16,512]{2,1,0:T(8,128)}, f32[1,16,256]{2,1,0:T(8,128)}) custom-call(f32[104,128]{1,0:T(8,128)S(1)} %get-tuple-element.20.refs_0_, f32[104,128]{1,0:T(8,128)S(1)} %collective-permute-done.6.refs_1_, f32[104,128]{1,0:T(8,128)S(1)} %collective-permute-done.7.refs_2_, f32[104,128]{1,0:T(8,128)S(1)} %collective-permute-done.8.refs_3_), custom_call_target="tpu_custom_call" | custom-call | tf_op jit(solution)/shard_map/finish/pallas_call | solution.py:418
  (16 shorter events, 0.2 us)
Async XLA Ops:
  1.5 7.6 %collective-permute-start.2 = (bf16[48,256]{1,0:T(8,128)(2,1)S(1)}, bf16[48,256]{1,0:T(8,128)(2,1)S(1)}, u32[]{:S(2)}, u32[]{:S(2)}) collective-permute-start(bf16[48,256]{1,0:T(8,128)(2,1)S(1)} %add_convert_fusion.1.refs_2_), channel_id=1, source_target_pairs={{0,16},{8,24},{16,0},{24,8},{1,17},{9,25},{17,1},{25,9},{2,18},{10... | collective-permute-start | bytes 73736 | tf_op jit(solution)/shard_map/ppermute | solution.py:27
  5.6 5.6 %collective-permute-start.1 = (bf16[48,256]{1,0:T(8,128)(2,1)S(1)}, bf16[48,256]{1,0:T(8,128)(2,1)S(1)}, u32[]{:S(2)}, u32[]{:S(2)}) collective-permute-start(bf16[48,256]{1,0:T(8,128)(2,1)S(1)} %add_convert_fusion.1.refs_2_), channel_id=1, source_target_pairs={{0,24},{8,16},{16,8},{24,0},{1,25},{9,17},{17,9},{25,1},{2,26},{10... | collective-permute-start | bytes 73736 | tf_op jit(solution)/shard_map/ppermute | solution.py:27
  6.9 4.3 %collective-permute-start = (bf16[48,256]{1,0:T(8,128)(2,1)S(1)}, bf16[48,256]{1,0:T(8,128)(2,1)S(1)}, u32[]{:S(2)}, u32[]{:S(2)}) collective-permute-start(bf16[48,256]{1,0:T(8,128)(2,1)S(1)} %add_convert_fusion.1.refs_2_), channel_id=1, source_target_pairs={{0,8},{8,0},{16,24},{24,16},{1,9},{9,1},{17,25},{25,17},{2,10},{10... | collective-permute-start | bytes 73736 | tf_op jit(solution)/shard_map/ppermute | solution.py:27
  15.0 2.6 %collective-permute-start.3 = (f32[2,4,16,512]{3,2,1,0:T(8,128)S(1)}, f32[2,4,16,512]{3,2,1,0:T(8,128)S(1)}, u32[]{:S(2)}, u32[]{:S(2)}) collective-permute-start(f32[2,4,16,512]{3,2,1,0:T(8,128)S(1)} %slice_bitcast_fusion), channel_id=1, source_target_pairs={{0,1},{1,0},{2,3},{3,2},{4,5},{5,4},{6,7},{7,6},{8,9},{9,8},{10,11... | collective-permute-start | bytes 786440 | tf_op jit(solution)/shard_map/ppermute | solution.py:27
  16.0 4.6 %collective-permute-start.5 = (f32[4,16,256]{2,1,0:T(8,128)S(1)}, f32[4,16,256]{2,1,0:T(8,128)S(1)}, u32[]{:S(2)}, u32[]{:S(2)}) collective-permute-start(f32[4,16,256]{2,1,0:T(8,128)S(1)} %acceptors.1), channel_id=1, source_target_pairs={{0,4},{4,0},{1,5},{5,1},{2,6},{6,2},{3,7},{7,3},{8,12},{12,8},{9,1... | collective-permute-start | bytes 196616 | tf_op jit(solution)/shard_map/ppermute | solution.py:27
  17.6 4.3 %collective-permute-start.4 = (bf16[4,16,512]{2,1,0:T(8,128)(2,1)S(1)}, bf16[4,16,512]{2,1,0:T(8,128)(2,1)S(1)}, u32[]{:S(2)}, u32[]{:S(2)}) collective-permute-start(bf16[4,16,512]{2,1,0:T(8,128)(2,1)S(1)} %fusion.5), channel_id=1, source_target_pairs={{0,2},{1,3},{2,0},{3,1},{4,6},{5,7},{6,4},{7,5},{8,10},{9,11},{10,... | collective-permute-start | bytes 196616 | tf_op jit(solution)/shard_map/ppermute | solution.py:27
  22.1 5.7 %collective-permute-start.8 = (f32[104,128]{1,0:T(8,128)S(1)}, f32[104,128]{1,0:T(8,128)S(1)}, u32[]{:S(2)}, u32[]{:S(2)}) collective-permute-start(f32[104,128]{1,0:T(8,128)S(1)} %get-tuple-element.17), channel_id=1, source_target_pairs={{0,16},{8,24},{16,0},{24,8},{1,17},{9,25},{17,1},{25,9},{2,18},{10... | collective-permute-start | bytes 159752 | tf_op jit(solution)/shard_map/ppermute | solution.py:27
  23.4 5.9 %collective-permute-start.7 = (f32[104,128]{1,0:T(8,128)S(1)}, f32[104,128]{1,0:T(8,128)S(1)}, u32[]{:S(2)}, u32[]{:S(2)}) collective-permute-start(f32[104,128]{1,0:T(8,128)S(1)} %get-tuple-element.18), channel_id=1, source_target_pairs={{0,24},{8,16},{16,8},{24,0},{1,25},{9,17},{17,9},{25,1},{2,26},{10... | collective-permute-start | bytes 159752 | tf_op jit(solution)/shard_map/ppermute | solution.py:27
  24.4 5.0 %collective-permute-start.6 = (f32[104,128]{1,0:T(8,128)S(1)}, f32[104,128]{1,0:T(8,128)S(1)}, u32[]{:S(2)}, u32[]{:S(2)}) collective-permute-start(f32[104,128]{1,0:T(8,128)S(1)} %get-tuple-element.19), channel_id=1, source_target_pairs={{0,8},{8,0},{16,24},{24,16},{1,9},{9,1},{17,25},{25,17},{2,10},{10... | collective-permute-start | bytes 159752 | tf_op jit(solution)/shard_map/ppermute | solution.py:27

commit v7 on v6

--- a/solution.py
+++ b/solution.py
@@ -144,14 +144,14 @@
 def head_kernel(blocks, blk, width, *refs):
     (base_ref, w_ref) = refs[:2]
     packed = refs[2 : blocks + 2]
-    (gh_ref, loss_ref, grad_s, dpre_s) = refs[blocks + 2 : blocks + 6]
-    (source, aux, picks_s, pair_s, act_s, dhid_s, gh_s) = refs[blocks + 6 :]
+    (gh_ref, send_ref, loss_ref, grad_s, dpre_s) = refs[blocks + 2 : blocks + 7]
+    (source, aux, picks_s, pair_s, act_s, dhid_s) = refs[blocks + 7 :]
     here = lax.axis_index("ctx")
     rep = lax.axis_index("rep")
     cross = lax.div(rep, 2)
     core = lax.rem(rep, 2)
     f32, bf16 = jnp.float32, jnp.bfloat16
-    hidden = gh_s.shape[1]
+    hidden = gh_ref.shape[1]
     pairs = blk * blk
     sites = blocks * blk
     slots = (SPAN_BLOCKS + 1) * blk
@@ -279,14 +279,29 @@
         rows = jnp.concatenate([rows] * (hidden // LANES), axis=1)
         grad_s[tile] = (rows * dhid_s[tile]).astype(bf16)
         if tile == middle:
-            gh_s[...] = gradient_of(0, middle)
-    total = gh_s[...] + gradient_of(middle, len(tiles))
-    chunk = gh_ref.shape[3]
-    for c in range(blocks):
-        for x in range(2):
-            for y in range(2):
-                start = ((c * 2 + x) * 2 + y) * chunk
-                gh_ref[y ^ core, x ^ cross, c ^ here] = total[start : start + chunk, :]
+            gh_ref[...] = gradient_of(0, middle)
+    gh_ref[...] += gradient_of(middle, len(tiles))
+    chunk = send_ref.shape[2]
+    for x in range(2):
+        for c in range(blocks):
+            start = (((c ^ here) * 2 + (x ^ cross)) * 2 + 1 - core) * chunk
+            send_ref[x, c] = gh_ref[pl.ds(pl.multiple_of(start, chunk), chunk), :]
+
+
+def core_kernel(blocks, gh_ref, sent_ref, kept_ref, send_ref):
+    here = lax.axis_index("ctx")
+    rep = lax.axis_index("rep")
+    cross = lax.div(rep, 2)
+    core = lax.rem(rep, 2)
+    chunk = sent_ref.shape[2]
+    for x in range(2):
+        for c in range(blocks):
+            start = (((c ^ here) * 2 + (x ^ cross)) * 2 + core) * chunk
+            rows = gh_ref[pl.ds(pl.multiple_of(start, chunk), chunk), :] + sent_ref[x, c]
+            if x:
+                send_ref[c] = rows.astype(send_ref.dtype)
+            else:
+                kept_ref[c] = rows
 
 
 def finish_kernel(parts, width, hidden, *refs):
@@ -376,10 +391,11 @@
     tiles = len(tiles_of(blocks))
     chunk = width // (4 * blocks)
     pairs = blk * blk
-    partial, loss, grad, slope = pl.pallas_call(
+    partial, sent, loss, grad, slope = pl.pallas_call(
         functools.partial(head_kernel, blocks, blk, width),
         out_shape=(
-            jax.ShapeDtypeStruct((2, 2, blocks, chunk, hidden), f32),
+            jax.ShapeDtypeStruct((width, hidden), f32),
+            jax.ShapeDtypeStruct((2, blocks, chunk, hidden), f32),
             jax.ShapeDtypeStruct((blocks, 8, LANES), f32),
             jax.ShapeDtypeStruct((tiles, pairs, hidden), bf16),
             jax.ShapeDtypeStruct((tiles, pairs, width), f32),
@@ -391,12 +407,11 @@
             pltpu.VMEM((tiles, pairs, width), bf16),
             pltpu.VMEM((tiles, pairs, hidden), bf16),
             pltpu.VMEM((tiles, pairs, hidden), f32),
-            pltpu.VMEM((width, hidden), f32),
         ],
         compiler_params=pltpu.CompilerParams(vmem_limit_bytes=32 * 2**20),
         name="head",
     )(base, w_in, packed, *pieces)
-    kept, sent = partial[0], swapped(partial[1], "rep", 1)
+    sent = swapped(sent, "rep", 1)
     acc = pl.pallas_call(
         functools.partial(acceptor_kernel, blocks, blk),
         out_shape=jax.ShapeDtypeStruct((blocks, blk, width), f32),
@@ -408,10 +423,18 @@
         ),
         name="acceptors",
     )(grad, w_in, slope)
-    partial = kept + sent
-    sent = swapped(partial[1].astype(bf16), "rep", 2)
+    kept, sent = pl.pallas_call(
+        functools.partial(core_kernel, blocks),
+        out_shape=(
+            jax.ShapeDtypeStruct((blocks, chunk, hidden), f32),
+            jax.ShapeDtypeStruct((blocks, chunk, hidden), bf16),
+        ),
+        compiler_params=pltpu.CompilerParams(vmem_limit_bytes=8 * 2**20),
+        name="core",
+    )(partial, sent)
+    sent = swapped(sent, "rep", 2)
     acc = acc + swapped(acc, "tis", 1)
-    partial = partial[0] + sent.astype(jnp.float32)
+    partial = kept + sent.astype(f32)
     cuts = [part[:, :, i : i + LANES] for part in (partial, acc) for i in range(0, part.shape[2], LANES)]
     send = jnp.concatenate(cuts + [loss], axis=1)
     arrived = [send[0]] + [swapped(send[k], "ctx", k) for k in RETURN_ORDER]

time: 30.3 us -> 30.2 us (level)
  no operation moved by 1% of the time
where the time goes in v7:
time: 30.2 us; the launch traced here: 30 us
  starting transfers between devices  12.4 us (41%)
  waiting for transfers between devices  8.5 us (28%)
  Pallas kernels  5.42 us (18%)
  other arithmetic  2.88 us (10%)
  between operations  0.76 us (3%)
    ppermute x9, starting transfers between devices, swapped(): lax.ppermute(value, axis, [(i, i ^ bits) for i in range(lax.axis_size(axi...  12.4 us
    ppermute x9, waiting for transfers between devices, swapped(): lax.ppermute(value, axis, [(i, i ^ bits) for i in range(lax.axis_size(axi...  8.5 us
    pallas_call x1, Pallas kernels, shared(): pl.pallas_call(functools.partial(head_kernel, blocks, blk, width), out_sh...  3.83 us
    convert_element_type x1, other arithmetic, halved(): return (value.astype(jnp.float32) * 0.5).astype(value.dtype)  0.99 us
    convert_element_type x1, other arithmetic, shared(): base = (base.astype(f32) + spots.astype(f32)).astype(bf16)  0.98 us
    pallas_call x1, Pallas kernels, shared(): pl.pallas_call(functools.partial(acceptor_kernel, blocks, blk), out_shape...  0.88 us
    convert_element_type x1, other arithmetic, shared(): packed = (sites.astype(f32) + whole).astype(bf16)  0.86 us
    pallas_call x1, Pallas kernels, shared(): pl.pallas_call(functools.partial(finish_kernel, blocks, width, hidden), o...  0.68 us
  transfers between devices with their start and end apart: 9, of which 5 were waited for; matrix products, arithmetic and copies ran while one was open for 7% of the time, Pallas kernels for 3%

profile of v7, /device:TPU:0, one launch (start us, length us, event | category | flops | bytes accessed | tf_op | source)
XLA Modules:
  0.0 30.0 jit_solution(6813328284140063041)
XLA Ops:
  0.7 0.9 %add_convert_fusion.1.refs_2_ = bf16[48,256]{1,0:T(8,128)(2,1)S(1)} fusion(s32[4,16]{1,0:T(4,128)} %bitcast.20, s32[1,16]{1,0:T(1,128)} %param.11, s32[16,80]{1,0:T(8,128)} %bitcast.17, bf16[16,256]{1,0:T(8,128)(2,1)} %bitcast.18, bf16[16,256]{1,0:T(8,128)(2,1)} %bitcast.19, pred[256]{0:T(512)(128)(4,1)S(1)} %iota_compare_fusion, ...), kind=kLoop, calls=%fused_computation.13 | loop fusion | flops 172032 | bytes 46704 | tf_op jit(solution)/shard_map/convert_element_type | solution.py:375
  1.5 4.0 %collective-permute-start.2 = (bf16[48,256]{1,0:T(8,128)(2,1)S(1)}, bf16[48,256]{1,0:T(8,128)(2,1)S(1)}, u32[]{:S(2)}, u32[]{:S(2)}) collective-permute-start(bf16[48,256]{1,0:T(8,128)(2,1)S(1)} %add_convert_fusion.1.refs_2_), channel_id=1, source_target_pairs={{0,16},{8,24},{16,0},{24,8},{1,17},{9,25},{17,1},{25,9},{2,18},{10... | collective-permute-start | bytes 73736 | tf_op jit(solution)/shard_map/ppermute | solution.py:27
  5.6 1.3 %collective-permute-start.1 = (bf16[48,256]{1,0:T(8,128)(2,1)S(1)}, bf16[48,256]{1,0:T(8,128)(2,1)S(1)}, u32[]{:S(2)}, u32[]{:S(2)}) collective-permute-start(bf16[48,256]{1,0:T(8,128)(2,1)S(1)} %add_convert_fusion.1.refs_2_), channel_id=1, source_target_pairs={{0,24},{8,16},{16,8},{24,0},{1,25},{9,17},{17,9},{25,1},{2,26},{10... | collective-permute-start | bytes 73736 | tf_op jit(solution)/shard_map/ppermute | solution.py:27
  6.9 0.2 collective-permute-start
  7.1 1.0 %add_convert_fusion.refs_0_ = bf16[144,256]{1,0:T(8,128)(2,1)S(1)} fusion(s32[1,64]{1,0:T(1,128)} %param.12, bf16[4,512]{1,0:T(4,128)(2,1)} %param.17, bf16[128,256]{1,0:T(8,128)(2,1)} %param.15, pred[144]{0:T(512)(128)(4,1)S(1)} %iota_compare_fusion.1), kind=kLoop, calls=%fused_computation.2 | loop fusion | flops 552960 | bytes 143760 | tf_op jit(solution)/shard_map/convert_element_type | solution.py:388
  8.1 1.0 %fusion.refs_1_.w_ref = bf16[256,512]{1,0:T(8,128)(2,1)S(1)} fusion(bf16[4,256,512]{2,1,0:T(8,128)(2,1)} %param.16, s32[]{:T(128)S(6)} %select_n.13), kind=kLoop, calls=%fused_computation.1 | loop fusion | flops 393216 | bytes 524292 | tf_op jit(solution)/shard_map/convert_element_type | solution.py:127
  9.1 0.0 collective-permute-done.2.refs_5_
  9.1 2.0 %collective-permute-done.1.refs_4_ = bf16[48,256]{1,0:T(8,128)(2,1)S(1)} collective-permute-done((bf16[48,256]{1,0:T(8,128)(2,1)S(1)}, bf16[48,256]{1,0:T(8,128)(2,1)S(1)}, u32[]{:S(2)}, u32[]{:S(2)}) %collective-permute-start.1) | collective-permute-done | bytes 24608 | tf_op jit(solution)/shard_map/ppermute | solution.py:27
  11.2 0.0 collective-permute-done.refs_3_
  11.2 3.8 %head.1 = (f32[256,512]{1,0:T(8,128)S(1)}, f32[2,4,16,512]{3,2,1,0:T(8,128)S(1)}, f32[4,8,128]{2,1,0:T(8,128)S(1)}, bf16[10,256,512]{2,1,0:T(8,128)(2,1)S(1)}, f32[10,256,256]{2,1,0:T(8,128)S(1)}) custom-call(bf16[144,256]{1,0:T(8,128)(2,1)S(1)} %add_convert_fusion.refs_0_, bf16[256,512]{1,0:T(8,128)(2,1)S(1)} %fusion.refs_1_.w_ref, ...), custom_call_target="tpu_custom_call" | custom-call | tf_op jit(solution)/shard_map/head/pallas_call | solution.py:394
  15.0 0.1 collective-permute-start.3
  15.1 0.9 %acceptors.1 = f32[4,16,256]{2,1,0:T(8,128)S(1)} custom-call(bf16[10,256,512]{2,1,0:T(8,128)(2,1)S(1)} %get-tuple-element.17.grad_ref, bf16[256,512]{1,0:T(8,128)(2,1)S(1)} %fusion.refs_1_.w_ref, f32[10,256,256]{2,1,0:T(8,128)S(1)} %get-tuple-element.18.slope_ref), custom_call_target="tpu_custom_call" | custom-call | flops 671088640 | bytes 5242880 | tf_op jit(solution)/shard_map/acceptors/pallas_call | solution.py:415
  16.0 1.6 %collective-permute-start.5 = (f32[4,16,256]{2,1,0:T(8,128)S(1)}, f32[4,16,256]{2,1,0:T(8,128)S(1)}, u32[]{:S(2)}, u32[]{:S(2)}) collective-permute-start(f32[4,16,256]{2,1,0:T(8,128)S(1)} %acceptors.1), channel_id=1, source_target_pairs={{0,4},{4,0},{1,5},{5,1},{2,6},{6,2},{3,7},{7,3},{8,12},{12,8},{9,1... | collective-permute-start | bytes 196616 | tf_op jit(solution)/shard_map/ppermute | solution.py:27
  17.6 0.0 collective-permute-done.3.sent_ref
  17.6 1.5 %collective-permute-start.4 = (bf16[4,16,512]{2,1,0:T(8,128)(2,1)S(1)}, bf16[4,16,512]{2,1,0:T(8,128)(2,1)S(1)}, u32[]{:S(2)}, u32[]{:S(2)}) collective-permute-start(bf16[4,16,512]{2,1,0:T(8,128)(2,1)S(1)} %get-tuple-element.16), channel_id=1, source_target_pairs={{0,2},{1,3},{2,0},{3,1},{4,6},{5,7},{6,4},{7,5},{8,10},{9,11},{10,... | collective-permute-start | bytes 196616 | tf_op jit(solution)/shard_map/ppermute | solution.py:27
  19.2 1.4 %collective-permute-done.5 = f32[4,16,256]{2,1,0:T(8,128)S(1)} collective-permute-done((f32[4,16,256]{2,1,0:T(8,128)S(1)}, f32[4,16,256]{2,1,0:T(8,128)S(1)}, u32[]{:S(2)}, u32[]{:S(2)}) %collective-permute-start.5) | collective-permute-done | bytes 65568 | tf_op jit(solution)/shard_map/ppermute | solution.py:27
  20.6 1.4 %collective-permute-done.4 = bf16[4,16,512]{2,1,0:T(8,128)(2,1)S(1)} collective-permute-done((bf16[4,16,512]{2,1,0:T(8,128)(2,1)S(1)}, bf16[4,16,512]{2,1,0:T(8,128)(2,1)S(1)}, u32[]{:S(2)}, u32[]{:S(2)}) %collective-permute-start.4) | collective-permute-done | bytes 65568 | tf_op jit(solution)/shard_map/ppermute | solution.py:27
  22.1 1.3 %collective-permute-start.8 = (f32[104,128]{1,0:T(8,128)S(1)}, f32[104,128]{1,0:T(8,128)S(1)}, u32[]{:S(2)}, u32[]{:S(2)}) collective-permute-start(f32[104,128]{1,0:T(8,128)S(1)} %get-tuple-element.23), channel_id=1, source_target_pairs={{0,16},{8,24},{16,0},{24,8},{1,17},{9,25},{17,1},{25,9},{2,18},{10... | collective-permute-start | bytes 159752 | tf_op jit(solution)/shard_map/ppermute | solution.py:27
  23.4 1.0 %collective-permute-start.7 = (f32[104,128]{1,0:T(8,128)S(1)}, f32[104,128]{1,0:T(8,128)S(1)}, u32[]{:S(2)}, u32[]{:S(2)}) collective-permute-start(f32[104,128]{1,0:T(8,128)S(1)} %get-tuple-element.24), channel_id=1, source_target_pairs={{0,24},{8,16},{16,8},{24,0},{1,25},{9,17},{17,9},{25,1},{2,26},{10... | collective-permute-start | bytes 159752 | tf_op jit(solution)/shard_map/ppermute | solution.py:27
  24.3 1.3 %collective-permute-start.6 = (f32[104,128]{1,0:T(8,128)S(1)}, f32[104,128]{1,0:T(8,128)S(1)}, u32[]{:S(2)}, u32[]{:S(2)}) collective-permute-start(f32[104,128]{1,0:T(8,128)S(1)} %get-tuple-element.25), channel_id=1, source_target_pairs={{0,8},{8,0},{16,24},{24,16},{1,9},{9,1},{17,25},{25,17},{2,10},{10... | collective-permute-start | bytes 159752 | tf_op jit(solution)/shard_map/ppermute | solution.py:27
  25.6 2.2 %collective-permute-done.8.refs_3_ = f32[104,128]{1,0:T(8,128)S(1)} collective-permute-done((f32[104,128]{1,0:T(8,128)S(1)}, f32[104,128]{1,0:T(8,128)S(1)}, u32[]{:S(2)}, u32[]{:S(2)}) %collective-permute-start.8) | collective-permute-done | bytes 53280 | tf_op jit(solution)/shard_map/ppermute | solution.py:27
  27.8 1.5 %collective-permute-done.7.refs_2_ = f32[104,128]{1,0:T(8,128)S(1)} collective-permute-done((f32[104,128]{1,0:T(8,128)S(1)}, f32[104,128]{1,0:T(8,128)S(1)}, u32[]{:S(2)}, u32[]{:S(2)}) %collective-permute-start.7) | collective-permute-done | bytes 53280 | tf_op jit(solution)/shard_map/ppermute | solution.py:27
  29.3 0.0 collective-permute-done.6.refs_1_
  29.3 0.7 %finish.1 = (f32[1,4,16]{2,1,0:T(4,128)}, f32[4,16,512]{2,1,0:T(8,128)}, f32[1,16,256]{2,1,0:T(8,128)}) custom-call(f32[104,128]{1,0:T(8,128)S(1)} %get-tuple-element.26.refs_0_, f32[104,128]{1,0:T(8,128)S(1)} %collective-permute-done.6.refs_1_, f32[104,128]{1,0:T(8,128)S(1)} %collective-permute-done.7.refs_2_, f32[104,128]{1,0:T(8,128)S(1)} %collective-permute-done.8.refs_3_), custom_call_target="tpu_custom_call" | custom-call | tf_op jit(solution)/shard_map/finish/pallas_call | solution.py:441
  (14 shorter events, 0.1 us)
Async XLA Ops:
  1.5 7.6 %collective-permute-start.2 = (bf16[48,256]{1,0:T(8,128)(2,1)S(1)}, bf16[48,256]{1,0:T(8,128)(2,1)S(1)}, u32[]{:S(2)}, u32[]{:S(2)}) collective-permute-start(bf16[48,256]{1,0:T(8,128)(2,1)S(1)} %add_convert_fusion.1.refs_2_), channel_id=1, source_target_pairs={{0,16},{8,24},{16,0},{24,8},{1,17},{9,25},{17,1},{25,9},{2,18},{10... | collective-permute-start | bytes 73736 | tf_op jit(solution)/shard_map/ppermute | solution.py:27
  5.6 5.6 %collective-permute-start.1 = (bf16[48,256]{1,0:T(8,128)(2,1)S(1)}, bf16[48,256]{1,0:T(8,128)(2,1)S(1)}, u32[]{:S(2)}, u32[]{:S(2)}) collective-permute-start(bf16[48,256]{1,0:T(8,128)(2,1)S(1)} %add_convert_fusion.1.refs_2_), channel_id=1, source_target_pairs={{0,24},{8,16},{16,8},{24,0},{1,25},{9,17},{17,9},{25,1},{2,26},{10... | collective-permute-start | bytes 73736 | tf_op jit(solution)/shard_map/ppermute | solution.py:27
  6.9 4.3 %collective-permute-start = (bf16[48,256]{1,0:T(8,128)(2,1)S(1)}, bf16[48,256]{1,0:T(8,128)(2,1)S(1)}, u32[]{:S(2)}, u32[]{:S(2)}) collective-permute-start(bf16[48,256]{1,0:T(8,128)(2,1)S(1)} %add_convert_fusion.1.refs_2_), channel_id=1, source_target_pairs={{0,8},{8,0},{16,24},{24,16},{1,9},{9,1},{17,25},{25,17},{2,10},{10... | collective-permute-start | bytes 73736 | tf_op jit(solution)/shard_map/ppermute | solution.py:27
  15.0 2.6 %collective-permute-start.3 = (f32[2,4,16,512]{3,2,1,0:T(8,128)S(1)}, f32[2,4,16,512]{3,2,1,0:T(8,128)S(1)}, u32[]{:S(2)}, u32[]{:S(2)}) collective-permute-start(f32[2,4,16,512]{3,2,1,0:T(8,128)S(1)} %get-tuple-element.14), channel_id=1, source_target_pairs={{0,1},{1,0},{2,3},{3,2},{4,5},{5,4},{6,7},{7,6},{8,9},{9,8},{10,11... | collective-permute-start | bytes 786440 | tf_op jit(solution)/shard_map/ppermute | solution.py:27
  16.0 4.6 %collective-permute-start.5 = (f32[4,16,256]{2,1,0:T(8,128)S(1)}, f32[4,16,256]{2,1,0:T(8,128)S(1)}, u32[]{:S(2)}, u32[]{:S(2)}) collective-permute-start(f32[4,16,256]{2,1,0:T(8,128)S(1)} %acceptors.1), channel_id=1, source_target_pairs={{0,4},{4,0},{1,5},{5,1},{2,6},{6,2},{3,7},{7,3},{8,12},{12,8},{9,1... | collective-permute-start | bytes 196616 | tf_op jit(solution)/shard_map/ppermute | solution.py:27
  17.6 4.3 %collective-permute-start.4 = (bf16[4,16,512]{2,1,0:T(8,128)(2,1)S(1)}, bf16[4,16,512]{2,1,0:T(8,128)(2,1)S(1)}, u32[]{:S(2)}, u32[]{:S(2)}) collective-permute-start(bf16[4,16,512]{2,1,0:T(8,128)(2,1)S(1)} %get-tuple-element.16), channel_id=1, source_target_pairs={{0,2},{1,3},{2,0},{3,1},{4,6},{5,7},{6,4},{7,5},{8,10},{9,11},{10,... | collective-permute-start | bytes 196616 | tf_op jit(solution)/shard_map/ppermute | solution.py:27
  22.1 5.7 %collective-permute-start.8 = (f32[104,128]{1,0:T(8,128)S(1)}, f32[104,128]{1,0:T(8,128)S(1)}, u32[]{:S(2)}, u32[]{:S(2)}) collective-permute-start(f32[104,128]{1,0:T(8,128)S(1)} %get-tuple-element.23), channel_id=1, source_target_pairs={{0,16},{8,24},{16,0},{24,8},{1,17},{9,25},{17,1},{25,9},{2,18},{10... | collective-permute-start | bytes 159752 | tf_op jit(solution)/shard_map/ppermute | solution.py:27
  23.4 5.9 %collective-permute-start.7 = (f32[104,128]{1,0:T(8,128)S(1)}, f32[104,128]{1,0:T(8,128)S(1)}, u32[]{:S(2)}, u32[]{:S(2)}) collective-permute-start(f32[104,128]{1,0:T(8,128)S(1)} %get-tuple-element.24), channel_id=1, source_target_pairs={{0,24},{8,16},{16,8},{24,0},{1,25},{9,17},{17,9},{25,1},{2,26},{10... | collective-permute-start | bytes 159752 | tf_op jit(solution)/shard_map/ppermute | solution.py:27
  24.3 5.0 %collective-permute-start.6 = (f32[104,128]{1,0:T(8,128)S(1)}, f32[104,128]{1,0:T(8,128)S(1)}, u32[]{:S(2)}, u32[]{:S(2)}) collective-permute-start(f32[104,128]{1,0:T(8,128)S(1)} %get-tuple-element.25), channel_id=1, source_target_pairs={{0,8},{8,0},{16,24},{24,16},{1,9},{9,1},{17,25},{25,17},{2,10},{10... | collective-permute-start | bytes 159752 | tf_op jit(solution)/shard_map/ppermute | solution.py:27

commit v8 on v7

--- a/solution.py
+++ b/solution.py
@@ -272,7 +272,7 @@
             preferred_element_type=f32,
         )
 
-    middle = len(tiles) // 2
+    middle = 7 * len(tiles) // 10
     for tile, (b, a) in enumerate(tiles):
         rows = jnp.where(twice_of[a], grads[b][:, None, :], 0.0).astype(bf16)
         rows = ones_dot(rows.reshape(pairs, LANES), ones)

time: 30.2 us -> 30.2 us (level)
  no operation moved by 1% of the time
where the time goes in v8:
time: 30.2 us; the launch traced here: 30 us
  starting transfers between devices  12.4 us (41%)
  waiting for transfers between devices  8.5 us (28%)
  Pallas kernels  5.42 us (18%)
  other arithmetic  2.88 us (10%)
  between operations  0.76 us (3%)
    ppermute x9, starting transfers between devices, swapped(): lax.ppermute(value, axis, [(i, i ^ bits) for i in range(lax.axis_size(axi...  12.4 us
    ppermute x9, waiting for transfers between devices, swapped(): lax.ppermute(value, axis, [(i, i ^ bits) for i in range(lax.axis_size(axi...  8.5 us
    pallas_call x1, Pallas kernels, shared(): pl.pallas_call(functools.partial(head_kernel, blocks, blk, width), out_sh...  3.82 us
    convert_element_type x1, other arithmetic, halved(): return (value.astype(jnp.float32) * 0.5).astype(value.dtype)  0.99 us
    convert_element_type x1, other arithmetic, shared(): base = (base.astype(f32) + spots.astype(f32)).astype(bf16)  0.98 us
    pallas_call x1, Pallas kernels, shared(): pl.pallas_call(functools.partial(acceptor_kernel, blocks, blk), out_shape...  0.88 us
    convert_element_type x1, other arithmetic, shared(): packed = (sites.astype(f32) + whole).astype(bf16)  0.86 us
    pallas_call x1, Pallas kernels, shared(): pl.pallas_call(functools.partial(finish_kernel, blocks, width, hidden), o...  0.68 us
  transfers between devices with their start and end apart: 9, of which 5 were waited for; matrix products, arithmetic and copies ran while one was open for 7% of the time, Pallas kernels for 3%

profile of v8, /device:TPU:0, one launch (start us, length us, event | category | flops | bytes accessed | tf_op | source)
XLA Modules:
  0.0 30.0 jit_solution(9335952257811410482)
XLA Ops:
  0.7 0.9 %add_convert_fusion.1.refs_2_ = bf16[48,256]{1,0:T(8,128)(2,1)S(1)} fusion(s32[4,16]{1,0:T(4,128)} %bitcast.20, s32[1,16]{1,0:T(1,128)} %param.11, s32[16,80]{1,0:T(8,128)} %bitcast.17, bf16[16,256]{1,0:T(8,128)(2,1)} %bitcast.18, bf16[16,256]{1,0:T(8,128)(2,1)} %bitcast.19, pred[256]{0:T(512)(128)(4,1)S(1)} %iota_compare_fusion, ...), kind=kLoop, calls=%fused_computation.13 | loop fusion | flops 172032 | bytes 46704 | tf_op jit(solution)/shard_map/convert_element_type | solution.py:375
  1.5 4.0 %collective-permute-start.2 = (bf16[48,256]{1,0:T(8,128)(2,1)S(1)}, bf16[48,256]{1,0:T(8,128)(2,1)S(1)}, u32[]{:S(2)}, u32[]{:S(2)}) collective-permute-start(bf16[48,256]{1,0:T(8,128)(2,1)S(1)} %add_convert_fusion.1.refs_2_), channel_id=1, source_target_pairs={{0,16},{8,24},{16,0},{24,8},{1,17},{9,25},{17,1},{25,9},{2,18},{10... | collective-permute-start | bytes 73736 | tf_op jit(solution)/shard_map/ppermute | solution.py:27
  5.6 1.3 %collective-permute-start.1 = (bf16[48,256]{1,0:T(8,128)(2,1)S(1)}, bf16[48,256]{1,0:T(8,128)(2,1)S(1)}, u32[]{:S(2)}, u32[]{:S(2)}) collective-permute-start(bf16[48,256]{1,0:T(8,128)(2,1)S(1)} %add_convert_fusion.1.refs_2_), channel_id=1, source_target_pairs={{0,24},{8,16},{16,8},{24,0},{1,25},{9,17},{17,9},{25,1},{2,26},{10... | collective-permute-start | bytes 73736 | tf_op jit(solution)/shard_map/ppermute | solution.py:27
  6.9 0.2 collective-permute-start
  7.1 1.0 %add_convert_fusion.refs_0_ = bf16[144,256]{1,0:T(8,128)(2,1)S(1)} fusion(s32[1,64]{1,0:T(1,128)} %param.12, bf16[4,512]{1,0:T(4,128)(2,1)} %param.17, bf16[128,256]{1,0:T(8,128)(2,1)} %param.15, pred[144]{0:T(512)(128)(4,1)S(1)} %iota_compare_fusion.1), kind=kLoop, calls=%fused_computation.2 | loop fusion | flops 552960 | bytes 143760 | tf_op jit(solution)/shard_map/convert_element_type | solution.py:388
  8.1 1.0 %fusion.refs_1_.w_ref = bf16[256,512]{1,0:T(8,128)(2,1)S(1)} fusion(bf16[4,256,512]{2,1,0:T(8,128)(2,1)} %param.16, s32[]{:T(128)S(6)} %select_n.13), kind=kLoop, calls=%fused_computation.1 | loop fusion | flops 393216 | bytes 524292 | tf_op jit(solution)/shard_map/convert_element_type | solution.py:127
  9.1 0.0 collective-permute-done.2.refs_5_
  9.1 2.0 %collective-permute-done.1.refs_4_ = bf16[48,256]{1,0:T(8,128)(2,1)S(1)} collective-permute-done((bf16[48,256]{1,0:T(8,128)(2,1)S(1)}, bf16[48,256]{1,0:T(8,128)(2,1)S(1)}, u32[]{:S(2)}, u32[]{:S(2)}) %collective-permute-start.1) | collective-permute-done | bytes 24608 | tf_op jit(solution)/shard_map/ppermute | solution.py:27
  11.2 0.0 collective-permute-done.refs_3_
  11.2 3.8 %head.1 = (f32[256,512]{1,0:T(8,128)S(1)}, f32[2,4,16,512]{3,2,1,0:T(8,128)S(1)}, f32[4,8,128]{2,1,0:T(8,128)S(1)}, bf16[10,256,512]{2,1,0:T(8,128)(2,1)S(1)}, f32[10,256,256]{2,1,0:T(8,128)S(1)}) custom-call(bf16[144,256]{1,0:T(8,128)(2,1)S(1)} %add_convert_fusion.refs_0_, bf16[256,512]{1,0:T(8,128)(2,1)S(1)} %fusion.refs_1_.w_ref, ...), custom_call_target="tpu_custom_call" | custom-call | tf_op jit(solution)/shard_map/head/pallas_call | solution.py:394
  15.0 0.1 collective-permute-start.3
  15.1 0.9 %acceptors.1 = f32[4,16,256]{2,1,0:T(8,128)S(1)} custom-call(bf16[10,256,512]{2,1,0:T(8,128)(2,1)S(1)} %get-tuple-element.17.grad_ref, bf16[256,512]{1,0:T(8,128)(2,1)S(1)} %fusion.refs_1_.w_ref, f32[10,256,256]{2,1,0:T(8,128)S(1)} %get-tuple-element.18.slope_ref), custom_call_target="tpu_custom_call" | custom-call | flops 671088640 | bytes 5242880 | tf_op jit(solution)/shard_map/acceptors/pallas_call | solution.py:415
  16.0 1.6 %collective-permute-start.5 = (f32[4,16,256]{2,1,0:T(8,128)S(1)}, f32[4,16,256]{2,1,0:T(8,128)S(1)}, u32[]{:S(2)}, u32[]{:S(2)}) collective-permute-start(f32[4,16,256]{2,1,0:T(8,128)S(1)} %acceptors.1), channel_id=1, source_target_pairs={{0,4},{4,0},{1,5},{5,1},{2,6},{6,2},{3,7},{7,3},{8,12},{12,8},{9,1... | collective-permute-start | bytes 196616 | tf_op jit(solution)/shard_map/ppermute | solution.py:27
  17.6 0.0 collective-permute-done.3.sent_ref
  17.6 1.5 %collective-permute-start.4 = (bf16[4,16,512]{2,1,0:T(8,128)(2,1)S(1)}, bf16[4,16,512]{2,1,0:T(8,128)(2,1)S(1)}, u32[]{:S(2)}, u32[]{:S(2)}) collective-permute-start(bf16[4,16,512]{2,1,0:T(8,128)(2,1)S(1)} %get-tuple-element.16), channel_id=1, source_target_pairs={{0,2},{1,3},{2,0},{3,1},{4,6},{5,7},{6,4},{7,5},{8,10},{9,11},{10,... | collective-permute-start | bytes 196616 | tf_op jit(solution)/shard_map/ppermute | solution.py:27
  19.1 1.4 %collective-permute-done.5 = f32[4,16,256]{2,1,0:T(8,128)S(1)} collective-permute-done((f32[4,16,256]{2,1,0:T(8,128)S(1)}, f32[4,16,256]{2,1,0:T(8,128)S(1)}, u32[]{:S(2)}, u32[]{:S(2)}) %collective-permute-start.5) | collective-permute-done | bytes 65568 | tf_op jit(solution)/shard_map/ppermute | solution.py:27
  20.6 1.4 %collective-permute-done.4 = bf16[4,16,512]{2,1,0:T(8,128)(2,1)S(1)} collective-permute-done((bf16[4,16,512]{2,1,0:T(8,128)(2,1)S(1)}, bf16[4,16,512]{2,1,0:T(8,128)(2,1)S(1)}, u32[]{:S(2)}, u32[]{:S(2)}) %collective-permute-start.4) | collective-permute-done | bytes 65568 | tf_op jit(solution)/shard_map/ppermute | solution.py:27
  22.1 1.3 %collective-permute-start.8 = (f32[104,128]{1,0:T(8,128)S(1)}, f32[104,128]{1,0:T(8,128)S(1)}, u32[]{:S(2)}, u32[]{:S(2)}) collective-permute-start(f32[104,128]{1,0:T(8,128)S(1)} %get-tuple-element.23), channel_id=1, source_target_pairs={{0,16},{8,24},{16,0},{24,8},{1,17},{9,25},{17,1},{25,9},{2,18},{10... | collective-permute-start | bytes 159752 | tf_op jit(solution)/shard_map/ppermute | solution.py:27
  23.4 0.9 %collective-permute-start.7 = (f32[104,128]{1,0:T(8,128)S(1)}, f32[104,128]{1,0:T(8,128)S(1)}, u32[]{:S(2)}, u32[]{:S(2)}) collective-permute-start(f32[104,128]{1,0:T(8,128)S(1)} %get-tuple-element.24), channel_id=1, source_target_pairs={{0,24},{8,16},{16,8},{24,0},{1,25},{9,17},{17,9},{25,1},{2,26},{10... | collective-permute-start | bytes 159752 | tf_op jit(solution)/shard_map/ppermute | solution.py:27
  24.3 1.3 %collective-permute-start.6 = (f32[104,128]{1,0:T(8,128)S(1)}, f32[104,128]{1,0:T(8,128)S(1)}, u32[]{:S(2)}, u32[]{:S(2)}) collective-permute-start(f32[104,128]{1,0:T(8,128)S(1)} %get-tuple-element.25), channel_id=1, source_target_pairs={{0,8},{8,0},{16,24},{24,16},{1,9},{9,1},{17,25},{25,17},{2,10},{10... | collective-permute-start | bytes 159752 | tf_op jit(solution)/shard_map/ppermute | solution.py:27
  25.6 2.2 %collective-permute-done.8.refs_3_ = f32[104,128]{1,0:T(8,128)S(1)} collective-permute-done((f32[104,128]{1,0:T(8,128)S(1)}, f32[104,128]{1,0:T(8,128)S(1)}, u32[]{:S(2)}, u32[]{:S(2)}) %collective-permute-start.8) | collective-permute-done | bytes 53280 | tf_op jit(solution)/shard_map/ppermute | solution.py:27
  27.8 1.5 %collective-permute-done.7.refs_2_ = f32[104,128]{1,0:T(8,128)S(1)} collective-permute-done((f32[104,128]{1,0:T(8,128)S(1)}, f32[104,128]{1,0:T(8,128)S(1)}, u32[]{:S(2)}, u32[]{:S(2)}) %collective-permute-start.7) | collective-permute-done | bytes 53280 | tf_op jit(solution)/shard_map/ppermute | solution.py:27
  29.3 0.0 collective-permute-done.6.refs_1_
  29.3 0.7 %finish.1 = (f32[1,4,16]{2,1,0:T(4,128)}, f32[4,16,512]{2,1,0:T(8,128)}, f32[1,16,256]{2,1,0:T(8,128)}) custom-call(f32[104,128]{1,0:T(8,128)S(1)} %get-tuple-element.26.refs_0_, f32[104,128]{1,0:T(8,128)S(1)} %collective-permute-done.6.refs_1_, f32[104,128]{1,0:T(8,128)S(1)} %collective-permute-done.7.refs_2_, f32[104,128]{1,0:T(8,128)S(1)} %collective-permute-done.8.refs_3_), custom_call_target="tpu_custom_call" | custom-call | tf_op jit(solution)/shard_map/finish/pallas_call | solution.py:441
  (14 shorter events, 0.1 us)
Async XLA Ops:
  1.5 7.6 %collective-permute-start.2 = (bf16[48,256]{1,0:T(8,128)(2,1)S(1)}, bf16[48,256]{1,0:T(8,128)(2,1)S(1)}, u32[]{:S(2)}, u32[]{:S(2)}) collective-permute-start(bf16[48,256]{1,0:T(8,128)(2,1)S(1)} %add_convert_fusion.1.refs_2_), channel_id=1, source_target_pairs={{0,16},{8,24},{16,0},{24,8},{1,17},{9,25},{17,1},{25,9},{2,18},{10... | collective-permute-start | bytes 73736 | tf_op jit(solution)/shard_map/ppermute | solution.py:27
  5.6 5.6 %collective-permute-start.1 = (bf16[48,256]{1,0:T(8,128)(2,1)S(1)}, bf16[48,256]{1,0:T(8,128)(2,1)S(1)}, u32[]{:S(2)}, u32[]{:S(2)}) collective-permute-start(bf16[48,256]{1,0:T(8,128)(2,1)S(1)} %add_convert_fusion.1.refs_2_), channel_id=1, source_target_pairs={{0,24},{8,16},{16,8},{24,0},{1,25},{9,17},{17,9},{25,1},{2,26},{10... | collective-permute-start | bytes 73736 | tf_op jit(solution)/shard_map/ppermute | solution.py:27
  6.9 4.3 %collective-permute-start = (bf16[48,256]{1,0:T(8,128)(2,1)S(1)}, bf16[48,256]{1,0:T(8,128)(2,1)S(1)}, u32[]{:S(2)}, u32[]{:S(2)}) collective-permute-start(bf16[48,256]{1,0:T(8,128)(2,1)S(1)} %add_convert_fusion.1.refs_2_), channel_id=1, source_target_pairs={{0,8},{8,0},{16,24},{24,16},{1,9},{9,1},{17,25},{25,17},{2,10},{10... | collective-permute-start | bytes 73736 | tf_op jit(solution)/shard_map/ppermute | solution.py:27
  15.0 2.6 %collective-permute-start.3 = (f32[2,4,16,512]{3,2,1,0:T(8,128)S(1)}, f32[2,4,16,512]{3,2,1,0:T(8,128)S(1)}, u32[]{:S(2)}, u32[]{:S(2)}) collective-permute-start(f32[2,4,16,512]{3,2,1,0:T(8,128)S(1)} %get-tuple-element.14), channel_id=1, source_target_pairs={{0,1},{1,0},{2,3},{3,2},{4,5},{5,4},{6,7},{7,6},{8,9},{9,8},{10,11... | collective-permute-start | bytes 786440 | tf_op jit(solution)/shard_map/ppermute | solution.py:27
  16.0 4.6 %collective-permute-start.5 = (f32[4,16,256]{2,1,0:T(8,128)S(1)}, f32[4,16,256]{2,1,0:T(8,128)S(1)}, u32[]{:S(2)}, u32[]{:S(2)}) collective-permute-start(f32[4,16,256]{2,1,0:T(8,128)S(1)} %acceptors.1), channel_id=1, source_target_pairs={{0,4},{4,0},{1,5},{5,1},{2,6},{6,2},{3,7},{7,3},{8,12},{12,8},{9,1... | collective-permute-start | bytes 196616 | tf_op jit(solution)/shard_map/ppermute | solution.py:27
  17.6 4.3 %collective-permute-start.4 = (bf16[4,16,512]{2,1,0:T(8,128)(2,1)S(1)}, bf16[4,16,512]{2,1,0:T(8,128)(2,1)S(1)}, u32[]{:S(2)}, u32[]{:S(2)}) collective-permute-start(bf16[4,16,512]{2,1,0:T(8,128)(2,1)S(1)} %get-tuple-element.16), channel_id=1, source_target_pairs={{0,2},{1,3},{2,0},{3,1},{4,6},{5,7},{6,4},{7,5},{8,10},{9,11},{10,... | collective-permute-start | bytes 196616 | tf_op jit(solution)/shard_map/ppermute | solution.py:27
  22.1 5.7 %collective-permute-start.8 = (f32[104,128]{1,0:T(8,128)S(1)}, f32[104,128]{1,0:T(8,128)S(1)}, u32[]{:S(2)}, u32[]{:S(2)}) collective-permute-start(f32[104,128]{1,0:T(8,128)S(1)} %get-tuple-element.23), channel_id=1, source_target_pairs={{0,16},{8,24},{16,0},{24,8},{1,17},{9,25},{17,1},{25,9},{2,18},{10... | collective-permute-start | bytes 159752 | tf_op jit(solution)/shard_map/ppermute | solution.py:27
  23.4 5.9 %collective-permute-start.7 = (f32[104,128]{1,0:T(8,128)S(1)}, f32[104,128]{1,0:T(8,128)S(1)}, u32[]{:S(2)}, u32[]{:S(2)}) collective-permute-start(f32[104,128]{1,0:T(8,128)S(1)} %get-tuple-element.24), channel_id=1, source_target_pairs={{0,24},{8,16},{16,8},{24,0},{1,25},{9,17},{17,9},{25,1},{2,26},{10... | collective-permute-start | bytes 159752 | tf_op jit(solution)/shard_map/ppermute | solution.py:27
  24.3 5.0 %collective-permute-start.6 = (f32[104,128]{1,0:T(8,128)S(1)}, f32[104,128]{1,0:T(8,128)S(1)}, u32[]{:S(2)}, u32[]{:S(2)}) collective-permute-start(f32[104,128]{1,0:T(8,128)S(1)} %get-tuple-element.25), channel_id=1, source_target_pairs={{0,8},{8,0},{16,24},{24,16},{1,9},{9,1},{17,25},{25,17},{2,10},{10... | collective-permute-start | bytes 159752 | tf_op jit(solution)/shard_map/ppermute | solution.py:27
